TPU v7x, 32 devices: a whole 2x2x4 slice. The times are simulated.
32 devices in a mesh: seq: 2 (over x), dp: 16 (over z, y, core).
Axes of the slice: x: 2, y: 2, z: 4, core: 2. Of those that a mesh axis runs over, the one named last changes fastest.
Arguments:
- tokens: bfloat16 [16384, 1536], P(('dp', 'seq')), may hold values from -6 to 6
- cotangent: bfloat16 [16384, 1536], P(('dp', 'seq')), may hold values from -6 to 6
- in_weight: float32 [1536, 6448], P(('seq', 'dp')), may hold values from -0.15625 to 0.15625
- in_moment: float32 [1536, 6448], P(('seq', 'dp')), may hold values from -24 to 24
- in_square: float32 [1536, 6448], P(('seq', 'dp')), may hold values from 1.47456 to 5.89824
- out_weight: float32 [3072, 1536], P(('seq', 'dp')), may hold values from -0.109375 to 0.109375
- out_moment: float32 [3072, 1536], P(('seq', 'dp')), may hold values from -80 to 80
- out_square: float32 [3072, 1536], P(('seq', 'dp')), may hold values from 16.384 to 65.536
- conv_table: float32 [5, 3328], P(None, ('seq', 'dp')), may hold values from -3 to 3
- conv_moment: float32 [5, 3328], P(None, ('seq', 'dp')), may hold values from -24 to 24
- conv_square: float32 [5, 3328], P(None, ('seq', 'dp')), may hold values from 1.47456 to 5.89824
- norm_gains: float32 [4608], P(('seq', 'dp')), may hold values from 0.5 to 1.5
- gain_moment: float32 [4608], P(('seq', 'dp')), may hold values from -48 to 48
- gain_square: float32 [4608], P(('seq', 'dp')), may hold values from 5.89824 to 23.59296
- head_table: float32 [3, 48], replicated, may hold values from -10 to 1.5, as said below
- head_moment: float32 [3, 48], replicated, may hold values from -80 to 80
- head_square: float32 [3, 48], replicated, may hold values from 16.384 to 65.536
Outputs:
- layer_out: float32 [16384, 1536], P(('dp', 'seq'))
- tokens_grad: float32 [16384, 1536], P(('dp', 'seq'))
- in_weight_new: float32 [1536, 6448], P(('seq', 'dp'))
- in_moment_new: float32 [1536, 6448], P(('seq', 'dp'))
- in_square_new: float32 [1536, 6448], P(('seq', 'dp'))
- out_weight_new: float32 [3072, 1536], P(('seq', 'dp'))
- out_moment_new: float32 [3072, 1536], P(('seq', 'dp'))
- out_square_new: float32 [3072, 1536], P(('seq', 'dp'))
- conv_table_new: float32 [5, 3328], P(None, ('seq', 'dp'))
- conv_moment_new: float32 [5, 3328], P(None, ('seq', 'dp'))
- conv_square_new: float32 [5, 3328], P(None, ('seq', 'dp'))
- norm_gains_new: float32 [4608], P(('seq', 'dp'))
- gain_moment_new: float32 [4608], P(('seq', 'dp'))
- gain_square_new: float32 [4608], P(('seq', 'dp'))
- head_table_new: float32 [3, 48], replicated
- head_moment_new: float32 [3, 48], replicated
- head_square_new: float32 [3, 48], replicated
Inputs may be any that keep to these rules, and one draw needn't show every extreme that they name: `head_table`: row 0 holds the logarithm of each head's decay rate, row 1 its step bias, row 2 its skip factor, which lies between 0.5 and 1.5.
All inputs are finite; a program needn't handle non-finite values.
Results may differ from a plain program's by a relative error of at most 0.012.
The roundings to bfloat16 on the way count: a program that leaves them out, or rounds other values in their place, can miss the bound.
Values may be sent and summed in bfloat16 or wider, within the bound.
No kernel may reach another device: no remote copies, remote signals or barrier semaphores. Data moves between devices by JAX's collectives and lax.ppermute only.
A program may use at most 160 MiB of HBM per device.

v0:
```python
import functools

import jax
import jax.numpy as jnp
from jax import lax
from jax.experimental import pallas as pl
from jax.experimental.pallas import tpu as pltpu
from jax.sharding import PartitionSpec as P

D = 1536
HEADS = 48
HEAD_DIM = 64
STATE = 128
CONV = 4
STEP = 10
DI = 3072
CH = 3328

QUARTERS = 4
QH = HEADS // QUARTERS
QW = DI // QUARTERS
QC = QW + 2 * STATE
WIDE = QC + 128
GC = QW // 2
LEN = 256
ROWS = 1024
HALF = ROWS // 2
BLOCKS = ROWS // LEN

norm_epsilon = 1e-05
adam_epsilon = 1e-08
beta_first = 0.9
beta_second = 0.999
rate_matrix = 0.05
rate_vector = 0.5
rate_heads = 2.0
weight_decay = 0.1
LOG2E = 1.4426950408889634

f32 = jnp.float32
bf16 = jnp.bfloat16
NN = (((1,), (0,)), ((), ()))
NT = (((1,), (1,)), ((), ()))
TN = (((0,), (0,)), ((), ()))
MIB = 1024 * 1024


def mm(a, b, dims=NN):
    return lax.dot_general(a, b, dims, preferred_element_type=f32)


def mm_exact(a, b, dims=NN):
    return lax.dot_general(
        a, b, dims, precision=lax.Precision.HIGHEST, preferred_element_type=f32
    )


def spread_heads(columns, first_head, count):
    rows = columns.shape[0]
    low = lax.broadcasted_iota(jnp.int32, (rows, 128), 1) < HEAD_DIM
    parts = []
    for h in range(first_head, first_head + count, 2):
        first = jnp.broadcast_to(columns[:, h : h + 1], (rows, 128))
        second = jnp.broadcast_to(columns[:, h + 1 : h + 2], (rows, 128))
        parts.append(jnp.where(low, first, second))
    return jnp.concatenate(parts, axis=1)


def softplus(v):
    return jnp.maximum(v, 0.0) + jnp.log1p(jnp.exp(-jnp.abs(v)))


def triangle(lower):
    rows = lax.broadcasted_iota(jnp.int32, (LEN, LEN), 0)
    cols = lax.broadcasted_iota(jnp.int32, (LEN, LEN), 1)
    return rows >= cols if lower else rows <= cols


def halves(pair):
    low = lax.broadcasted_iota(jnp.int32, pair.shape, 1) < HEAD_DIM
    zero = jnp.zeros_like(pair)
    return jnp.where(low, pair, zero), jnp.where(low, zero, pair)


def parts_of(v):
    high = v.astype(bf16)
    return high, (v - high.astype(f32)).astype(bf16)


def affinity_of(first, second):
    both = jnp.concatenate(first, axis=1)
    high = jnp.concatenate([second[0], second[0]], axis=1)
    return mm(both, high, NT) + mm(first[0], second[1], NT)


def running(mask, v):
    high = v.astype(bf16).astype(f32)
    left = v - high
    middle = left.astype(bf16).astype(f32)
    packed = high + pltpu.roll(middle, 16, 1) + pltpu.roll(left - middle, 32, 1)
    product = mm(mask.astype(f32).astype(bf16), packed.astype(bf16))
    return product + pltpu.roll(product, 112, 1) + pltpu.roll(product, 96, 1)


def twice(pair):
    low = lax.broadcasted_iota(jnp.int32, pair.shape, 1) < HEAD_DIM
    turned = pltpu.roll(pair, HEAD_DIM, 1)
    return jnp.where(low, pair, turned).astype(bf16), jnp.where(low, turned, pair).astype(bf16)


def beside_rest(pair, rest):
    low = lax.broadcasted_iota(jnp.int32, pair.shape, 1) < HEAD_DIM
    turned = pltpu.roll(rest, HEAD_DIM, 1).astype(bf16)
    return jnp.where(low, pair, turned), jnp.where(low, turned, pair)


def filter_rows(ext, conv_ref):
    width = ext.shape[1]
    total = conv_ref[CONV : CONV + 1, :width]
    for k in range(CONV):
        total = total + conv_ref[k : k + 1, :width] * ext[5 + k : 5 + k + LEN, :]
    return total


def forward_kernel(
    half, place, near, far, gain, w, conv, head, skip, tail_in, state_in, *rest
):
    normed_out, turned_out, proj_out, filtered_out, scanned_out, mem_out = rest[-10:-4]
    tail_out, state_out, ext, mem = rest[-4:]
    j = pl.program_id(0)

    @pl.when(j == 0)
    def _():
        ext[0:8, :] = tail_in[...]
        mem[...] = state_in[...]

    wide = jnp.where(place[0] == half, near[...], far[...]).astype(f32)
    inv_one = lax.rsqrt(jnp.mean(wide * wide, axis=1, keepdims=True) + norm_epsilon)
    normed = (wide * inv_one * gain[...]).astype(bf16)
    normed_out[...] = normed
    turned_out[...] = normed.T
    proj = mm(normed, w[...])
    proj_out[...] = proj
    ext[8 : 8 + LEN, :] = proj[:, :QC]
    filtered = filter_rows(ext, conv)
    filtered_out[:, :QC] = filtered
    ext[0:8, :] = ext[LEN : LEN + 8, :]
    active = filtered * jax.nn.sigmoid(filtered)
    payload = active[:, :QW]
    writers = parts_of(active[:, QW : QW + STATE])
    readers = parts_of(active[:, QW + STATE :])
    writer = writers[0]

    steps = softplus(pltpu.roll(proj[:, QC:], place[2], 1) + head[1:2, :])
    rates = head[0:1, :] * steps
    causal = triangle(True)
    summed = running(causal, rates) * LOG2E
    across = summed.T
    affinity = jnp.where(causal, affinity_of(readers, writers), 0.0)

    dosed = payload * spread_heads(steps, 0, QH)
    dosed_low = dosed.astype(bf16)
    state = mem[...]
    mem_out[0] = state
    grown = jnp.exp2(spread_heads(summed, 0, QH))
    state_low, state_rest = parts_of(state)
    carried = mm(jnp.concatenate(readers, axis=1), jnp.concatenate([state_low] * 2, axis=0))
    carried = (carried + mm(readers[0], state_rest)) * grown
    within = []
    for pair in range(QH // 2):
        weights = []
        for h in (2 * pair, 2 * pair + 1):
            gap = jnp.minimum(summed[:, h : h + 1] - across[h : h + 1, :], 0.0)
            weights.append((jnp.exp2(gap) * affinity).astype(bf16))
        first, second = halves(dosed_low[:, 128 * pair : 128 * pair + 128])
        within.append(
            mm(jnp.concatenate(weights, axis=1), jnp.concatenate([first, second], axis=0))
        )
    scanned_out[...] = jnp.concatenate(within, axis=1) + carried + payload * skip[...]

    last = summed[LEN - 1 : LEN, :]
    remain = jnp.exp2(spread_heads(last - summed, 0, QH))
    added = mm(writer, (dosed * remain).astype(bf16), TN)
    mem[...] = state * jnp.exp2(spread_heads(last, 0, QH)) + added
    tail_out[...] = ext[0:8, :]
    state_out[...] = mem[...]


def by_core(core, own, other):
    first = core == 0
    return jnp.where(first, own, other), jnp.where(first, other, own)


def at_hand(side, near_a, far_a, near_b, far_b):
    j = pl.program_id(0)
    near = (j % BLOCKS) // (BLOCKS // 2) == side
    first = jnp.where(near, near_a[...], far_a[...])
    return jnp.where(j < BLOCKS, first, jnp.where(near, near_b[...], far_b[...]))


def gate_kernel(
    place, normed, w_gate, cot_na, cot_fa, cot_nb, cot_fb, w_own, w_other, gain, scanned,
    gate_out, shaped_grad_out, stats_out,
):
    gate = mm(normed[...], w_gate[...])
    cot = at_hand(place[0], cot_na, cot_fa, cot_nb, cot_fb)
    left, right = by_core(place[1], w_own[...], w_other[...])
    grad_shaped = mm(cot[:, :QW], left, NT) + mm(cot[:, QW:], right, NT)
    gate_out[...] = gate
    shaped_grad_out[...] = grad_shaped
    gated = scanned[...] * (gate * jax.nn.sigmoid(gate))
    squares = jnp.sum(gated * gated, axis=1, keepdims=True)
    inner = jnp.sum(grad_shaped * gain[...] * gated, axis=1, keepdims=True)
    lane = lax.broadcasted_iota(jnp.int32, (LEN, 128), 1)
    both = jnp.where(lane == 0, squares, jnp.where(lane == 1, inner, 0.0))
    stats_out[...] = both.T[0:8, :]


def finish_kernel(
    place, stats, gate_in, grad_shaped_in, scanned_in, w_own, w_other, gain,
    turned_out, layer_a_out, layer_b_out, scan_grad_out, gate_grad_out, gain_grad,
):
    j = pl.program_id(0)
    table = jnp.concatenate([stats[...], jnp.zeros((120, LEN), f32)], axis=0).T
    inv_two = lax.rsqrt(table[:, 0:1] / DI + norm_epsilon)
    mean = inv_two * table[:, 1:2] / DI
    gate = gate_in[...]
    scanned = scanned_in[...]
    grad_shaped = grad_shaped_in[...]
    sig = jax.nn.sigmoid(gate)
    lift = gate * sig
    unit = scanned * lift * inv_two
    shaped = (unit * gain[...]).astype(bf16)
    turned_out[...] = shaped.T
    left, right = by_core(place[1], w_own[...], w_other[...])
    layer = jnp.concatenate([mm(shaped, left), mm(shaped, right)], axis=1).astype(bf16)

    @pl.when(j < BLOCKS)
    def _():
        layer_a_out[...] = layer

    @pl.when(j >= BLOCKS)
    def _():
        layer_b_out[...] = layer

    grad_gated = inv_two * (grad_shaped * gain[...] - unit * mean)
    scan_grad_out[...] = grad_gated * lift
    gate_grad_out[...] = (grad_gated * scanned * sig * (1.0 + gate * (1.0 - sig))).astype(bf16)

    @pl.when(j == 0)
    def _():
        gain_grad[...] = jnp.zeros_like(gain_grad)

    gain_grad[0:1, :] += jnp.sum(grad_shaped * unit, axis=0, keepdims=True)


def backward_kernel(
    place, proj_in, filtered_in, scanned_in, grad_in, mem_in, conv, head, skip, later_in, state_in,
    *rest
):
    out, conv_grad, head_grad, skip_grad, later_out, state_out, later, grad_mem = rest[-8:]
    i = pl.program_id(0)

    @pl.when(i == 0)
    def _():
        later[LEN : LEN + 8, :] = later_in[...]
        grad_mem[...] = state_in[...]
        conv_grad[...] = jnp.zeros_like(conv_grad)
        head_grad[...] = jnp.zeros_like(head_grad)
        skip_grad[...] = jnp.zeros_like(skip_grad)

    @pl.when(i > 0)
    def _():
        later[LEN : LEN + 8, :] = later[0:8, :]

    conv_in = proj_in[:, :QC]
    filtered = filtered_in[:, :QC]
    sig = jax.nn.sigmoid(filtered)
    active = filtered * sig
    slope = sig * (1.0 + filtered * (1.0 - sig))
    payload = active[:, :QW]
    writers = parts_of(active[:, QW : QW + STATE])
    readers = parts_of(active[:, QW + STATE :])
    writer, reader = writers[0], readers[0]

    raw = pltpu.roll(proj_in[:, QC:], place[2], 1) + head[1:2, :]
    steps = softplus(raw)
    rates = head[0:1, :] * steps
    summed = running(triangle(True), rates) * LOG2E
    across = summed.T
    upper = triangle(False)
    affinity = jnp.where(upper, affinity_of(writers, readers), 0.0)

    grad = grad_in[...]
    grad_low = grad.astype(bf16)
    grad_rest = grad - grad_low.astype(f32)
    dose = spread_heads(steps, 0, QH)
    dosed = payload * dose
    dosed_low = dosed.astype(bf16)
    state = mem_in[0]
    state_grad = grad_mem[...]
    state_grad_low = state_grad.astype(bf16)
    last = summed[LEN - 1 : LEN, :]
    remain = jnp.exp2(spread_heads(last - summed, 0, QH))
    from_state = mm(writer, state_grad_low) * remain

    mixed = jnp.zeros((LEN, LEN), f32)
    within = []
    for pair in range(QH // 2):
        lanes = slice(128 * pair, 128 * pair + 128)
        grads = halves(grad_low[:, lanes])
        doses = twice(dosed[:, lanes])
        parts = beside_rest(grad_low[:, lanes], grad_rest[:, lanes])
        weights = []
        for n in range(2):
            h = 2 * pair + n
            gap = jnp.minimum(across[h : h + 1, :] - summed[:, h : h + 1], 0.0)
            decay = jnp.exp2(gap)
            weights.append((decay * affinity).astype(bf16))
            mixed = mixed + decay * mm(doses[n], parts[n], NT)
        within.append(mm(jnp.concatenate(weights, axis=1), jnp.concatenate(grads, axis=0)))
    unit = jnp.concatenate(within, axis=1) + from_state

    payload_grad = dose * unit + skip[...] * grad
    core = scanned_in[...] - payload * skip[...]
    dosed_wide = dosed_low.astype(f32)
    balance = grad_low.astype(f32) * core - dosed_wide * unit
    high_part = balance.astype(bf16)
    low_part = (balance - high_part.astype(f32)).astype(bf16)
    decay_last = jnp.exp2(spread_heads(last, 0, QH))
    at_end = jnp.sum(dosed_wide * from_state, axis=0, keepdims=True) + decay_last * jnp.sum(
        state_grad * state, axis=0, keepdims=True
    )
    end_high = at_end.astype(bf16).astype(f32)
    end_middle = (at_end - end_high).astype(bf16).astype(f32)
    row = lax.broadcasted_iota(jnp.int32, (16, QW), 0)
    end_parts = jnp.where(
        row == 0,
        end_high,
        jnp.where(row == 1, end_middle, jnp.where(row == 2, at_end - end_high - end_middle, 0.0)),
    ).astype(bf16)
    heads_of = (
        lax.broadcasted_iota(jnp.int32, (QW, 128), 0) // HEAD_DIM
        == lax.broadcasted_iota(jnp.int32, (QW, 128), 1)
    ).astype(f32)
    by_head = mm(
        jnp.concatenate([high_part, low_part, (payload * unit).astype(bf16), end_parts], axis=0),
        heads_of.astype(bf16),
    )
    balance_sum = by_head[:LEN] + by_head[LEN : 2 * LEN]
    direct = by_head[2 * LEN : 3 * LEN]
    end_sum = jnp.sum(by_head[3 * LEN :], axis=0, keepdims=True)
    rate_grad = running(upper, balance_sum) + end_sum
    step_grad = direct + head[0:1, :] * rate_grad
    raw_grad = step_grad * jax.nn.sigmoid(raw)
    head_grad[0:1, :] += jnp.sum(rate_grad * rates, axis=0, keepdims=True)
    head_grad[1:2, :] += jnp.sum(raw_grad, axis=0, keepdims=True)
    skip_grad[0:1, :] += jnp.sum(grad * payload, axis=0, keepdims=True)

    grown_wide = jnp.exp2(spread_heads(summed, 0, QH)) * grad
    grown_grad = grown_wide.astype(bf16)
    grown_rest = (grown_wide - grown_grad.astype(f32)).astype(bf16)
    kept = (remain * dosed).astype(bf16)
    mixed_low = jnp.where(upper, mixed, 0.0).astype(bf16)
    writer_grad = mm(mixed_low, reader) + mm(kept, state_grad_low, NT)
    state_low = state.astype(bf16)
    reader_grad = (
        mm(mixed_low, writer, TN) + mm(grown_grad, state_low, NT) + mm(grown_rest, state_low, NT)
    )
    grad_mem[...] = decay_last * state_grad + mm(reader, grown_grad, TN)

    filtered_grad = jnp.concatenate([payload_grad, writer_grad, reader_grad], axis=1) * slope
    later[0:LEN, :] = filtered_grad
    back = None
    sums = []
    for k in range(CONV):
        ahead = later[CONV - 1 - k : CONV - 1 - k + LEN, :]
        sums.append(jnp.sum(ahead * conv_in, axis=0, keepdims=True))
        term = conv[k : k + 1, :QC] * ahead
        back = term if back is None else back + term
    sums.append(jnp.sum(filtered_grad, axis=0, keepdims=True))
    conv_grad[...] += jnp.concatenate(sums + [jnp.zeros((7 - CONV, QC), f32)], axis=0)
    out[:, :QC] = back.astype(bf16)
    out[:, QC:] = pltpu.roll(raw_grad, place[3], 1).astype(bf16)
    later_out[...] = later[0:8, :]
    state_out[...] = grad_mem[...]


def outer_kernel(left, *rest):
    out = rest[-1]
    total = None
    for n, right in enumerate(rest[:-1]):
        part = mm(left[:, n * HALF : (n + 1) * HALF], right[...])
        total = part if total is None else total + part
    out[...] = total.astype(bf16)


def pieces_kernel(chip_rows, blocks, place, left, right, *rest):
    out, dots = rest[-2:]
    weights, others = rest[:blocks], rest[blocks:-2]
    tile = left.shape[0]
    i = pl.program_id(0)
    per = tile // chip_rows
    steps = out.shape[0] // per
    result = mm(left[...], right[...])
    sums = jnp.zeros((tile, 128), f32)
    for n, weight in enumerate(weights):
        product = result[:, n * GC : (n + 1) * GC] * weight[...].astype(f32)
        sums = sums + (product[:, :128] + product[:, 128:256] + product[:, 256:])
    dots[...] = jnp.broadcast_to(jnp.sum(sums.T, axis=0, keepdims=True), (8, tile))
    for n in range(per):
        part = result[n * chip_rows : (n + 1) * chip_rows].astype(bf16)
        if others:
            out[(i % steps) * per + n, 0, i // steps] = part
        else:
            out[(i % steps) * per + n, i // steps] = part
    if others:
        half = out.shape[0] // 2

        @pl.when(i == 0)
        def _():
            own, other = others
            core = place[1]
            out[pl.ds(core * half, half), 1] = own[...]
            out[pl.ds((1 - core) * half, half), 1] = other[...]


def input_grad(gate_grad, wide_grad, w_gate, w_wide):
    grad = mm(gate_grad[...], w_gate[...], NT) + mm(wide_grad[...], w_wide[...], NT)
    return grad.astype(bf16)


def input_grad_kernel(place, *refs):
    refs[-1][...] = input_grad(*refs[:-1])


def own_first(j, place):
    per = BLOCKS // 2
    half = j // per
    side = place[0]
    return (half + side - 2 * half * side) * per + j % per


def rows_of(width, first=0):
    return pl.BlockSpec((LEN, width), lambda j, *_: (j + first, 0))


def moved_columns(height):
    return pl.BlockSpec(
        (height, LEN),
        lambda j, place: (0, own_first(j % BLOCKS, place) + (j // BLOCKS) * BLOCKS),
    )


def first_rows(width):
    return pl.BlockSpec(
        (LEN, width), lambda j, place: (own_first(jnp.minimum(j, BLOCKS - 1), place), 0)
    )


def second_rows(width):
    return pl.BlockSpec(
        (LEN, width), lambda j, place: (own_first(jnp.maximum(j - BLOCKS, 0), place), 0)
    )


def whole(*shape):
    return pl.BlockSpec(shape, lambda j, *_: (0,) * len(shape))


def params():
    return pltpu.CompilerParams(
        vmem_limit_bytes=60 * MIB, dimension_semantics=("arbitrary",)
    )


def shape(dims, dtype):
    return jax.ShapeDtypeStruct(dims, dtype)


def cost(microseconds):
    return pl.CostEstimate(
        flops=int(microseconds * 1e9),
        bytes_accessed=int(microseconds * 3.5e6),
        transcendentals=0,
    )


def run_forward(place, near, far, gain, w, conv, head, skip, carried, buffers, part):
    per = BLOCKS // 2
    first = part * per
    if buffers is None:
        buffers = ()
    anywhere = pl.BlockSpec(memory_space=pl.ANY)
    return pl.pallas_call(
        functools.partial(forward_kernel, part % 2),
        grid_spec=pltpu.PrefetchScalarGridSpec(
            num_scalar_prefetch=1,
            grid=(per,),
            in_specs=[
                rows_of(D), rows_of(D), whole(1, D), whole(D, WIDE), whole(8, WIDE), whole(8, 128), whole(1, QW),
                whole(8, QC), whole(STATE, QW),
            ] + [anywhere] * len(buffers),
            out_specs=[
                rows_of(D, first), pl.BlockSpec((D, LEN), lambda j, *_: (0, j + first)),
                rows_of(WIDE, first), rows_of(WIDE, first), rows_of(QW, first),
                pl.BlockSpec((1, STATE, QW), lambda j, *_: (j + first, 0, 0)),
                whole(8, QC), whole(STATE, QW),
            ],
            scratch_shapes=[pltpu.VMEM((LEN + 8, QC), f32), pltpu.VMEM((STATE, QW), f32)],
        ),
        out_shape=[
            shape((2 * ROWS, D), bf16), shape((D, 2 * ROWS), bf16),
            shape((2 * ROWS, WIDE), f32), shape((2 * ROWS, WIDE), f32),
            shape((2 * ROWS, QW), f32), shape((2 * BLOCKS, STATE, QW), f32), shape((8, QC), f32), shape((STATE, QW), f32),
        ],
        input_output_aliases={10 + n: n for n in range(len(buffers))},
        compiler_params=params(),
        cost_estimate=cost(13),
        name="forward_scan",
    )(place, near, far, gain, w, conv, head, skip, *carried, *buffers)


def assemble_kernel(count, place, *refs):
    pieces, (gate, own, send) = refs[:count], refs[count:]
    half = count // 2
    for n, piece in enumerate(pieces):
        chip = place[4 + n]
        gate[0, chip] = piece[0, 0]
        gate[1, chip] = piece[0, 1]
        mine = chip // half == place[1]

        @pl.when(mine)
        def _():
            own[chip % half] = piece[1]

        @pl.when(jnp.logical_not(mine))
        def _():
            send[chip % half] = piece[1]


def run_assemble(place, pieces):
    count = len(pieces)
    _, _, rows, width = pieces[0].shape
    outs = [(2, count, rows, width)] + [(count // 2, 2, rows, width)] * 2
    return pl.pallas_call(
        functools.partial(assemble_kernel, count),
        grid_spec=pltpu.PrefetchScalarGridSpec(
            num_scalar_prefetch=1,
            grid=(1,),
            in_specs=[whole(2, 2, rows, width)] * count,
            out_specs=[whole(*dims) for dims in outs],
        ),
        out_shape=[shape(dims, bf16) for dims in outs],
        compiler_params=params(),
        cost_estimate=cost(3),
        name="assemble",
    )(place, *pieces)


def run_gate(place, normed, w_gate, cots, w_out, gain, scanned):
    per = BLOCKS // 2

    def half(sequence, far):
        def index(j, place):
            first = sequence * BLOCKS + (1 - place[0] if far else place[0]) * per
            return (jnp.clip(j - first, 0, per - 1), 0)

        return pl.BlockSpec((LEN, D), index)

    return pl.pallas_call(
        gate_kernel,
        grid_spec=pltpu.PrefetchScalarGridSpec(
            num_scalar_prefetch=1,
            grid=(2 * BLOCKS,),
            in_specs=[
                rows_of(D), whole(D, QW), half(0, False), half(0, True), half(1, False),
                half(1, True), whole(QW, QW), whole(QW, QW), whole(1, QW), rows_of(QW),
            ],
            out_specs=[
                rows_of(QW), rows_of(QW), pl.BlockSpec((8, LEN), lambda j, *_: (0, j)),
            ],
        ),
        out_shape=[
            shape((2 * ROWS, QW), f32), shape((2 * ROWS, QW), f32), shape((8, 2 * ROWS), f32),
        ],
        compiler_params=params(),
        cost_estimate=cost(2),
        name="gate_and_stats",
    )(place, normed, w_gate, *cots, *w_out, gain, scanned)


def run_finish(place, stats, gate, grad_shaped, scanned, w_out, gain):
    return pl.pallas_call(
        finish_kernel,
        grid_spec=pltpu.PrefetchScalarGridSpec(
            num_scalar_prefetch=1,
            grid=(2 * BLOCKS,),
            in_specs=[
                pl.BlockSpec((8, LEN), lambda j, *_: (0, j)), rows_of(QW), rows_of(QW),
                rows_of(QW), whole(QW, QW), whole(QW, QW), whole(1, QW),
            ],
            out_specs=[
                moved_columns(QW), first_rows(D), second_rows(D), rows_of(QW), rows_of(QW),
                whole(8, QW),
            ],
        ),
        out_shape=[
            shape((QW, 2 * ROWS), bf16), shape((ROWS, D), bf16), shape((ROWS, D), bf16),
            shape((2 * ROWS, QW), f32), shape((2 * ROWS, QW), bf16), shape((8, QW), f32),
        ],
        compiler_params=params(),
        cost_estimate=cost(2),
        name="finish",
    )(place, stats, gate, grad_shaped, scanned, *w_out, gain)


def run_backward(
    place, sequence, half, proj, filtered, scanned, grad, mem, conv, head, skip, carried, buffers
):
    per = BLOCKS // 2
    top = sequence * BLOCKS + (half + 1) * per - 1

    def back(width):
        return pl.BlockSpec((LEN, width), lambda i, *_: (top - i, 0))

    args = [place, proj, filtered, scanned, grad, mem, conv, head, skip, *carried]
    return pl.pallas_call(
        backward_kernel,
        grid_spec=pltpu.PrefetchScalarGridSpec(
            num_scalar_prefetch=1,
            grid=(per,),
            in_specs=[
                back(WIDE), back(WIDE), back(QW), back(QW),
                pl.BlockSpec((1, STATE, QW), lambda i, *_: (top - i, 0, 0)),
                whole(8, WIDE), whole(8, 128), whole(1, QW), whole(8, QC), whole(STATE, QW),
            ] + [pl.BlockSpec(memory_space=pl.ANY)] * len(buffers),
            out_specs=[
                back(WIDE), whole(8, QC), whole(8, 128), whole(8, QW), whole(8, QC),
                whole(STATE, QW),
            ],
            scratch_shapes=[pltpu.VMEM((LEN + 8, QC), f32), pltpu.VMEM((STATE, QW), f32)],
        ),
        out_shape=[
            shape((2 * ROWS, WIDE), bf16), shape((8, QC), f32), shape((8, 128), f32),
            shape((8, QW), f32), shape((8, QC), f32), shape((STATE, QW), f32),
        ],
        input_output_aliases={len(args) + n: n for n in range(len(buffers))},
        compiler_params=params(),
        cost_estimate=cost(2),
        name="backward_scan",
    )(*args, *buffers)


def run_outer(left, rights):
    tall, width = left.shape[0], rights[0].shape[1]
    tile = 384
    return pl.pallas_call(
        outer_kernel,
        grid=(tall // tile,),
        in_specs=[pl.BlockSpec((tile, 2 * ROWS), lambda i: (i, 0))]
        + [whole(HALF, width) for _ in rights],
        out_specs=pl.BlockSpec((tile, width), lambda i: (i, 0)),
        out_shape=shape((tall, width), bf16),
        compiler_params=params(),
        cost_estimate=cost(1),
        name="weight_grad",
    )(left, *rights)


def run_pieces(place, left, right, chips, weights, columns, others=()):
    tall, width = left.shape[0], right.shape[1]
    tile = 384
    chip_rows = tall // (2 * chips)
    dims = (chips,) + (2,) * (2 if others else 1) + (chip_rows, width)

    def block(column):
        return pl.BlockSpec((tile, GC), lambda i, *_: (i, column))

    beside_specs = []
    if others:
        part = others[1].shape
        beside_specs = [
            pl.BlockSpec(part, lambda i, place: (0, 0, 0, place[1])),
            whole(*part),
        ]
    return pl.pallas_call(
        functools.partial(pieces_kernel, chip_rows, len(columns)),
        grid_spec=pltpu.PrefetchScalarGridSpec(
            num_scalar_prefetch=1,
            grid=(tall // tile,),
            in_specs=[
                pl.BlockSpec((tile, 2 * ROWS), lambda i, *_: (i, 0)), whole(*right.shape),
            ] + [block(column) for column in columns] + beside_specs,
            out_specs=[whole(*dims), pl.BlockSpec((8, tile), lambda i, *_: (0, i))],
        ),
        out_shape=[shape(dims, bf16), shape((8, tall), f32)],
        compiler_params=params(),
        cost_estimate=cost(1),
        name="weight_grad",
    )(place, left, right, *([weights] * len(columns)), *others)


def tokens_grad_kernel(tok, cot, gain, near, core, *rest):
    sides, out = rest[:-1], rest[-1]
    i = pl.program_id(0)
    rows = out.shape[0]
    parts = [ref[n : n + rows, :] for ref in sides for n in range(0, ref.shape[0], rows)]
    side = parts[0]
    for n in range(1, len(parts)):
        side = jnp.where(i == n, parts[n], side)
    grad = near[...].astype(f32) + core[...].astype(f32) + side.astype(f32)
    wide = tok[...].astype(f32)
    inv_one = lax.rsqrt(jnp.mean(wide * wide, axis=1, keepdims=True) + norm_epsilon)
    unit = wide * inv_one
    lifted = grad * gain[...]
    mean = jnp.mean(lifted * unit, axis=1, keepdims=True)
    out[...] = cot[...].astype(f32) + inv_one * (lifted - unit * mean)


def run_tokens_grad(tokens, cotangent, gain, near, core, sides):
    rows = min(part.shape[0] for part in sides)
    block = pl.BlockSpec((rows, D), lambda i: (i, 0))
    return pl.pallas_call(
        tokens_grad_kernel,
        grid=(HALF // rows,),
        in_specs=[block, block, whole(1, D), block, block]
        + [whole(*part.shape) for part in sides],
        out_specs=block,
        out_shape=shape((HALF, D), f32),
        compiler_params=params(),
        cost_estimate=cost(4),
        name="tokens_grad",
    )(tokens, cotangent, gain, near, core, *sides)


def run_input_grad(place, sequence, far, gate_grad, wide_grad, w_gate, w_wide):
    per = BLOCKS // 2

    def rows(width):
        def index(j, place):
            half = 1 - place[0] if far else place[0]
            return (sequence * BLOCKS + half * per + j, 0)

        return pl.BlockSpec((LEN, width), index)

    return pl.pallas_call(
        input_grad_kernel,
        grid_spec=pltpu.PrefetchScalarGridSpec(
            num_scalar_prefetch=1,
            grid=(per,),
            in_specs=[rows(QW), rows(WIDE), whole(D, QW), whole(D, WIDE)],
            out_specs=rows_of(D),
        ),
        out_shape=shape((HALF, D), bf16),
        compiler_params=params(),
        cost_estimate=cost(1),
        name="input_grad",
    )(place, gate_grad, wide_grad, w_gate, w_wide)


def other_side(block):
    return lax.ppermute(block, "seq", [(0, 1), (1, 0)])


def after(block, *others):
    return lax.optimization_barrier((block, *others))[0]


def tie(*blocks):
    return lax.optimization_barrier(blocks)


def flip(block, bit):
    count = lax.axis_size("dp")
    return lax.ppermute(block, "dp", [(d, d ^ bit) for d in range(count)])


def other_core(block):
    return flip(block, 1)


def beside(block):
    return flip(block, 2)


def along(block):
    count = lax.axis_size("dp")
    return lax.ppermute(block, "dp", [(d, (d + 4) % count) for d in range(count)])


def in_order(place, own, received, axis=0):
    return jnp.where(
        place == 0,
        jnp.concatenate([own, received], axis=axis),
        jnp.concatenate([received, own], axis=axis),
    )


def pick(block, place, axis):
    return lax.dynamic_index_in_dim(block, place, axis, False)


class Spread:
    def __init__(self, piece, groups, put, base, hold=()):
        dp = lax.axis_index("dp")
        self.ring, self.beside_place = dp // 4, (dp // 2) % 2
        self.groups, self.put, self.base = groups, put, base
        self.hop, self.current = 0, piece
        self.neighbour = beside(after(piece, *hold) if hold else piece)

    def place(self, hold=()):
        origin = (self.ring + self.groups - self.hop) % self.groups
        current, neighbour = self.current, self.neighbour
        if hold:
            current, neighbour, *_ = tie(current, neighbour, *hold)
        self.base = self.put(self.base, current, 2 * origin + self.beside_place)
        self.base = self.put(self.base, neighbour, 2 * origin + 1 - self.beside_place)

    def step(self, hold=(), place_hold=()):
        moved = along(self.current)
        if hold:
            moved = after(moved, *hold)
        self.place(place_hold)
        self.hop, self.current, self.neighbour = self.hop + 1, moved, beside(moved)
        return moved


class Collect:
    def __init__(self, block_of, groups):
        dp = lax.axis_index("dp")
        self.ring, self.beside_place = dp // 4, (dp // 2) % 2
        self.block_of, self.groups = block_of, groups
        self.hop, self.total = 0, None
        self.first = self.block(1 - self.beside_place)
        self.received = beside(self.first)

    def block(self, place):
        target = (self.ring + 2 * self.groups - 1 - self.hop) % self.groups
        return self.block_of(2 * target + place)

    def step(self, *hold):
        received = after(self.received, *hold) if hold else self.received
        part = self.block(self.beside_place).astype(f32) + received.astype(f32)
        if self.hop:
            part = part + self.total.astype(f32)
        part = part.astype(bf16)
        self.hop += 1
        if self.hop < self.groups:
            part, following = tie(part, self.block(1 - self.beside_place))
            self.total = along(part)
            self.received = beside(following)
        return part

    def rest(self):
        part = None
        while self.hop < self.groups:
            part = self.step()
        return part


def gather_small(row, hold, later):
    dp = lax.axis_index("dp")
    block = row.reshape((1, 1) + row.shape)
    block = hold(in_order(lax.axis_index("seq"), block, other_side(block), axis=0))
    bit = 1
    while bit < lax.axis_size("dp"):
        received = flip(block, bit)
        if bit in later:
            received = after(received, later[bit])
        block = in_order((dp // bit) % 2, block, received, axis=1)
        bit *= 2
    return block.reshape((-1,) + row.shape)


def sum_small(block, bit, hold):
    while bit < lax.axis_size("dp"):
        block = block + after(flip(block, bit), hold)
        bit *= 2
    return block


def columns_of(block, half):
    return lax.dynamic_slice(block, (0, half * QW), (block.shape[0], QW))


def adamw_step(weight, moment, square, gradient, step_rate, decay_rate):
    moment_new = beta_first * moment + (1.0 - beta_first) * gradient
    square_new = beta_second * square + (1.0 - beta_second) * gradient * gradient
    first_fix = moment_new / (1.0 - beta_first**STEP)
    second_fix = square_new / (1.0 - beta_second**STEP)
    weight_new = weight - step_rate * (
        first_fix / (jnp.sqrt(second_fix) + adam_epsilon) + decay_rate * weight
    )
    return (weight_new, moment_new, square_new)


def to_side(halves_of, side):
    return in_order(side, halves_of(side)[None], other_side(halves_of(1 - side))[None])


def to_core(pair, quarter_of, core):
    return in_order(
        core, quarter_of(pair, core)[:, None], other_core(quarter_of(pair, 1 - core))[:, None], 1
    )


def from_cores(piece, core):
    return in_order(core, pick(piece, core, 1), other_core(pick(piece, 1 - core, 1)), 2)


def from_sides(cores, side, *hold):
    received = after(other_side(pick(cores, 1 - side, 0)), *hold)
    return in_order(side, pick(cores, side, 0), received, 1)


def from_cores_shared(piece, core):
    mine, got = pick(piece, core, 1), other_core(pick(piece, 1 - core, 1))
    cores = in_order(core, mine[:, :, :QW], got[:, :, :QW], 2)
    shared = (mine[:, :, QW:].astype(f32) + got[:, :, QW:].astype(f32)).astype(bf16)
    return jnp.concatenate([cores, shared], axis=2)


def from_sides_shared(both, side):
    mine, got = pick(both, side, 0), other_side(pick(both, 1 - side, 0))
    sides = in_order(side, mine[:, : 2 * QW], got[:, : 2 * QW], 1)
    return sides, mine[:, 2 * QW :].astype(f32) + got[:, 2 * QW :].astype(f32)


def on_device(
    tokens,
    cotangent,
    in_weight,
    in_moment,
    in_square,
    out_weight,
    out_moment,
    out_square,
    conv_table,
    conv_moment,
    conv_square,
    norm_gains,
    gain_moment,
    gain_square,
    head_table,
    head_moment,
    head_square,
):
    side = lax.axis_index("seq")
    dp = lax.axis_index("dp")
    core = dp % 2
    groups = lax.axis_size("dp") // 4
    chips = 2 * groups
    quarter = 2 * side + core
    number = side * lax.axis_size("dp") + dp
    turn = quarter * QH
    place = jnp.stack([side, core, 128 - turn, turn]).astype(jnp.int32)
    in_rows, out_rows = in_weight.shape[0], out_weight.shape[0]
    chip_rows = 2 * in_rows

    low = in_weight.astype(bf16)
    shared_own = jnp.pad(low[:, 2 * DI :], ((0, 0), (0, GC - 2 * STATE - HEADS)))

    def wide_half(side):
        own = lax.dynamic_slice(low, (0, DI + side * 2 * QW), (in_rows, 2 * QW))
        return jnp.concatenate([own, shared_own], axis=1)

    def wide_quarter(pair, core):
        own = lax.dynamic_slice(pair, (0, 0, core * QW), (2, in_rows, QW))
        return jnp.concatenate([own, pair[:, :, 2 * QW :]], axis=2)

    def gate_half(side):
        return lax.dynamic_slice(low, (0, side * 2 * QW), (in_rows, 2 * QW))

    def gate_quarter(pair, core):
        return lax.dynamic_slice(pair, (0, 0, core * QW), (2, in_rows, QW))

    wide_pair = to_side(wide_half, side)
    low, wide_pair = tie(low, wide_pair)
    gate_pair = to_side(gate_half, side)
    wide_piece = to_core(wide_pair, wide_quarter, core).reshape(2, chip_rows, WIDE)
    gate_piece = to_core(gate_pair, gate_quarter, core).reshape(4 * in_rows, QW)

    def put_in(base, piece, chip):
        return lax.dynamic_update_slice(base, piece[:, None], (0, chip, 0, 0))

    wide_spread = Spread(
        wide_piece, groups, put_in, jnp.zeros((2, chips, chip_rows, WIDE), bf16)
    )

    conv_width, gain_width = conv_table.shape[1], norm_gains.shape[0]
    small_size = 5 * conv_width + gain_width
    small_pad = -(-small_size // 128) * 128
    small_row = jnp.concatenate(
        [conv_table.astype(bf16).reshape(-1), norm_gains.astype(bf16)]
    )
    wide_hops = [wide_spread.step() for _ in range(groups - 1)]
    small_all = gather_small(
        jnp.pad(small_row, (0, small_pad - small_size)),
        lambda block: after(block, wide_hops[0]),
        {4: wide_hops[1]},
    )
    small_all = after(small_all, wide_hops[-1])
    devices = small_all.shape[0]
    conv_full = small_all[:, : 5 * conv_width].reshape(devices, 5, conv_width)
    conv_full = conv_full.transpose(1, 0, 2).reshape(5, CH).astype(f32)
    gains_full = small_all[:, 5 * conv_width : small_size].reshape(1, D + DI).astype(f32)
    first_gain = gains_full[:, :D]
    second_gain = lax.dynamic_slice(gains_full, (0, D + quarter * QW), (1, QW))
    conv_own = jnp.concatenate(
        [lax.dynamic_slice(conv_full, (0, quarter * QW), (5, QW)), conv_full[:, DI:]], axis=1
    )
    conv_own = jnp.pad(conv_own, ((0, 3), (0, WIDE - QC)))
    head_own = lax.dynamic_slice(head_table, (0, quarter * QH), (3, QH))
    head_rows = jnp.concatenate([-jnp.exp(head_own[0:1]), head_own[1:2]], axis=0)
    head_rows = jnp.pad(head_rows, ((0, 6), (0, 128 - QH)))
    skip = jnp.repeat(head_own[2:3], HEAD_DIM, axis=1)

    small = (first_gain, second_gain, conv_own, head_rows, skip)
    wide_spread.place()
    w_wide = wide_spread.base.reshape(D, WIDE)

    tokens_sent, gate_piece = tie(tokens, gate_piece)
    tok_far = other_side(tokens_sent)
    cotangent_sent, tok_far = tie(cotangent, tok_far)
    tok_near_b, tok_far_b = other_core(tokens), other_core(tok_far)

    out_low = out_weight.astype(bf16)
    out_piece = in_order(
        core, columns_of(out_low, core), other_core(columns_of(out_low, 1 - core))
    )
    both_piece = jnp.stack([gate_piece, out_piece]).reshape(2, 2, chip_rows, QW)
    both_piece = after(both_piece, wide_hops[-1])

    def keep(base, piece, chip):
        return base + [(piece, chip)]

    both_spread = Spread(both_piece, groups, keep, [], (w_wide,))
    cot_far = other_side(cotangent_sent)
    cots = (cotangent, cot_far, other_core(cotangent), other_core(cot_far))

    start = (jnp.zeros((8, QC), f32), jnp.zeros((STATE, QW), f32))
    buffers, carried = None, start
    gain = first_gain
    for part in range(4):
        near, far = (tok_near_b, tok_far_b) if part >= 2 else (tokens, tok_far)
        *buffers, tail, state = run_forward(
            place, near, far, gain, w_wide, conv_own, head_rows, skip,
            carried if part % 2 else start, buffers, part,
        )
        carried = (tail, state)
        if both_spread.hop < groups - 1:
            moved = both_spread.step((buffers[0],), (buffers[0],))
            waits = [piece for piece, _ in both_spread.base[-2:]]
            gain = after(first_gain, moved, *waits)
    while both_spread.hop < groups - 1:
        both_spread.step()
    both_spread.place((buffers[0],))
    pieces, origins = zip(*both_spread.base)
    w_gate, w_own, w_send = run_assemble(
        jnp.concatenate([place, jnp.stack(origins).astype(jnp.int32)]), pieces
    )
    w_gate = w_gate.reshape(D, QW)
    w_out = (w_own.reshape(QW, QW), other_core(w_send).reshape(QW, QW))
    normed, normed_turned, proj, filtered, scanned, mem = buffers
    gate, grad_shaped, stats = run_gate(
        place, normed, w_gate, cots, w_out, second_gain, scanned
    )
    stats = stats + other_side(stats)
    swapped = other_core(stats)
    stats = stats + jnp.concatenate([swapped[:, ROWS:], swapped[:, :ROWS]], axis=1)
    shaped_turned, layer_a, layer_b, scan_grad, gate_grad, gain_grad = run_finish(
        place, stats, gate, grad_shaped, scanned, w_out, second_gain
    )

    layer_far = other_core(layer_b)
    out_grad = run_outer(shaped_turned, cots)
    layer_far, out_grad = tie(layer_far, out_grad)
    layer_send = (layer_a[HALF:].astype(f32) + layer_far[HALF:].astype(f32)).astype(bf16)
    layer_side = other_side(layer_send)

    split = (chips // 2, 2, chip_rows)
    out_far = other_core(columns_of(out_grad, 1 - core)).reshape(*split, QW)
    out_pieces = (out_grad.reshape(*split, D), out_far)
    both_pieces, gate_dots = run_pieces(
        place, normed_turned, after(gate_grad, layer_send), chips, w_gate, (0, 1), out_pieces
    )

    def blocks_of(pieces):
        return lambda chip: pick(pieces, chip, 0)

    both_sums = Collect(blocks_of(both_pieces), groups)

    waits = (both_pieces,)
    buffers, sums = (), []
    for sequence in (1, 0):
        carried = start
        for half in (1, 0):
            wide_grad, *part_sums, later, state = run_backward(
                place, sequence, half, proj, filtered, scanned, after(scan_grad, *waits), mem,
                conv_own, head_rows, skip, carried, buffers,
            )
            buffers, carried = (wide_grad,), (later, state)
            sums.append(part_sums)
            both_sum = both_sums.step(part_sums[0])
            waits = (both_sum,)
            if len(sums) == 2:
                waits = (both_sum, layer_side)
    both_sum = both_sums.rest() if groups > 4 else both_sum
    conv_grad, head_grad, skip_grad = (sum(parts[1:], parts[0]) for parts in zip(*sums))
    rest_pieces, rest_dots = run_pieces(
        place, normed_turned, after(wide_grad, both_sum), chips, w_wide, (0, 1, 2)
    )
    rest_sums = Collect(blocks_of(rest_pieces), groups)
    both_sum, wide_grad = tie(both_sum, wide_grad)
    gate_cores = from_cores(both_sum[0].reshape(2, 2, in_rows, QW), core)
    out_rows_sum = both_sum[1].reshape(2, out_rows, QW)
    out_rows_far = other_core(pick(out_rows_sum, 1 - core, 0))

    skip_grad = skip_grad[0].reshape(QH, HEAD_DIM).sum(axis=1)
    conv_all = jnp.concatenate(
        [
            lax.dynamic_update_slice(
                jnp.zeros((5, DI), f32), conv_grad[:5, :QW], (0, quarter * QW)
            ),
            conv_grad[:5, QW:],
        ],
        axis=1,
    )
    gains_all = jnp.concatenate(
        [
            (gate_dots + rest_dots)[0:1] / first_gain,
            lax.dynamic_update_slice(jnp.zeros((1, DI), f32), gain_grad[0:1], (0, quarter * QW)),
        ],
        axis=1,
    )
    heads_all = lax.dynamic_update_slice(
        jnp.zeros((3, HEADS), f32),
        jnp.concatenate([head_grad[0:2, :QH], skip_grad[None]], axis=0),
        (0, quarter * QH),
    )
    packed = jnp.concatenate(
        [
            conv_all.reshape(-1, 128),
            gains_all.reshape(-1, 128),
            jnp.pad(heads_all.reshape(-1), (0, 256 - 3 * HEADS)).reshape(2, 128),
        ],
        axis=0,
    )

    def input_rows(sequence, far, *waits):
        return run_input_grad(
            place, sequence, far, gate_grad, after(wide_grad, *waits), w_gate, w_wide
        )

    far_b = input_rows(1, True, rest_sums.first, packed, gate_cores, out_rows_far)
    far_core = other_core(far_b)
    packed = packed + after(other_side(packed), far_b)
    far_a = input_rows(0, True, packed)
    rest_sum = rest_sums.step(far_a)
    gate_sum = from_sides(gate_cores, side, rest_sum)
    packed = packed + after(other_core(packed), far_a)
    grad_send = (far_a.astype(f32) + far_core.astype(f32)).astype(bf16)
    near_b = input_rows(1, False, rest_sum, grad_send, packed, gate_sum)
    part = HALF // 4
    sides = [other_side(grad_send[:part])]
    near_core = other_core(near_b)
    sides[0], near_b = tie(sides[0], near_b)
    rest_sum = rest_sums.step(sides[0])
    near_a = input_rows(0, False, rest_sum)
    sides.append(other_side(grad_send[part : 2 * part]))
    sides.append(other_side(grad_send[2 * part : 3 * part]))
    sides[1], near_a = tie(sides[1], near_a)
    rest_sum = rest_sums.step(sides[1])
    out_rows_sum = after(out_rows_sum, rest_sum)
    layer_side = after(layer_side, rest_sum)
    layer_out = (
        tokens.astype(f32) + layer_a[:HALF].astype(f32) + layer_far[:HALF].astype(f32)
    ) + layer_side.astype(f32)
    sides[2], rest_sum, layer_out = tie(sides[2], rest_sum, layer_out)
    rest_sum = rest_sums.step(sides[2])
    if rest_sums.hop < groups:
        rest_sum = rest_sums.rest()
    sides.append(other_side(grad_send[3 * part :]))
    out_grad = in_order(core, pick(out_rows_sum, core, 0), out_rows_far, axis=1).astype(f32)

    both_group, rest_sum = tie(
        from_cores_shared(rest_sum.reshape(2, 2, in_rows, WIDE), core), rest_sum
    )
    packed = after(packed, rest_sum)
    packed = packed + after(flip(packed, 2), both_group)
    rest_sum, shared_sum = from_sides_shared(both_group, side)
    packed = packed + after(flip(packed, 4), rest_sum)
    tokens_grad = run_tokens_grad(
        tokens, cotangent, after(first_gain, rest_sum), near_a, near_core, sides
    )
    packed = sum_small(packed, 8, tokens_grad)
    conv_rows, gain_rows = 5 * CH // 128, (D + DI) // 128
    conv_sum = lax.dynamic_slice(
        packed[:conv_rows].reshape(5, CH), (0, number * conv_width), (5, conv_width)
    )
    gains_sum = lax.dynamic_slice(
        packed[conv_rows : conv_rows + gain_rows].reshape(-1), (number * gain_width,), (gain_width,)
    )
    head_sum = packed[conv_rows + gain_rows :].reshape(-1)[: 3 * HEADS].reshape(3, HEADS)

    in_grad = jnp.concatenate(
        [gate_sum.astype(f32), rest_sum.astype(f32), shared_sum[:, : 2 * STATE + HEADS]], axis=1
    )
    in_new = adamw_step(in_weight, in_moment, in_square, in_grad, rate_matrix, weight_decay)
    out_new = adamw_step(out_weight, out_moment, out_square, out_grad, rate_matrix, weight_decay)
    conv_new = adamw_step(conv_table, conv_moment, conv_square, conv_sum, rate_vector, 0.0)
    gains_new = adamw_step(norm_gains, gain_moment, gain_square, gains_sum, rate_vector, 0.0)
    head_new = adamw_step(head_table, head_moment, head_square, head_sum, rate_heads, 0.0)
    return (layer_out, tokens_grad, *in_new, *out_new, *conv_new, *gains_new, *head_new)


def solution(mesh):
    tokens = P(("dp", "seq"), None)
    rows = P(("seq", "dp"), None)
    columns = P(None, ("seq", "dp"))
    line = P(("seq", "dp"))
    return jax.shard_map(
        on_device,
        mesh=mesh,
        in_specs=(tokens,) * 2 + (rows,) * 6 + (columns,) * 3 + (line,) * 3 + (P(),) * 3,
        out_specs=(tokens,) * 2 + (rows,) * 6 + (columns,) * 3 + (line,) * 3 + (P(),) * 3,
        check_vma=False,
    )
```

profile of v0, /device:TPU:0, one launch (start us, length us, event | category | flops | bytes accessed | tf_op | source)
XLA Modules:
  0.0 441.9 jit_solution(3081033812241937017)
XLA Ops:
  0.7 1.4 convert_element_type.216
  2.4 3.0 collective-permute-start.1
  10.4 1.8 collective-permute-start.2
  12.4 3.3 collective-permute-done.2
  15.8 1.9 collective-permute-start.8
  17.8 1.6 collective-permute-start.17
  19.7 1.6 collective-permute-start.4
  21.3 6.8 %collective-permute-done.8 = bf16[2,96,1152]{2,1,0:T(8,128)(2,1)S(1)} collective-permute-done((bf16[2,96,1152]{2,1,0:T(8,128)(2,1)S(1)}, bf16[2,96,1152]{2,1,0:T(8,128)(2,1)S(1)}, u32[]{:S(2)}, u32[]{:S(2)}) %collective-permute-start.8) | collective-permute-done | bytes 442400 | tf_op jit(solution)/shard_map/ppermute | solution.py:789
  29.0 1.5 collective-permute-start.18
  31.9 9.7 %collective-permute-done.10 = bf16[2,2,768]{2,1,0:T(2,128)(2,1)S(1)} collective-permute-done((bf16[2,2,768]{2,1,0:T(2,128)(2,1)S(1)}, bf16[2,2,768]{2,1,0:T(2,128)(2,1)S(1)}, u32[]{:S(2)}, u32[]{:S(2)}) %collective-permute-start.10) | collective-permute-done | bytes 6176 | tf_op jit(solution)/shard_map/ppermute | solution.py:776
  41.8 3.6 collective-permute-done.11
  46.5 1.5 collective-permute-start.19
  50.6 10.2 %collective-permute-done.14 = bf16[2,96,1152]{2,1,0:T(8,128)(2,1)} collective-permute-done((bf16[2,96,1152]{2,1,0:T(8,128)(2,1)}, bf16[2,96,1152]{2,1,0:T(8,128)(2,1)}, u32[]{:S(2)}, u32[]{:S(2)}) %collective-permute-start.14) | collective-permute-done | bytes 442400 | tf_op jit(solution)/shard_map/ppermute | solution.py:789
  62.1 1.6 reshape.274
  63.8 1.6 copy.72
  65.3 1.6 reshape.265
  67.7 1.5 reshape.264
  74.6 1.5 collective-permute-start.27
  76.1 4.4 collective-permute-done.20
  83.1 13.2 %forward_scan.4 = (bf16[2048,1536]{1,0:T(8,128)(2,1)}, bf16[1536,2048]{1,0:T(8,128)(2,1)}, f32[2048,1152]{1,0:T(8,128)}, f32[2048,1152]{1,0:T(8,128)}, f32[2048,...) custom-call(s32[4]{0:T(128)} %pad_add_fusion.place, bf16[512,1536]{1,0:T(8,128)(2,1)} %tok.1, ...), custom_call_target="tpu_custom_call" | custom-call | flops 12999999488 | bytes 45500000 | tf_op jit(solution)/shard_map/forward_scan/pallas_call | solution.py:495
  98.6 13.3 %forward_scan.5 = (bf16[2048,1536]{1,0:T(8,128)(2,1)}, bf16[1536,2048]{1,0:T(8,128)(2,1)}, f32[2048,1152]{1,0:T(8,128)}, f32[2048,1152]{1,0:T(8,128)}, f32[2048,...) custom-call(s32[4]{0:T(128)} %pad_add_fusion.place, ...), custom_call_target="tpu_custom_call", output_to_operand_aliasing={{0}: (10, {}), {1}: (11, {}), {2}: (12, {}), {3}: (13, {}),... | custom-call | flops 12999999488 | bytes 45500000 | tf_op jit(solution)/shard_map/forward_scan/pallas_call | solution.py:495
  112.0 1.5 collective-permute-start.25
  113.8 13.2 %forward_scan.6 = (bf16[2048,1536]{1,0:T(8,128)(2,1)}, bf16[1536,2048]{1,0:T(8,128)(2,1)}, f32[2048,1152]{1,0:T(8,128)}, f32[2048,1152]{1,0:T(8,128)}, f32[2048,...) custom-call(s32[4]{0:T(128)} %pad_add_fusion.place, ...), custom_call_target="tpu_custom_call", output_to_operand_aliasing={{0}: (10, {}), {1}: (11, {}), {2}: (12, {}), {3}: (13, {}),... | custom-call | flops 12999999488 | bytes 45500000 | tf_op jit(solution)/shard_map/forward_scan/pallas_call | solution.py:495
  128.1 2.9 collective-permute-done.23.refs_6_
  131.6 13.2 %forward_scan.7 = (bf16[2048,1536]{1,0:T(8,128)(2,1)}, bf16[1536,2048]{1,0:T(8,128)(2,1)}, f32[2048,1152]{1,0:T(8,128)}, f32[2048,1152]{1,0:T(8,128)}, f32[2048,...) custom-call(s32[4]{0:T(128)} %pad_add_fusion.place, ...), custom_call_target="tpu_custom_call", output_to_operand_aliasing={{0}: (10, {}), {1}: (11, {}), {2}: (12, {}), {3}: (13, {}),... | custom-call | flops 12999999488 | bytes 45500000 | tf_op jit(solution)/shard_map/forward_scan/pallas_call | solution.py:495
  145.9 5.9 %assemble.1 = (bf16[2,8,96,768]{3,2,1,0:T(8,128)(2,1)}, bf16[4,2,96,768]{3,2,1,0:T(8,128)(2,1)}, bf16[4,2,96,768]{3,2,1,0:T(8,128)(2,1)}) custom-call(s32[12]{0:T(128)} %concatenate.191.place, bf16[2,2,96,768]{3,2,1,0:T(8,128)(2,1)} %pad_maximum_fusion.1.refs_0_, bf16[2,2,96,768]{3,2,1,0:T(8,128)(2,1)} %collective-permute-done.22.refs_1_, ...), custom_call_target="tpu_custom_call" | custom-call | flops 3000000000 | bytes 10500000 | tf_op jit(solution)/shard_map/assemble/pallas_call | solution.py:546
  152.4 2.6 collective-permute-done.30
  155.0 18.7 %gate_and_stats.1 = (f32[2048,768]{1,0:T(8,128)}, f32[2048,768]{1,0:T(8,128)}, f32[8,2048]{1,0:T(8,128)}) custom-call(s32[4]{0:T(128)} %pad_add_fusion.place, bf16[2048,1536]{1,0:T(8,128)(2,1)} %get-tuple-element.199.normed, bf16[1536,768]{1,0:T(8,128)(2,1)} %bitcast.158, bf16[512,1536]{1,0:T(8,128)(2,1)} %cot.1, ...), custom_call_target="tpu_custom_call" | custom-call | flops 2000000000 | bytes 7000000 | tf_op jit(solution)/shard_map/gate_and_stats/pallas_call | solution.py:571
  175.0 3.2 collective-permute-done.31
  181.0 21.1 %finish.1 = (bf16[768,2048]{1,0:T(8,128)(2,1)}, bf16[1024,1536]{1,0:T(8,128)(2,1)}, bf16[1024,1536]{1,0:T(8,128)(2,1)}, f32[2048,768]{1,0:T(8,128)}, bf16[2048,768]{1,0:T(8,128)(2,1)}, /*index=5*/f32[8,768]{1,0:T(8,128)}) custom-call(s32[4]{0:T(128)} %pad_add_fusion.place, f32[8,2048]{1,0:T(8,128)} %maximum_add_fusion.stats, ...), custom_call_target="tpu_custom_call" | custom-call | flops 2000000000 | bytes 7000000 | tf_op jit(solution)/shard_map/finish/pallas_call | solution.py:594
  202.4 9.7 %weight_grad.3 = bf16[768,1536]{1,0:T(8,128)(2,1)} custom-call(bf16[768,2048]{1,0:T(8,128)(2,1)} %get-tuple-element.214.left, bf16[512,1536]{1,0:T(8,128)(2,1)} %cot.1, bf16[512,1536]{1,0:T(8,128)(2,1)} %collective-permute-done.27.cot_fa.rest_1_, bf16[512,1536]{1,0:T(8,128)(2,1)} %copy-done.3, bf16[512,1536]{1,0:T(8,128)(2,1)} %collective-permute-done.29.cot_fb.rest_3_), custom_call_target="tpu_custom_call" | custom-call | flops 1000000000 | bytes 3500000 | tf_op jit(solution)/shard_map/weight_grad/pallas_call | solution.py:658
  212.1 2.4 constant_dynamic-slice_fusion.1
  214.8 2.9 add_convert_fusion.1
  217.7 12.3 %weight_grad.4 = (bf16[8,2,2,96,768]{4,3,2,1,0:T(8,128)(2,1)}, f32[8,1536]{1,0:T(8,128)}) custom-call(s32[4]{0:T(128)} %pad_add_fusion.place, bf16[1536,2048]{1,0:T(8,128)(2,1)} %get-tuple-element.211.left, bf16[2048,768]{1,0:T(8,128)(2,1)} %get-tuple-element.216.right.refs_0_, bf16[1536,768]{1,0:T(8,128)(2,1)} %bitcast.159, bf16[1536,768]{1,0:T(8,128)(2,1)} %bitcast.160, ...), custom_call_target="tpu_custom_call" | custom-call | flops 1000000000 | bytes 3500000 | tf_op jit(solution)/shard_map/weight_grad/pallas_call | solution.py:687
  230.0 3.2 dynamic-slice_bitcast_fusion
  235.1 16.2 %backward_scan.4 = (bf16[2048,1152]{1,0:T(8,128)(2,1)}, f32[8,1024]{1,0:T(8,128)}, f32[8,128]{1,0:T(8,128)}, f32[8,768]{1,0:T(8,128)}, f32[8,1024]{1,0:T(8,128)}, /*index=5*/f32[128,768]{1,0:T(8,128)}) custom-call(s32[4]{0:T(128)} %pad_add_fusion.place, f32[2048,1152]{1,0:T(8,128)} %get-tuple-element.219.proj_in, ...), custom_call_target="tpu_custom_call" | custom-call | flops 2000000000 | bytes 7000000 | tf_op jit(solution)/shard_map/backward_scan/pallas_call | solution.py:628
  251.3 2.2 fusion.1
  254.9 16.5 %backward_scan.5 = (bf16[2048,1152]{1,0:T(8,128)(2,1)}, f32[8,1024]{1,0:T(8,128)}, f32[8,128]{1,0:T(8,128)}, f32[8,768]{1,0:T(8,128)}, f32[8,1024]{1,0:T(8,128)}, /*index=5*/f32[128,768]{1,0:T(8,128)}) custom-call(s32[4]{0:T(128)} %pad_add_fusion.place, f32[2048,1152]{1,0:T(8,128)} %get-tuple-element.219.proj_in, ...), custom_call_target="tpu_custom_call", output_to_operand_aliasing={{0}: (11, {})} | custom-call | flops 2000000000 | bytes 7000000 | tf_op jit(solution)/shard_map/backward_scan/pallas_call | solution.py:628
  271.6 2.4 fusion.3
  274.7 1.8 collective-permute-start.40
  277.3 16.1 %backward_scan.6 = (bf16[2048,1152]{1,0:T(8,128)(2,1)}, f32[8,1024]{1,0:T(8,128)}, f32[8,128]{1,0:T(8,128)}, f32[8,768]{1,0:T(8,128)}, f32[8,1024]{1,0:T(8,128)}, /*index=5*/f32[128,768]{1,0:T(8,128)}) custom-call(s32[4]{0:T(128)} %pad_add_fusion.place, f32[2048,1152]{1,0:T(8,128)} %get-tuple-element.219.proj_in, ...), custom_call_target="tpu_custom_call", output_to_operand_aliasing={{0}: (11, {})} | custom-call | flops 2000000000 | bytes 7000000 | tf_op jit(solution)/shard_map/backward_scan/pallas_call | solution.py:628
  293.5 1.7 fusion.5
  296.9 16.3 %backward_scan.7 = (bf16[2048,1152]{1,0:T(8,128)(2,1)}, f32[8,1024]{1,0:T(8,128)}, f32[8,128]{1,0:T(8,128)}, f32[8,768]{1,0:T(8,128)}, f32[8,1024]{1,0:T(8,128)}, /*index=5*/f32[128,768]{1,0:T(8,128)}) custom-call(s32[4]{0:T(128)} %pad_add_fusion.place, f32[2048,1152]{1,0:T(8,128)} %get-tuple-element.219.proj_in, ...), custom_call_target="tpu_custom_call", output_to_operand_aliasing={{0}: (11, {})} | custom-call | flops 2000000000 | bytes 7000000 | tf_op jit(solution)/shard_map/backward_scan/pallas_call | solution.py:628
  318.3 15.3 %weight_grad.5 = (bf16[8,2,96,1152]{3,2,1,0:T(8,128)(2,1)}, f32[8,1536]{1,0:T(8,128)}) custom-call(s32[4]{0:T(128)} %pad_add_fusion.place, bf16[1536,2048]{1,0:T(8,128)(2,1)} %get-tuple-element.211.left, bf16[2048,1152]{1,0:T(8,128)(2,1)} %get-tuple-element.277.right.refs_1_, bf16[1536,1152]{1,0:T(8,128)(2,1)} %bitcast.151, bf16[1536,1152]{1,0:T(8,128)(2,1)} %bitcast.152, ...), custom_call_target="tpu_custom_call" | custom-call | flops 1000000000 | bytes 3500000 | tf_op jit(solution)/shard_map/weight_grad/pallas_call | solution.py:687
  333.6 2.5 dynamic-slice_bitcast_fusion.4
  337.7 8.3 %input_grad.4 = bf16[512,1536]{1,0:T(8,128)(2,1)} custom-call(s32[4]{0:T(128)} %pad_add_fusion.place, bf16[2048,768]{1,0:T(8,128)(2,1)} %get-tuple-element.216.right.refs_0_, bf16[2048,1152]{1,0:T(8,128)(2,1)} %get-tuple-element.277.right.refs_1_, bf16[1536,768]{1,0:T(8,128)(2,1)} %bitcast.161, bf16[1536,1152]{1,0:T(8,128)(2,1)} %bitcast.154), custom_call_target="tpu_custom_call" | custom-call | flops 1000000000 | bytes 3500000 | tf_op jit(solution)/shard_map/input_grad/pallas_call | solution.py:747
  346.6 1.5 collective-permute-start.48
  348.1 2.8 collective-permute-done.43
  352.1 8.4 %input_grad.5 = bf16[512,1536]{1,0:T(8,128)(2,1)} custom-call(s32[4]{0:T(128)} %pad_add_fusion.place, bf16[2048,768]{1,0:T(8,128)(2,1)} %get-tuple-element.216.right.refs_0_, bf16[2048,1152]{1,0:T(8,128)(2,1)} %get-tuple-element.277.right.refs_1_, bf16[1536,768]{1,0:T(8,128)(2,1)} %bitcast.162, bf16[1536,1152]{1,0:T(8,128)(2,1)} %bitcast.155), custom_call_target="tpu_custom_call" | custom-call | flops 1000000000 | bytes 3500000 | tf_op jit(solution)/shard_map/input_grad/pallas_call | solution.py:747
  360.5 1.7 add.600
  362.2 1.9 fusion.10
  364.1 3.5 collective-permute-start.53
  368.2 1.8 add_convert_fusion
  373.2 8.3 %input_grad.6 = bf16[512,1536]{1,0:T(8,128)(2,1)} custom-call(s32[4]{0:T(128)} %pad_add_fusion.place, bf16[2048,768]{1,0:T(8,128)(2,1)} %get-tuple-element.216.right.refs_0_, bf16[2048,1152]{1,0:T(8,128)(2,1)} %get-tuple-element.277.right.refs_1_, bf16[1536,768]{1,0:T(8,128)(2,1)} %bitcast.163, bf16[1536,1152]{1,0:T(8,128)(2,1)} %bitcast.156), custom_call_target="tpu_custom_call" | custom-call | flops 1000000000 | bytes 3500000 | tf_op jit(solution)/shard_map/input_grad/pallas_call | solution.py:747
  382.2 2.1 fusion.12
  388.0 8.3 %input_grad.7.near = bf16[512,1536]{1,0:T(8,128)(2,1)} custom-call(s32[4]{0:T(128)} %pad_add_fusion.place, bf16[2048,768]{1,0:T(8,128)(2,1)} %get-tuple-element.216.right.refs_0_, bf16[2048,1152]{1,0:T(8,128)(2,1)} %get-tuple-element.277.right.refs_1_, bf16[1536,768]{1,0:T(8,128)(2,1)} %bitcast.164, bf16[1536,1152]{1,0:T(8,128)(2,1)} %bitcast.157), custom_call_target="tpu_custom_call" | custom-call | flops 1000000000 | bytes 3500000 | tf_op jit(solution)/shard_map/input_grad/pallas_call | solution.py:747
  396.3 2.0 collective-permute-done.55.rest_1_
  402.0 4.8 %convert_add_fusion = f32[512,1536]{1,0:T(8,128)} fusion(bf16[512,1536]{1,0:T(8,128)(2,1)S(1)} %copy-done.10, bf16[512,1536]{1,0:T(8,128)(2,1)} %tok.1, bf16[1024,1536]{1,0:T(8,128)(2,1)} %collective-permute-done.33, bf16[1024,1536]{1,0:T(8,128)(2,1)} %get-tuple-element.212), kind=kLoop, calls=%fused_computation | loop fusion | flops 5505024 | bytes 9437184 | tf_op jit(solution)/shard_map/add | solution.py:1177
  406.8 3.0 collective-permute-done.57
  409.9 1.5 collective-permute-done.58
  415.9 2.7 multiply_subtract_fusion.1
  418.8 9.3 %collective-permute-done.60 = bf16[48,1920]{1,0:T(8,128)(2,1)S(1)} collective-permute-done((bf16[48,1920]{1,0:T(8,128)(2,1)S(1)}, bf16[48,1920]{1,0:T(8,128)(2,1)S(1)}, u32[]{:S(2)}, u32[]{:S(2)}) %collective-permute-start.60) | collective-permute-done | bytes 184352 | tf_op jit(solution)/shard_map/ppermute | solution.py:763
  429.3 2.5 multiply_subtract_fusion
  432.6 6.6 %tokens_grad.1 = f32[512,1536]{1,0:T(8,128)} custom-call(bf16[512,1536]{1,0:T(8,128)(2,1)} %tok.1, bf16[512,1536]{1,0:T(8,128)(2,1)} %cot.1, f32[1,1536]{1,0:T(1,128)} %slice.165.gain, bf16[512,1536]{1,0:T(8,128)(2,1)} %input_grad.7.near, bf16[512,1536]{1,0:T(8,128)(2,1)} %collective-permute-done.61.core, bf16[128,1536]{1,0:T(8,128)(2,1)} %collective-permute-done.50.rest_0_, ...), custom_call_target="tpu_custom_call" | custom-call | flops 4000000000 | bytes 14000000 | tf_op jit(solution)/shard_map/tokens_grad/pallas_call | solution.py:724
  (298 shorter events, 68.0 us)
Async XLA Ops:
  2.4 7.8 %collective-permute-start.1 = (bf16[48,1920]{1,0:T(8,128)(2,1)S(1)}, bf16[48,1920]{1,0:T(8,128)(2,1)S(1)}, u32[]{:S(2)}, u32[]{:S(2)}) collective-permute-start(bf16[48,1920]{1,0:T(8,128)(2,1)S(1)} %get-tuple-element.350), channel_id=1, source_target_pairs={{0,16},{16,0},{1,17},{17,1},{2,18},{18,2},{3,19},{19,3},{4,20},{20... | collective-permute-start | bytes 552968 | tf_op jit(solution)/shard_map/ppermute | solution.py:763
  5.6 4.5 %collective-permute-start.6 = (bf16[1,1,768]{2,1,0:T(2,128)(2,1)S(1)}, bf16[1,1,768]{2,1,0:T(2,128)(2,1)S(1)}, u32[]{:S(2)}, u32[]{:S(2)}) collective-permute-start(bf16[1,1,768]{2,1,0:T(2,128)(2,1)S(1)} %concatenate.170), channel_id=1, source_target_pairs={{0,16},{16,0},{1,17},{17,1},{2,18},{18,2},{3,19},{19,3},{4,20},{20... | collective-permute-start | bytes 4616 | tf_op jit(solution)/shard_map/ppermute | solution.py:763
  5.7 4.4 collective-permute-start.15
  5.8 107.7 %collective-permute-start = (bf16[512,1536]{1,0:T(8,128)(2,1)}, bf16[512,1536]{1,0:T(8,128)(2,1)}, u32[]{:S(2)}, u32[]{:S(2)}) collective-permute-start(bf16[512,1536]{1,0:T(8,128)(2,1)} %tok.1), channel_id=1, source_target_pairs={{0,1},{1,0},{2,3},{3,2},{4,5},{5,4},{6,7},{7,6},{8,9},{9,8},{10,11... | collective-permute-start | bytes 4718600 | tf_op jit(solution)/shard_map/ppermute | solution.py:776
  10.4 5.2 %collective-permute-start.2 = (bf16[48,1536]{1,0:T(8,128)(2,1)S(1)}, bf16[48,1536]{1,0:T(8,128)(2,1)S(1)}, u32[]{:S(2)}, u32[]{:S(2)}) collective-permute-start(bf16[48,1536]{1,0:T(8,128)(2,1)S(1)} %get-tuple-element.325), channel_id=1, source_target_pairs={{0,16},{16,0},{1,17},{17,1},{2,18},{18,2},{3,19},{19,3},{4,20},{20... | collective-permute-start | bytes 442376 | tf_op jit(solution)/shard_map/ppermute | solution.py:763
  12.3 3.4 collective-permute-start.7
  15.8 12.3 %collective-permute-start.8 = (bf16[2,96,1152]{2,1,0:T(8,128)(2,1)S(1)}, bf16[2,96,1152]{2,1,0:T(8,128)(2,1)S(1)}, u32[]{:S(2)}, u32[]{:S(2)}) collective-permute-start(bf16[2,96,1152]{2,1,0:T(8,128)(2,1)S(1)} %bitcast.168), channel_id=1, source_target_pairs={{0,4},{1,5},{2,6},{3,7},{4,8},{5,9},{6,10},{7,11},{8,12},{9,13},{1... | collective-permute-start | bytes 1327112 | tf_op jit(solution)/shard_map/ppermute | solution.py:789
  17.7 2.0 collective-permute-start.3
  17.8 12.7 %collective-permute-start.17 = (bf16[2,96,1152]{2,1,0:T(8,128)(2,1)S(1)}, bf16[2,96,1152]{2,1,0:T(8,128)(2,1)S(1)}, u32[]{:S(2)}, u32[]{:S(2)}) collective-permute-start(bf16[2,96,1152]{2,1,0:T(8,128)(2,1)S(1)} %bitcast.169), channel_id=1, source_target_pairs={{0,2},{1,3},{2,0},{3,1},{4,6},{5,7},{6,4},{7,5},{8,10},{9,11},{10,... | collective-permute-start | bytes 1327112 | tf_op jit(solution)/shard_map/ppermute | solution.py:776
  19.7 54.8 %collective-permute-start.4 = (bf16[512,1536]{1,0:T(8,128)(2,1)}, bf16[512,1536]{1,0:T(8,128)(2,1)}, u32[]{:S(2)}, u32[]{:S(2)}) collective-permute-start(bf16[512,1536]{1,0:T(8,128)(2,1)} %tok.1), channel_id=1, source_target_pairs={{0,16},{16,0},{1,17},{17,1},{2,18},{18,2},{3,19},{19,3},{4,20},{20... | collective-permute-start | bytes 4718600 | tf_op jit(solution)/shard_map/ppermute | solution.py:763
  28.1 2.4 collective-permute-start.9
  29.0 19.0 %collective-permute-start.18 = (bf16[2,96,1152]{2,1,0:T(8,128)(2,1)S(1)}, bf16[2,96,1152]{2,1,0:T(8,128)(2,1)S(1)}, u32[]{:S(2)}, u32[]{:S(2)}) collective-permute-start(bf16[2,96,1152]{2,1,0:T(8,128)(2,1)S(1)} %collective-permute-done.8), channel_id=1, source_target_pairs={{0,2},{1,3},{2,0},{3,1},{4,6},{5,7},{6,4},{7,5},{8,10},{9,11},{10,... | collective-permute-start | bytes 1327112 | tf_op jit(solution)/shard_map/ppermute | solution.py:776
  30.5 15.0 %collective-permute-start.12 = (bf16[2,96,1152]{2,1,0:T(8,128)(2,1)S(1)}, bf16[2,96,1152]{2,1,0:T(8,128)(2,1)}, u32[]{:S(2)}, u32[]{:S(2)}) collective-permute-start(bf16[2,96,1152]{2,1,0:T(8,128)(2,1)S(1)} %collective-permute-done.8), channel_id=1, source_target_pairs={{0,4},{1,5},{2,6},{3,7},{4,8},{5,9},{6,10},{7,11},{8,12},{9,13},{1... | collective-permute-start | bytes 1327112 | tf_op jit(solution)/shard_map/ppermute | solution.py:789
  30.5 11.1 %collective-permute-start.10 = (bf16[2,2,768]{2,1,0:T(2,128)(2,1)S(1)}, bf16[2,2,768]{2,1,0:T(2,128)(2,1)S(1)}, u32[]{:S(2)}, u32[]{:S(2)}) collective-permute-start(bf16[2,2,768]{2,1,0:T(2,128)(2,1)S(1)} %broadcast_select_fusion.1), channel_id=1, source_target_pairs={{0,2},{1,3},{2,0},{3,1},{4,6},{5,7},{6,4},{7,5},{8,10},{9,11},{10,... | collective-permute-start | bytes 18440 | tf_op jit(solution)/shard_map/ppermute | solution.py:776
  41.7 3.8 collective-permute-start.11
  45.5 5.0 %collective-permute-start.13 = (bf16[2,8,768]{2,1,0:T(8,128)(2,1)S(1)}, bf16[2,8,768]{2,1,0:T(8,128)(2,1)S(1)}, u32[]{:S(2)}, u32[]{:S(2)}) collective-permute-start(bf16[2,8,768]{2,1,0:T(8,128)(2,1)S(1)} %maximum_select_fusion.11), channel_id=1, source_target_pairs={{0,8},{1,9},{2,10},{3,11},{4,12},{5,13},{6,14},{7,15},{8,0},{9,1},... | collective-permute-start | bytes 73736 | tf_op jit(solution)/shard_map/ppermute | solution.py:776
  46.5 25.9 %collective-permute-start.19 = (bf16[2,96,1152]{2,1,0:T(8,128)(2,1)}, bf16[2,96,1152]{2,1,0:T(8,128)(2,1)}, u32[]{:S(2)}, u32[]{:S(2)}) collective-permute-start(bf16[2,96,1152]{2,1,0:T(8,128)(2,1)} %collective-permute-done.12), channel_id=1, source_target_pairs={{0,2},{1,3},{2,0},{3,1},{4,6},{5,7},{6,4},{7,5},{8,10},{9,11},{10,... | collective-permute-start | bytes 1327112 | tf_op jit(solution)/shard_map/ppermute | solution.py:776
  48.0 12.8 %collective-permute-start.14 = (bf16[2,96,1152]{2,1,0:T(8,128)(2,1)}, bf16[2,96,1152]{2,1,0:T(8,128)(2,1)}, u32[]{:S(2)}, u32[]{:S(2)}) collective-permute-start(bf16[2,96,1152]{2,1,0:T(8,128)(2,1)} %collective-permute-done.12), channel_id=1, source_target_pairs={{0,4},{1,5},{2,6},{3,7},{4,8},{5,9},{6,10},{7,11},{8,12},{9,13},{1... | collective-permute-start | bytes 1327112 | tf_op jit(solution)/shard_map/ppermute | solution.py:789
  70.4 25.9 %collective-permute-start.16 = (bf16[2,2,96,768]{3,2,1,0:T(8,128)(2,1)}, bf16[2,2,96,768]{3,2,1,0:T(8,128)(2,1)}, u32[]{:S(2)}, u32[]{:S(2)}) collective-permute-start(bf16[2,2,96,768]{3,2,1,0:T(8,128)(2,1)} %pad_maximum_fusion.1.refs_0_), channel_id=1, source_target_pairs={{0,4},{1,5},{2,6},{3,7},{4,8},{5,9},{6,10},{7,11},{8,12},{9,13},{1... | collective-permute-start | bytes 1769480 | tf_op jit(solution)/shard_map/ppermute | solution.py:789
  70.4 10.1 %collective-permute-start.20 = (bf16[2,96,1152]{2,1,0:T(8,128)(2,1)}, bf16[2,96,1152]{2,1,0:T(8,128)(2,1)S(1)}, u32[]{:S(2)}, u32[]{:S(2)}) collective-permute-start(bf16[2,96,1152]{2,1,0:T(8,128)(2,1)} %collective-permute-done.14), channel_id=1, source_target_pairs={{0,2},{1,3},{2,0},{3,1},{4,6},{5,7},{6,4},{7,5},{8,10},{9,11},{10,... | collective-permute-start | bytes 1327112 | tf_op jit(solution)/shard_map/ppermute | solution.py:776
  74.5 39.3 %collective-permute-start.5 = (bf16[512,1536]{1,0:T(8,128)(2,1)}, bf16[512,1536]{1,0:T(8,128)(2,1)}, u32[]{:S(2)}, u32[]{:S(2)}) collective-permute-start(bf16[512,1536]{1,0:T(8,128)(2,1)} %collective-permute-done.4.far), channel_id=1, source_target_pairs={{0,1},{1,0},{2,3},{3,2},{4,5},{5,4},{6,7},{7,6},{8,9},{9,8},{10,11... | collective-permute-start | bytes 4718600 | tf_op jit(solution)/shard_map/ppermute | solution.py:776
  74.6 57.0 %collective-permute-start.27 = (bf16[512,1536]{1,0:T(8,128)(2,1)}, bf16[512,1536]{1,0:T(8,128)(2,1)}, u32[]{:S(2)}, u32[]{:S(2)}) collective-permute-start(bf16[512,1536]{1,0:T(8,128)(2,1)} %cot.1), channel_id=1, source_target_pairs={{0,16},{16,0},{1,17},{17,1},{2,18},{18,2},{3,19},{19,3},{4,20},{20... | collective-permute-start | bytes 4718600 | tf_op jit(solution)/shard_map/ppermute | solution.py:763
  80.6 16.8 %collective-permute-start.22 = (bf16[2,2,96,768]{3,2,1,0:T(8,128)(2,1)}, bf16[2,2,96,768]{3,2,1,0:T(8,128)(2,1)}, u32[]{:S(2)}, u32[]{:S(2)}) collective-permute-start(bf16[2,2,96,768]{3,2,1,0:T(8,128)(2,1)} %pad_maximum_fusion.1.refs_0_), channel_id=1, source_target_pairs={{0,2},{1,3},{2,0},{3,1},{4,6},{5,7},{6,4},{7,5},{8,10},{9,11},{10,... | collective-permute-start | bytes 1769480 | tf_op jit(solution)/shard_map/ppermute | solution.py:776
  96.3 15.6 %collective-permute-start.24 = (bf16[2,2,96,768]{3,2,1,0:T(8,128)(2,1)}, bf16[2,2,96,768]{3,2,1,0:T(8,128)(2,1)}, u32[]{:S(2)}, u32[]{:S(2)}) collective-permute-start(bf16[2,2,96,768]{3,2,1,0:T(8,128)(2,1)} %collective-permute-done.16.refs_2_), channel_id=1, source_target_pairs={{0,2},{1,3},{2,0},{3,1},{4,6},{5,7},{6,4},{7,5},{8,10},{9,11},{10,... | collective-permute-start | bytes 1769480 | tf_op jit(solution)/shard_map/ppermute | solution.py:776
  97.3 14.7 %collective-permute-start.21 = (bf16[2,2,96,768]{3,2,1,0:T(8,128)(2,1)}, bf16[2,2,96,768]{3,2,1,0:T(8,128)(2,1)}, u32[]{:S(2)}, u32[]{:S(2)}) collective-permute-start(bf16[2,2,96,768]{3,2,1,0:T(8,128)(2,1)} %collective-permute-done.16.refs_2_), channel_id=1, source_target_pairs={{0,4},{1,5},{2,6},{3,7},{4,8},{5,9},{6,10},{7,11},{8,12},{9,13},{1... | collective-permute-start | bytes 1769480 | tf_op jit(solution)/shard_map/ppermute | solution.py:789
  111.9 40.5 %collective-permute-start.28 = (bf16[512,1536]{1,0:T(8,128)(2,1)S(1)}, bf16[512,1536]{1,0:T(8,128)(2,1)S(1)}, u32[]{:S(2)}, u32[]{:S(2)}) collective-permute-start(bf16[512,1536]{1,0:T(8,128)(2,1)S(1)} %copy-done.2), channel_id=1, source_target_pairs={{0,1},{1,0},{2,3},{3,2},{4,5},{5,4},{6,7},{7,6},{8,9},{9,8},{10,11... | collective-permute-start | bytes 4718600 | tf_op jit(solution)/shard_map/ppermute | solution.py:776
  112.0 16.1 %collective-permute-start.25 = (bf16[2,2,96,768]{3,2,1,0:T(8,128)(2,1)}, bf16[2,2,96,768]{3,2,1,0:T(8,128)(2,1)}, u32[]{:S(2)}, u32[]{:S(2)}) collective-permute-start(bf16[2,2,96,768]{3,2,1,0:T(8,128)(2,1)} %collective-permute-done.21.refs_4_), channel_id=1, source_target_pairs={{0,2},{1,3},{2,0},{3,1},{4,6},{5,7},{6,4},{7,5},{8,10},{9,11},{10,... | collective-permute-start | bytes 1769480 | tf_op jit(solution)/shard_map/ppermute | solution.py:776
  113.5 17.5 %collective-permute-start.23 = (bf16[2,2,96,768]{3,2,1,0:T(8,128)(2,1)}, bf16[2,2,96,768]{3,2,1,0:T(8,128)(2,1)}, u32[]{:S(2)}, u32[]{:S(2)}) collective-permute-start(bf16[2,2,96,768]{3,2,1,0:T(8,128)(2,1)} %collective-permute-done.21.refs_4_), channel_id=1, source_target_pairs={{0,4},{1,5},{2,6},{3,7},{4,8},{5,9},{6,10},{7,11},{8,12},{9,13},{1... | collective-permute-start | bytes 1769480 | tf_op jit(solution)/shard_map/ppermute | solution.py:789
  131.0 14.9 %collective-permute-start.26 = (bf16[2,2,96,768]{3,2,1,0:T(8,128)(2,1)}, bf16[2,2,96,768]{3,2,1,0:T(8,128)(2,1)}, u32[]{:S(2)}, u32[]{:S(2)}) collective-permute-start(bf16[2,2,96,768]{3,2,1,0:T(8,128)(2,1)} %collective-permute-done.23.refs_6_), channel_id=1, source_target_pairs={{0,2},{1,3},{2,0},{3,1},{4,6},{5,7},{6,4},{7,5},{8,10},{9,11},{10,... | collective-permute-start | bytes 1769480 | tf_op jit(solution)/shard_map/ppermute | solution.py:776
  131.6 20.8 %collective-permute-start.29 = (bf16[512,1536]{1,0:T(8,128)(2,1)}, bf16[512,1536]{1,0:T(8,128)(2,1)}, u32[]{:S(2)}, u32[]{:S(2)}) collective-permute-start(bf16[512,1536]{1,0:T(8,128)(2,1)} %collective-permute-done.27.cot_fa.rest_1_), channel_id=1, source_target_pairs={{0,1},{1,0},{2,3},{3,2},{4,5},{5,4},{6,7},{7,6},{8,9},{9,8},{10,11... | collective-permute-start | bytes 4718600 | tf_op jit(solution)/shard_map/ppermute | solution.py:776
  151.8 3.2 collective-permute-start.30
  173.7 4.5 %collective-permute-start.31 = (f32[8,2048]{1,0:T(8,128)}, f32[8,2048]{1,0:T(8,128)S(1)}, u32[]{:S(2)}, u32[]{:S(2)}) collective-permute-start(f32[8,2048]{1,0:T(8,128)} %get-tuple-element.207), channel_id=1, source_target_pairs={{0,16},{16,0},{1,17},{17,1},{2,18},{18,2},{3,19},{19,3},{4,20},{20... | collective-permute-start | bytes 196616 | tf_op jit(solution)/shard_map/ppermute | solution.py:763
  202.1 9.9 %collective-permute-start.33 = (bf16[1024,1536]{1,0:T(8,128)(2,1)}, bf16[1024,1536]{1,0:T(8,128)(2,1)}, u32[]{:S(2)}, u32[]{:S(2)}) collective-permute-start(bf16[1024,1536]{1,0:T(8,128)(2,1)} %get-tuple-element.213), channel_id=1, source_target_pairs={{0,1},{1,0},{2,3},{3,2},{4,5},{5,4},{6,7},{7,6},{8,9},{9,8},{10,11... | collective-permute-start | bytes 9437192 | tf_op jit(solution)/shard_map/ppermute | solution.py:776
  214.4 3.3 collective-permute-start.34
  233.2 18.1 %collective-permute-start.35 = (bf16[2,2,96,768]{3,2,1,0:T(8,128)(2,1)}, bf16[2,2,96,768]{3,2,1,0:T(8,128)(2,1)}, u32[]{:S(2)}, u32[]{:S(2)}) collective-permute-start(bf16[2,2,96,768]{3,2,1,0:T(8,128)(2,1)} %get-tuple-element.315), channel_id=1, source_target_pairs={{0,2},{1,3},{2,0},{3,1},{4,6},{5,7},{6,4},{7,5},{8,10},{9,11},{10,... | collective-permute-start | bytes 1769480 | tf_op jit(solution)/shard_map/ppermute | solution.py:776
  233.8 43.5 %collective-permute-start.39 = (bf16[512,1536]{1,0:T(8,128)(2,1)S(1)}, bf16[512,1536]{1,0:T(8,128)(2,1)S(1)}, u32[]{:S(2)}, u32[]{:S(2)}) collective-permute-start(bf16[512,1536]{1,0:T(8,128)(2,1)S(1)} %copy-done.11), channel_id=1, source_target_pairs={{0,16},{16,0},{1,17},{17,1},{2,18},{18,2},{3,19},{19,3},{4,20},{20... | collective-permute-start | bytes 4718600 | tf_op jit(solution)/shard_map/ppermute | solution.py:763
  253.5 17.9 %collective-permute-start.36 = (bf16[2,2,96,768]{3,2,1,0:T(8,128)(2,1)}, bf16[2,2,96,768]{3,2,1,0:T(8,128)(2,1)}, u32[]{:S(2)}, u32[]{:S(2)}) collective-permute-start(bf16[2,2,96,768]{3,2,1,0:T(8,128)(2,1)} %get-tuple-element.226), channel_id=1, source_target_pairs={{0,2},{1,3},{2,0},{3,1},{4,6},{5,7},{6,4},{7,5},{8,10},{9,11},{10,... | collective-permute-start | bytes 1769480 | tf_op jit(solution)/shard_map/ppermute | solution.py:776
  254.9 16.8 %collective-permute-start.37 = (bf16[2,2,96,768]{3,2,1,0:T(8,128)(2,1)}, bf16[2,2,96,768]{3,2,1,0:T(8,128)(2,1)}, u32[]{:S(2)}, u32[]{:S(2)}) collective-permute-start(bf16[2,2,96,768]{3,2,1,0:T(8,128)(2,1)} %fusion.1), channel_id=1, source_target_pairs={{0,4},{1,5},{2,6},{3,7},{4,8},{5,9},{6,10},{7,11},{8,12},{9,13},{1... | collective-permute-start | bytes 1769480 | tf_op jit(solution)/shard_map/ppermute | solution.py:789
  274.1 19.4 %collective-permute-start.38 = (bf16[2,2,96,768]{3,2,1,0:T(8,128)(2,1)}, bf16[2,2,96,768]{3,2,1,0:T(8,128)(2,1)}, u32[]{:S(2)}, u32[]{:S(2)}) collective-permute-start(bf16[2,2,96,768]{3,2,1,0:T(8,128)(2,1)} %get-tuple-element.234), channel_id=1, source_target_pairs={{0,2},{1,3},{2,0},{3,1},{4,6},{5,7},{6,4},{7,5},{8,10},{9,11},{10,... | collective-permute-start | bytes 1769480 | tf_op jit(solution)/shard_map/ppermute | solution.py:776
  274.7 18.8 %collective-permute-start.40 = (bf16[2,2,96,768]{3,2,1,0:T(8,128)(2,1)}, bf16[2,2,96,768]{3,2,1,0:T(8,128)(2,1)}, u32[]{:S(2)}, u32[]{:S(2)}) collective-permute-start(bf16[2,2,96,768]{3,2,1,0:T(8,128)(2,1)} %fusion.3), channel_id=1, source_target_pairs={{0,4},{1,5},{2,6},{3,7},{4,8},{5,9},{6,10},{7,11},{8,12},{9,13},{1... | collective-permute-start | bytes 1769480 | tf_op jit(solution)/shard_map/ppermute | solution.py:789
  295.2 20.9 %collective-permute-start.42 = (bf16[2,2,96,768]{3,2,1,0:T(8,128)(2,1)S(1)}, bf16[2,2,96,768]{3,2,1,0:T(8,128)(2,1)S(1)}, u32[]{:S(2)}, u32[]{:S(2)}) collective-permute-start(bf16[2,2,96,768]{3,2,1,0:T(8,128)(2,1)S(1)} %fusion.5), channel_id=1, source_target_pairs={{0,4},{1,5},{2,6},{3,7},{4,8},{5,9},{6,10},{7,11},{8,12},{9,13},{1... | collective-permute-start | bytes 1769480 | tf_op jit(solution)/shard_map/ppermute | solution.py:789
  295.9 20.3 %collective-permute-start.41 = (bf16[2,2,96,768]{3,2,1,0:T(8,128)(2,1)S(1)}, bf16[2,2,96,768]{3,2,1,0:T(8,128)(2,1)S(1)}, u32[]{:S(2)}, u32[]{:S(2)}) collective-permute-start(bf16[2,2,96,768]{3,2,1,0:T(8,128)(2,1)S(1)} %copy-done.15), channel_id=1, source_target_pairs={{0,2},{1,3},{2,0},{3,1},{4,6},{5,7},{6,4},{7,5},{8,10},{9,11},{10,... | collective-permute-start | bytes 1769480 | tf_op jit(solution)/shard_map/ppermute | solution.py:776
  318.3 19.3 %collective-permute-start.44 = (bf16[2,48,768]{2,1,0:T(8,128)(2,1)S(1)}, bf16[2,48,768]{2,1,0:T(8,128)(2,1)S(1)}, u32[]{:S(2)}, u32[]{:S(2)}) collective-permute-start(bf16[2,48,768]{2,1,0:T(8,128)(2,1)S(1)} %get-tuple-element.340), channel_id=1, source_target_pairs={{0,1},{1,0},{2,3},{3,2},{4,5},{5,4},{6,7},{7,6},{8,9},{9,8},{10,11... | collective-permute-start | bytes 442376 | tf_op jit(solution)/shard_map/ppermute | solution.py:776
  346.0 22.2 %collective-permute-start.46 = (bf16[512,1536]{1,0:T(8,128)(2,1)}, bf16[512,1536]{1,0:T(8,128)(2,1)}, u32[]{:S(2)}, u32[]{:S(2)}) collective-permute-start(bf16[512,1536]{1,0:T(8,128)(2,1)} %input_grad.4), channel_id=1, source_target_pairs={{0,1},{1,0},{2,3},{3,2},{4,5},{5,4},{6,7},{7,6},{8,9},{9,8},{10,11... | collective-permute-start | bytes 4718600 | tf_op jit(solution)/shard_map/ppermute | solution.py:776
  346.3 4.6 %collective-permute-start.43 = (f32[168,128]{1,0:T(8,128)S(1)}, f32[168,128]{1,0:T(8,128)S(1)}, u32[]{:S(2)}, u32[]{:S(2)}) collective-permute-start(f32[168,128]{1,0:T(8,128)S(1)} %pad_maximum_fusion.6), channel_id=1, source_target_pairs={{0,16},{16,0},{1,17},{17,1},{2,18},{18,2},{3,19},{19,3},{4,20},{20... | collective-permute-start | bytes 258056 | tf_op jit(solution)/shard_map/ppermute | solution.py:763
  346.6 15.6 %collective-permute-start.48 = (bf16[2,96,1152]{2,1,0:T(8,128)(2,1)S(1)}, bf16[2,96,1152]{2,1,0:T(8,128)(2,1)}, u32[]{:S(2)}, u32[]{:S(2)}) collective-permute-start(bf16[2,96,1152]{2,1,0:T(8,128)(2,1)S(1)} %get-tuple-element.319), channel_id=1, source_target_pairs={{0,2},{1,3},{2,0},{3,1},{4,6},{5,7},{6,4},{7,5},{8,10},{9,11},{10,... | collective-permute-start | bytes 1327112 | tf_op jit(solution)/shard_map/ppermute | solution.py:776
  351.0 9.6 %collective-permute-start.51 = (f32[168,128]{1,0:T(8,128)S(1)}, f32[168,128]{1,0:T(8,128)}, u32[]{:S(2)}, u32[]{:S(2)}) collective-permute-start(f32[168,128]{1,0:T(8,128)S(1)} %fusion.40), channel_id=1, source_target_pairs={{0,1},{1,0},{2,3},{3,2},{4,5},{5,4},{6,7},{7,6},{8,9},{9,8},{10,11... | collective-permute-start | bytes 258056 | tf_op jit(solution)/shard_map/ppermute | solution.py:776
  351.8 15.8 %collective-permute-start.52 = (bf16[48,1536]{1,0:T(8,128)(2,1)}, bf16[48,1536]{1,0:T(8,128)(2,1)}, u32[]{:S(2)}, u32[]{:S(2)}) collective-permute-start(bf16[48,1536]{1,0:T(8,128)(2,1)} %get-tuple-element.337), channel_id=1, source_target_pairs={{0,16},{16,0},{1,17},{17,1},{2,18},{18,2},{3,19},{19,3},{4,20},{20... | collective-permute-start | bytes 442376 | tf_op jit(solution)/shard_map/ppermute | solution.py:763
  364.1 18.1 %collective-permute-start.53 = (bf16[2,96,1152]{2,1,0:T(8,128)(2,1)}, bf16[2,96,1152]{2,1,0:T(8,128)(2,1)}, u32[]{:S(2)}, u32[]{:S(2)}) collective-permute-start(bf16[2,96,1152]{2,1,0:T(8,128)(2,1)} %fusion.10), channel_id=1, source_target_pairs={{0,4},{1,5},{2,6},{3,7},{4,8},{5,9},{6,10},{7,11},{8,12},{9,13},{1... | collective-permute-start | bytes 1327112 | tf_op jit(solution)/shard_map/ppermute | solution.py:789
  367.6 14.6 %collective-permute-start.49 = (bf16[2,96,1152]{2,1,0:T(8,128)(2,1)}, bf16[2,96,1152]{2,1,0:T(8,128)(2,1)}, u32[]{:S(2)}, u32[]{:S(2)}) collective-permute-start(bf16[2,96,1152]{2,1,0:T(8,128)(2,1)} %get-tuple-element.268), channel_id=1, source_target_pairs={{0,2},{1,3},{2,0},{3,1},{4,6},{5,7},{6,4},{7,5},{8,10},{9,11},{10,... | collective-permute-start | bytes 1327112 | tf_op jit(solution)/shard_map/ppermute | solution.py:776
  371.2 11.0 %collective-permute-start.50 = (bf16[128,1536]{1,0:T(8,128)(2,1)}, bf16[128,1536]{1,0:T(8,128)(2,1)}, u32[]{:S(2)}, u32[]{:S(2)}) collective-permute-start(bf16[128,1536]{1,0:T(8,128)(2,1)} %get-tuple-element.322), channel_id=1, source_target_pairs={{0,16},{16,0},{1,17},{17,1},{2,18},{18,2},{3,19},{19,3},{4,20},{20... | collective-permute-start | bytes 1179656 | tf_op jit(solution)/shard_map/ppermute | solution.py:763
  384.3 14.1 %collective-permute-start.54 = (bf16[2,96,1152]{2,1,0:T(8,128)(2,1)}, bf16[2,96,1152]{2,1,0:T(8,128)(2,1)}, u32[]{:S(2)}, u32[]{:S(2)}) collective-permute-start(bf16[2,96,1152]{2,1,0:T(8,128)(2,1)} %get-tuple-element.275), channel_id=1, source_target_pairs={{0,2},{1,3},{2,0},{3,1},{4,6},{5,7},{6,4},{7,5},{8,10},{9,11},{10,... | collective-permute-start | bytes 1327112 | tf_op jit(solution)/shard_map/ppermute | solution.py:776
  385.6 12.8 %collective-permute-start.56 = (bf16[2,96,1152]{2,1,0:T(8,128)(2,1)}, bf16[2,96,1152]{2,1,0:T(8,128)(2,1)}, u32[]{:S(2)}, u32[]{:S(2)}) collective-permute-start(bf16[2,96,1152]{2,1,0:T(8,128)(2,1)} %fusion.12), channel_id=1, source_target_pairs={{0,4},{1,5},{2,6},{3,7},{4,8},{5,9},{6,10},{7,11},{8,12},{9,13},{1... | collective-permute-start | bytes 1327112 | tf_op jit(solution)/shard_map/ppermute | solution.py:789
  386.0 12.4 %collective-permute-start.55 = (bf16[128,1536]{1,0:T(8,128)(2,1)}, bf16[128,1536]{1,0:T(8,128)(2,1)}, u32[]{:S(2)}, u32[]{:S(2)}) collective-permute-start(bf16[128,1536]{1,0:T(8,128)(2,1)} %get-tuple-element.321), channel_id=1, source_target_pairs={{0,16},{16,0},{1,17},{17,1},{2,18},{18,2},{3,19},{19,3},{4,20},{20... | collective-permute-start | bytes 1179656 | tf_op jit(solution)/shard_map/ppermute | solution.py:763
  387.2 19.7 %collective-permute-start.47 = (bf16[128,1536]{1,0:T(8,128)(2,1)}, bf16[128,1536]{1,0:T(8,128)(2,1)}, u32[]{:S(2)}, u32[]{:S(2)}) collective-permute-start(bf16[128,1536]{1,0:T(8,128)(2,1)} %get-tuple-element.323), channel_id=1, source_target_pairs={{0,16},{16,0},{1,17},{17,1},{2,18},{18,2},{3,19},{19,3},{4,20},{20... | collective-permute-start | bytes 1179656 | tf_op jit(solution)/shard_map/ppermute | solution.py:763
  399.8 11.6 %collective-permute-start.58 = (bf16[2,96,1152]{2,1,0:T(8,128)(2,1)S(1)}, bf16[2,96,1152]{2,1,0:T(8,128)(2,1)S(1)}, u32[]{:S(2)}, u32[]{:S(2)}) collective-permute-start(bf16[2,96,1152]{2,1,0:T(8,128)(2,1)S(1)} %fusion.14), channel_id=1, source_target_pairs={{0,4},{1,5},{2,6},{3,7},{4,8},{5,9},{6,10},{7,11},{8,12},{9,13},{1... | collective-permute-start | bytes 1327112 | tf_op jit(solution)/shard_map/ppermute | solution.py:789
  400.7 9.1 %collective-permute-start.57 = (bf16[2,96,1152]{2,1,0:T(8,128)(2,1)}, bf16[2,96,1152]{2,1,0:T(8,128)(2,1)S(1)}, u32[]{:S(2)}, u32[]{:S(2)}) collective-permute-start(bf16[2,96,1152]{2,1,0:T(8,128)(2,1)} %get-tuple-element.283), channel_id=1, source_target_pairs={{0,2},{1,3},{2,0},{3,1},{4,6},{5,7},{6,4},{7,5},{8,10},{9,11},{10,... | collective-permute-start | bytes 1327112 | tf_op jit(solution)/shard_map/ppermute | solution.py:776
  411.6 3.0 collective-permute-start.59
  411.7 6.9 %collective-permute-start.63 = (f32[168,128]{1,0:T(8,128)}, f32[168,128]{1,0:T(8,128)S(1)}, u32[]{:S(2)}, u32[]{:S(2)}) collective-permute-start(f32[168,128]{1,0:T(8,128)} %add.600), channel_id=1, source_target_pairs={{0,2},{1,3},{2,0},{3,1},{4,6},{5,7},{6,4},{7,5},{8,10},{9,11},{10,... | collective-permute-start | bytes 258056 | tf_op jit(solution)/shard_map/ppermute | solution.py:776
  412.4 19.5 %collective-permute-start.61 = (bf16[512,1536]{1,0:T(8,128)(2,1)}, bf16[512,1536]{1,0:T(8,128)(2,1)}, u32[]{:S(2)}, u32[]{:S(2)}) collective-permute-start(bf16[512,1536]{1,0:T(8,128)(2,1)} %input_grad.6), channel_id=1, source_target_pairs={{0,1},{1,0},{2,3},{3,2},{4,5},{5,4},{6,7},{7,6},{8,9},{9,8},{10,11... | collective-permute-start | bytes 4718600 | tf_op jit(solution)/shard_map/ppermute | solution.py:776
  412.6 19.3 %collective-permute-start.62 = (bf16[128,1536]{1,0:T(8,128)(2,1)}, bf16[128,1536]{1,0:T(8,128)(2,1)S(1)}, u32[]{:S(2)}, u32[]{:S(2)}) collective-permute-start(bf16[128,1536]{1,0:T(8,128)(2,1)} %get-tuple-element.320), channel_id=1, source_target_pairs={{0,16},{16,0},{1,17},{17,1},{2,18},{18,2},{3,19},{19,3},{4,20},{20... | collective-permute-start | bytes 1179656 | tf_op jit(solution)/shard_map/ppermute | solution.py:763
  414.9 13.2 %collective-permute-start.60 = (bf16[48,1920]{1,0:T(8,128)(2,1)S(1)}, bf16[48,1920]{1,0:T(8,128)(2,1)S(1)}, u32[]{:S(2)}, u32[]{:S(2)}) collective-permute-start(bf16[48,1920]{1,0:T(8,128)(2,1)S(1)} %get-tuple-element.333), channel_id=1, source_target_pairs={{0,16},{16,0},{1,17},{17,1},{2,18},{18,2},{3,19},{19,3},{4,20},{20... | collective-permute-start | bytes 552968 | tf_op jit(solution)/shard_map/ppermute | solution.py:763
  418.7 9.5 %collective-permute-start.64 = (f32[168,128]{1,0:T(8,128)S(1)}, f32[168,128]{1,0:T(8,128)S(1)}, u32[]{:S(2)}, u32[]{:S(2)}) collective-permute-start(f32[168,128]{1,0:T(8,128)S(1)} %add.624), channel_id=1, source_target_pairs={{0,4},{1,5},{2,6},{3,7},{4,0},{5,1},{6,2},{7,3},{8,12},{9,13},{10,... | collective-permute-start | bytes 258056 | tf_op jit(solution)/shard_map/ppermute | solution.py:776
  428.2 11.0 %collective-permute-start.65 = (f32[168,128]{1,0:T(8,128)S(1)}, f32[168,128]{1,0:T(8,128)S(1)}, u32[]{:S(2)}, u32[]{:S(2)}) collective-permute-start(f32[168,128]{1,0:T(8,128)S(1)} %add.625), channel_id=1, source_target_pairs={{0,8},{1,9},{2,10},{3,11},{4,12},{5,13},{6,14},{7,15},{8,0},{9,1},... | collective-permute-start | bytes 258056 | tf_op jit(solution)/shard_map/ppermute | solution.py:776
  (42 other events, 352.3 us)
where the time goes:
time: 451 us; the launch traced here: 442 us
  Pallas kernels  241 us (53%)
  waiting for transfers between devices  71.1 us (16%)
  starting transfers between devices  52.8 us (12%)
  other arithmetic  43.7 us (10%)
  local copies, waits for them, and re-layouts  31.1 us (7%)
    pallas_call x4, Pallas kernels, run_backward(): pl.pallas_call(backward_kernel, grid_spec=pltpu.PrefetchScalarGridSpec(nu...  65.2 us
    pallas_call x4, Pallas kernels, run_forward(): pl.pallas_call(functools.partial(forward_kernel, part % 2), grid_spec=plt...  53 us
    pallas_call x4, Pallas kernels, run_input_grad(): pl.pallas_call(input_grad_kernel, grid_spec=pltpu.PrefetchScalarGridSpec(...  33.3 us
    pallas_call x2, Pallas kernels, run_pieces(): pl.pallas_call(functools.partial(pieces_kernel, chip_rows, len(columns)),...  27.6 us
    ppermute x40, waiting for transfers between devices, flip(): return lax.ppermute(block, 'dp', [(d, d ^ bit) for d in range(count)])  26.8 us
    ppermute x40, starting transfers between devices, flip(): return lax.ppermute(block, 'dp', [(d, d ^ bit) for d in range(count)])  24.5 us
    ppermute x14, waiting for transfers between devices, other_side(): return lax.ppermute(block, 'seq', [(0, 1), (1, 0)])  22.5 us
    ppermute x12, waiting for transfers between devices, along(): lax.ppermute(block, 'dp', [(d, (d + 4) % count) for d in range(count)])  21.8 us
  transfers between devices with their start and end apart: 66, of which 21 were waited for; matrix products, arithmetic and copies ran while one was open for 13% of the time, Pallas kernels for 41%

commit v1 on v0

--- a/solution.py
+++ b/solution.py
@@ -93,12 +93,24 @@
     return mm(both, high, NT) + mm(first[0], second[1], NT)
 
 
-def running(mask, v):
+def packed(v):
     high = v.astype(bf16).astype(f32)
     left = v - high
     middle = left.astype(bf16).astype(f32)
-    packed = high + pltpu.roll(middle, 16, 1) + pltpu.roll(left - middle, 32, 1)
-    product = mm(mask.astype(f32).astype(bf16), packed.astype(bf16))
+    parts = high + pltpu.roll(middle, 16, 1) + pltpu.roll(left - middle, 32, 1)
+    return parts.astype(bf16)
+
+
+def spread_product(v):
+    lane = lax.broadcasted_iota(jnp.int32, v.shape, 1)
+    row = lax.broadcasted_iota(jnp.int32, (128, QW), 0)
+    column = lax.broadcasted_iota(jnp.int32, (128, QW), 1)
+    ones = jnp.where((row % 16 == column // HEAD_DIM) & (row < 48), 1.0, 0.0)
+    return mm(packed(jnp.where(lane < QH, v, 0.0)), ones.astype(bf16))
+
+
+def running(mask, v):
+    product = mm(mask.astype(f32).astype(bf16), packed(v))
     return product + pltpu.roll(product, 112, 1) + pltpu.roll(product, 96, 1)
 
 
@@ -158,11 +170,12 @@
     across = summed.T
     affinity = jnp.where(causal, affinity_of(readers, writers), 0.0)
 
-    dosed = payload * spread_heads(steps, 0, QH)
+    dosed = payload * spread_product(steps)
     dosed_low = dosed.astype(bf16)
     state = mem[...]
     mem_out[0] = state
-    grown = jnp.exp2(spread_heads(summed, 0, QH))
+    summed_wide = spread_heads(summed, 0, QH)
+    grown = jnp.exp2(summed_wide)
     state_low, state_rest = parts_of(state)
     carried = mm(jnp.concatenate(readers, axis=1), jnp.concatenate([state_low] * 2, axis=0))
     carried = (carried + mm(readers[0], state_rest)) * grown
@@ -179,9 +192,10 @@
     scanned_out[...] = jnp.concatenate(within, axis=1) + carried + payload * skip[...]
 
     last = summed[LEN - 1 : LEN, :]
-    remain = jnp.exp2(spread_heads(last - summed, 0, QH))
+    last_wide = spread_heads(last, 0, QH)
+    remain = jnp.exp2(last_wide - summed_wide)
     added = mm(writer, (dosed * remain).astype(bf16), TN)
-    mem[...] = state * jnp.exp2(spread_heads(last, 0, QH)) + added
+    mem[...] = state * jnp.exp2(last_wide) + added
     tail_out[...] = ext[0:8, :]
     state_out[...] = mem[...]
 
@@ -294,14 +308,16 @@
     grad = grad_in[...]
     grad_low = grad.astype(bf16)
     grad_rest = grad - grad_low.astype(f32)
-    dose = spread_heads(steps, 0, QH)
+    dose = spread_product(steps)
     dosed = payload * dose
     dosed_low = dosed.astype(bf16)
     state = mem_in[0]
     state_grad = grad_mem[...]
     state_grad_low = state_grad.astype(bf16)
     last = summed[LEN - 1 : LEN, :]
-    remain = jnp.exp2(spread_heads(last - summed, 0, QH))
+    last_wide = spread_heads(last, 0, QH)
+    summed_wide = spread_heads(summed, 0, QH)
+    remain = jnp.exp2(last_wide - summed_wide)
     from_state = mm(writer, state_grad_low) * remain
 
     mixed = jnp.zeros((LEN, LEN), f32)
@@ -327,7 +343,7 @@
     balance = grad_low.astype(f32) * core - dosed_wide * unit
     high_part = balance.astype(bf16)
     low_part = (balance - high_part.astype(f32)).astype(bf16)
-    decay_last = jnp.exp2(spread_heads(last, 0, QH))
+    decay_last = jnp.exp2(last_wide)
     at_end = jnp.sum(dosed_wide * from_state, axis=0, keepdims=True) + decay_last * jnp.sum(
         state_grad * state, axis=0, keepdims=True
     )
@@ -357,7 +373,7 @@
     head_grad[1:2, :] += jnp.sum(raw_grad, axis=0, keepdims=True)
     skip_grad[0:1, :] += jnp.sum(grad * payload, axis=0, keepdims=True)
 
-    grown_wide = jnp.exp2(spread_heads(summed, 0, QH)) * grad
+    grown_wide = jnp.exp2(summed_wide) * grad
     grown_grad = grown_wide.astype(bf16)
     grown_rest = (grown_wide - grown_grad.astype(f32)).astype(bf16)
     kept = (remain * dosed).astype(bf16)

time: 451 us -> 446 us (0.989)
  Pallas kernels: 241 us -> 235 us
  transfers between devices with their start and end apart: 66 -> 66, of which waited for: 21 -> 20; matrix products, arithmetic and copies ran while one was open for 13% -> 13% of each run, Pallas kernels for 41% -> 40%
where the time goes in v1:
time: 446 us; the launch traced here: 438 us
  Pallas kernels  235 us (53%)
  waiting for transfers between devices  73.6 us (17%)
  starting transfers between devices  52 us (12%)
  other arithmetic  43.7 us (10%)
  local copies, waits for them, and re-layouts  31.1 us (7%)
    pallas_call x4, Pallas kernels, run_backward(): pl.pallas_call(backward_kernel, grid_spec=pltpu.PrefetchScalarGridSpec(nu...  62.8 us
    pallas_call x4, Pallas kernels, run_forward(): pl.pallas_call(functools.partial(forward_kernel, part % 2), grid_spec=plt...  49.5 us
    pallas_call x4, Pallas kernels, run_input_grad(): pl.pallas_call(input_grad_kernel, grid_spec=pltpu.PrefetchScalarGridSpec(...  33.3 us
    ppermute x40, waiting for transfers between devices, flip(): return lax.ppermute(block, 'dp', [(d, d ^ bit) for d in range(count)])  28.5 us
    pallas_call x2, Pallas kernels, run_pieces(): pl.pallas_call(functools.partial(pieces_kernel, chip_rows, len(columns)),...  27.6 us
    ppermute x40, starting transfers between devices, flip(): return lax.ppermute(block, 'dp', [(d, d ^ bit) for d in range(count)])  24.3 us
    ppermute x12, waiting for transfers between devices, along(): lax.ppermute(block, 'dp', [(d, (d + 4) % count) for d in range(count)])  22.6 us
    ppermute x14, waiting for transfers between devices, other_side(): return lax.ppermute(block, 'seq', [(0, 1), (1, 0)])  22.5 us
  transfers between devices with their start and end apart: 66, of which 20 were waited for; matrix products, arithmetic and copies ran while one was open for 13% of the time, Pallas kernels for 40%

profile of v1, /device:TPU:0, one launch (start us, length us, event | category | flops | bytes accessed | tf_op | source)
XLA Modules:
  0.0 437.7 jit_solution(1649057247348070)
XLA Ops:
  2.4 3.0 collective-permute-start.1
  10.4 1.8 collective-permute-start.2
  12.4 3.3 collective-permute-done.2
  15.8 1.9 collective-permute-start.8
  17.8 1.6 collective-permute-start.17
  19.7 1.6 collective-permute-start.4
  21.3 6.8 %collective-permute-done.8 = bf16[2,96,1152]{2,1,0:T(8,128)(2,1)S(1)} collective-permute-done((bf16[2,96,1152]{2,1,0:T(8,128)(2,1)S(1)}, bf16[2,96,1152]{2,1,0:T(8,128)(2,1)S(1)}, u32[]{:S(2)}, u32[]{:S(2)}) %collective-permute-start.8) | collective-permute-done | bytes 442400 | tf_op jit(solution)/shard_map/ppermute | solution.py:805
  29.0 1.5 collective-permute-start.18
  31.9 9.7 %collective-permute-done.10 = bf16[2,2,768]{2,1,0:T(2,128)(2,1)S(1)} collective-permute-done((bf16[2,2,768]{2,1,0:T(2,128)(2,1)S(1)}, bf16[2,2,768]{2,1,0:T(2,128)(2,1)S(1)}, u32[]{:S(2)}, u32[]{:S(2)}) %collective-permute-start.10) | collective-permute-done | bytes 6176 | tf_op jit(solution)/shard_map/ppermute | solution.py:792
  41.8 3.6 collective-permute-done.11
  46.5 1.5 collective-permute-start.19
  50.6 10.2 %collective-permute-done.14 = bf16[2,96,1152]{2,1,0:T(8,128)(2,1)} collective-permute-done((bf16[2,96,1152]{2,1,0:T(8,128)(2,1)}, bf16[2,96,1152]{2,1,0:T(8,128)(2,1)}, u32[]{:S(2)}, u32[]{:S(2)}) %collective-permute-start.14) | collective-permute-done | bytes 442400 | tf_op jit(solution)/shard_map/ppermute | solution.py:805
  62.1 1.6 reshape.274
  63.8 1.6 copy.72
  65.3 1.6 reshape.265
  67.7 1.5 reshape.264
  74.6 1.5 collective-permute-start.27
  76.1 4.4 collective-permute-done.20
  83.1 12.4 %forward_scan.4 = (bf16[2048,1536]{1,0:T(8,128)(2,1)}, bf16[1536,2048]{1,0:T(8,128)(2,1)}, f32[2048,1152]{1,0:T(8,128)}, f32[2048,1152]{1,0:T(8,128)}, f32[2048,...) custom-call(s32[4]{0:T(128)} %pad_add_fusion.place, bf16[512,1536]{1,0:T(8,128)(2,1)} %tok.1, ...), custom_call_target="tpu_custom_call" | custom-call | flops 12999999488 | bytes 45500000 | tf_op jit(solution)/shard_map/forward_scan/pallas_call | solution.py:511
  97.8 12.5 %forward_scan.5 = (bf16[2048,1536]{1,0:T(8,128)(2,1)}, bf16[1536,2048]{1,0:T(8,128)(2,1)}, f32[2048,1152]{1,0:T(8,128)}, f32[2048,1152]{1,0:T(8,128)}, f32[2048,...) custom-call(s32[4]{0:T(128)} %pad_add_fusion.place, ...), custom_call_target="tpu_custom_call", output_to_operand_aliasing={{0}: (10, {}), {1}: (11, {}), {2}: (12, {}), {3}: (13, {}),... | custom-call | flops 12999999488 | bytes 45500000 | tf_op jit(solution)/shard_map/forward_scan/pallas_call | solution.py:511
  110.4 1.5 collective-permute-start.25
  112.1 12.3 %forward_scan.6 = (bf16[2048,1536]{1,0:T(8,128)(2,1)}, bf16[1536,2048]{1,0:T(8,128)(2,1)}, f32[2048,1152]{1,0:T(8,128)}, f32[2048,1152]{1,0:T(8,128)}, f32[2048,...) custom-call(s32[4]{0:T(128)} %pad_add_fusion.place, ...), custom_call_target="tpu_custom_call", output_to_operand_aliasing={{0}: (10, {}), {1}: (11, {}), {2}: (12, {}), {3}: (13, {}),... | custom-call | flops 12999999488 | bytes 45500000 | tf_op jit(solution)/shard_map/forward_scan/pallas_call | solution.py:511
  124.5 1.9 collective-permute-done.25.refs_5_
  126.4 2.9 collective-permute-done.23.refs_6_
  130.0 12.3 %forward_scan.7 = (bf16[2048,1536]{1,0:T(8,128)(2,1)}, bf16[1536,2048]{1,0:T(8,128)(2,1)}, f32[2048,1152]{1,0:T(8,128)}, f32[2048,1152]{1,0:T(8,128)}, f32[2048,...) custom-call(s32[4]{0:T(128)} %pad_add_fusion.place, ...), custom_call_target="tpu_custom_call", output_to_operand_aliasing={{0}: (10, {}), {1}: (11, {}), {2}: (12, {}), {3}: (13, {}),... | custom-call | flops 12999999488 | bytes 45500000 | tf_op jit(solution)/shard_map/forward_scan/pallas_call | solution.py:511
  142.3 1.9 collective-permute-done.26.refs_7_
  144.2 5.9 %assemble.1 = (bf16[2,8,96,768]{3,2,1,0:T(8,128)(2,1)}, bf16[4,2,96,768]{3,2,1,0:T(8,128)(2,1)}, bf16[4,2,96,768]{3,2,1,0:T(8,128)(2,1)}) custom-call(s32[12]{0:T(128)} %concatenate.191.place, bf16[2,2,96,768]{3,2,1,0:T(8,128)(2,1)} %pad_maximum_fusion.1.refs_0_, bf16[2,2,96,768]{3,2,1,0:T(8,128)(2,1)} %collective-permute-done.22.refs_1_, ...), custom_call_target="tpu_custom_call" | custom-call | flops 3000000000 | bytes 10500000 | tf_op jit(solution)/shard_map/assemble/pallas_call | solution.py:562
  150.8 2.6 collective-permute-done.30
  153.3 18.7 %gate_and_stats.1 = (f32[2048,768]{1,0:T(8,128)}, f32[2048,768]{1,0:T(8,128)}, f32[8,2048]{1,0:T(8,128)}) custom-call(s32[4]{0:T(128)} %pad_add_fusion.place, bf16[2048,1536]{1,0:T(8,128)(2,1)} %get-tuple-element.199.normed, bf16[1536,768]{1,0:T(8,128)(2,1)} %bitcast.158, bf16[512,1536]{1,0:T(8,128)(2,1)} %cot.1, ...), custom_call_target="tpu_custom_call" | custom-call | flops 2000000000 | bytes 7000000 | tf_op jit(solution)/shard_map/gate_and_stats/pallas_call | solution.py:587
  173.3 3.2 collective-permute-done.31
  179.4 21.1 %finish.1 = (bf16[768,2048]{1,0:T(8,128)(2,1)}, bf16[1024,1536]{1,0:T(8,128)(2,1)}, bf16[1024,1536]{1,0:T(8,128)(2,1)}, f32[2048,768]{1,0:T(8,128)}, bf16[2048,768]{1,0:T(8,128)(2,1)}, /*index=5*/f32[8,768]{1,0:T(8,128)}) custom-call(s32[4]{0:T(128)} %pad_add_fusion.place, f32[8,2048]{1,0:T(8,128)} %maximum_add_fusion.stats, ...), custom_call_target="tpu_custom_call" | custom-call | flops 2000000000 | bytes 7000000 | tf_op jit(solution)/shard_map/finish/pallas_call | solution.py:610
  200.7 9.7 %weight_grad.3 = bf16[768,1536]{1,0:T(8,128)(2,1)} custom-call(bf16[768,2048]{1,0:T(8,128)(2,1)} %get-tuple-element.214.left, bf16[512,1536]{1,0:T(8,128)(2,1)} %cot.1, bf16[512,1536]{1,0:T(8,128)(2,1)} %collective-permute-done.27.cot_fa.rest_1_, bf16[512,1536]{1,0:T(8,128)(2,1)} %copy-done.3, bf16[512,1536]{1,0:T(8,128)(2,1)} %collective-permute-done.29.cot_fb.rest_3_), custom_call_target="tpu_custom_call" | custom-call | flops 1000000000 | bytes 3500000 | tf_op jit(solution)/shard_map/weight_grad/pallas_call | solution.py:674
  210.4 2.4 constant_dynamic-slice_fusion.1
  213.1 2.9 add_convert_fusion.1
  216.1 12.3 %weight_grad.4 = (bf16[8,2,2,96,768]{4,3,2,1,0:T(8,128)(2,1)}, f32[8,1536]{1,0:T(8,128)}) custom-call(s32[4]{0:T(128)} %pad_add_fusion.place, bf16[1536,2048]{1,0:T(8,128)(2,1)} %get-tuple-element.211.left, bf16[2048,768]{1,0:T(8,128)(2,1)} %get-tuple-element.216.right.refs_0_, bf16[1536,768]{1,0:T(8,128)(2,1)} %bitcast.159, bf16[1536,768]{1,0:T(8,128)(2,1)} %bitcast.160, ...), custom_call_target="tpu_custom_call" | custom-call | flops 1000000000 | bytes 3500000 | tf_op jit(solution)/shard_map/weight_grad/pallas_call | solution.py:703
  228.4 3.2 dynamic-slice_bitcast_fusion
  233.4 16.0 %backward_scan.4 = (bf16[2048,1152]{1,0:T(8,128)(2,1)}, f32[8,1024]{1,0:T(8,128)}, f32[8,128]{1,0:T(8,128)}, f32[8,768]{1,0:T(8,128)}, f32[8,1024]{1,0:T(8,128)}, /*index=5*/f32[128,768]{1,0:T(8,128)}) custom-call(s32[4]{0:T(128)} %pad_add_fusion.place, f32[2048,1152]{1,0:T(8,128)} %get-tuple-element.219.proj_in, ...), custom_call_target="tpu_custom_call" | custom-call | flops 2000000000 | bytes 7000000 | tf_op jit(solution)/shard_map/backward_scan/pallas_call | solution.py:644
  249.4 2.2 fusion.1
  253.0 15.6 %backward_scan.5 = (bf16[2048,1152]{1,0:T(8,128)(2,1)}, f32[8,1024]{1,0:T(8,128)}, f32[8,128]{1,0:T(8,128)}, f32[8,768]{1,0:T(8,128)}, f32[8,1024]{1,0:T(8,128)}, /*index=5*/f32[128,768]{1,0:T(8,128)}) custom-call(s32[4]{0:T(128)} %pad_add_fusion.place, f32[2048,1152]{1,0:T(8,128)} %get-tuple-element.219.proj_in, ...), custom_call_target="tpu_custom_call", output_to_operand_aliasing={{0}: (11, {})} | custom-call | flops 2000000000 | bytes 7000000 | tf_op jit(solution)/shard_map/backward_scan/pallas_call | solution.py:644
  269.8 2.4 fusion.3
  274.7 15.5 %backward_scan.6 = (bf16[2048,1152]{1,0:T(8,128)(2,1)}, f32[8,1024]{1,0:T(8,128)}, f32[8,128]{1,0:T(8,128)}, f32[8,768]{1,0:T(8,128)}, f32[8,1024]{1,0:T(8,128)}, /*index=5*/f32[128,768]{1,0:T(8,128)}) custom-call(s32[4]{0:T(128)} %pad_add_fusion.place, f32[2048,1152]{1,0:T(8,128)} %get-tuple-element.219.proj_in, ...), custom_call_target="tpu_custom_call", output_to_operand_aliasing={{0}: (11, {})} | custom-call | flops 2000000000 | bytes 7000000 | tf_op jit(solution)/shard_map/backward_scan/pallas_call | solution.py:644
  290.3 1.7 fusion.5
  293.7 15.7 %backward_scan.7 = (bf16[2048,1152]{1,0:T(8,128)(2,1)}, f32[8,1024]{1,0:T(8,128)}, f32[8,128]{1,0:T(8,128)}, f32[8,768]{1,0:T(8,128)}, f32[8,1024]{1,0:T(8,128)}, /*index=5*/f32[128,768]{1,0:T(8,128)}) custom-call(s32[4]{0:T(128)} %pad_add_fusion.place, f32[2048,1152]{1,0:T(8,128)} %get-tuple-element.219.proj_in, ...), custom_call_target="tpu_custom_call", output_to_operand_aliasing={{0}: (11, {})} | custom-call | flops 2000000000 | bytes 7000000 | tf_op jit(solution)/shard_map/backward_scan/pallas_call | solution.py:644
  314.5 15.3 %weight_grad.5 = (bf16[8,2,96,1152]{3,2,1,0:T(8,128)(2,1)}, f32[8,1536]{1,0:T(8,128)}) custom-call(s32[4]{0:T(128)} %pad_add_fusion.place, bf16[1536,2048]{1,0:T(8,128)(2,1)} %get-tuple-element.211.left, bf16[2048,1152]{1,0:T(8,128)(2,1)} %get-tuple-element.277.right.refs_1_, bf16[1536,1152]{1,0:T(8,128)(2,1)} %bitcast.151, bf16[1536,1152]{1,0:T(8,128)(2,1)} %bitcast.152, ...), custom_call_target="tpu_custom_call" | custom-call | flops 1000000000 | bytes 3500000 | tf_op jit(solution)/shard_map/weight_grad/pallas_call | solution.py:703
  329.7 2.5 dynamic-slice_bitcast_fusion.4
  333.9 8.3 %input_grad.4 = bf16[512,1536]{1,0:T(8,128)(2,1)} custom-call(s32[4]{0:T(128)} %pad_add_fusion.place, bf16[2048,768]{1,0:T(8,128)(2,1)} %get-tuple-element.216.right.refs_0_, bf16[2048,1152]{1,0:T(8,128)(2,1)} %get-tuple-element.277.right.refs_1_, bf16[1536,768]{1,0:T(8,128)(2,1)} %bitcast.161, bf16[1536,1152]{1,0:T(8,128)(2,1)} %bitcast.154), custom_call_target="tpu_custom_call" | custom-call | flops 1000000000 | bytes 3500000 | tf_op jit(solution)/shard_map/input_grad/pallas_call | solution.py:763
  342.8 1.5 collective-permute-start.48
  344.3 2.8 collective-permute-done.43
  348.3 8.4 %input_grad.5 = bf16[512,1536]{1,0:T(8,128)(2,1)} custom-call(s32[4]{0:T(128)} %pad_add_fusion.place, bf16[2048,768]{1,0:T(8,128)(2,1)} %get-tuple-element.216.right.refs_0_, bf16[2048,1152]{1,0:T(8,128)(2,1)} %get-tuple-element.277.right.refs_1_, bf16[1536,768]{1,0:T(8,128)(2,1)} %bitcast.162, bf16[1536,1152]{1,0:T(8,128)(2,1)} %bitcast.155), custom_call_target="tpu_custom_call" | custom-call | flops 1000000000 | bytes 3500000 | tf_op jit(solution)/shard_map/input_grad/pallas_call | solution.py:763
  356.7 1.7 add.600
  358.4 1.9 fusion.10
  360.2 3.4 collective-permute-start.53
  364.3 1.8 add_convert_fusion
  369.3 8.3 %input_grad.6 = bf16[512,1536]{1,0:T(8,128)(2,1)} custom-call(s32[4]{0:T(128)} %pad_add_fusion.place, bf16[2048,768]{1,0:T(8,128)(2,1)} %get-tuple-element.216.right.refs_0_, bf16[2048,1152]{1,0:T(8,128)(2,1)} %get-tuple-element.277.right.refs_1_, bf16[1536,768]{1,0:T(8,128)(2,1)} %bitcast.163, bf16[1536,1152]{1,0:T(8,128)(2,1)} %bitcast.156), custom_call_target="tpu_custom_call" | custom-call | flops 1000000000 | bytes 3500000 | tf_op jit(solution)/shard_map/input_grad/pallas_call | solution.py:763
  378.2 2.1 fusion.12
  384.9 8.3 %input_grad.7.near = bf16[512,1536]{1,0:T(8,128)(2,1)} custom-call(s32[4]{0:T(128)} %pad_add_fusion.place, bf16[2048,768]{1,0:T(8,128)(2,1)} %get-tuple-element.216.right.refs_0_, bf16[2048,1152]{1,0:T(8,128)(2,1)} %get-tuple-element.277.right.refs_1_, bf16[1536,768]{1,0:T(8,128)(2,1)} %bitcast.164, bf16[1536,1152]{1,0:T(8,128)(2,1)} %bitcast.157), custom_call_target="tpu_custom_call" | custom-call | flops 1000000000 | bytes 3500000 | tf_op jit(solution)/shard_map/input_grad/pallas_call | solution.py:763
  393.2 2.1 collective-permute-done.55.rest_1_
  398.1 4.8 %convert_add_fusion = f32[512,1536]{1,0:T(8,128)} fusion(bf16[512,1536]{1,0:T(8,128)(2,1)S(1)} %copy-done.10, bf16[512,1536]{1,0:T(8,128)(2,1)} %tok.1, bf16[1024,1536]{1,0:T(8,128)(2,1)} %collective-permute-done.33, bf16[1024,1536]{1,0:T(8,128)(2,1)} %get-tuple-element.212), kind=kLoop, calls=%fused_computation | loop fusion | flops 5505024 | bytes 9437184 | tf_op jit(solution)/shard_map/add | solution.py:1193
  402.9 3.0 collective-permute-done.57
  405.9 1.5 collective-permute-done.58
  412.0 2.7 multiply_subtract_fusion.1
  414.8 9.3 %collective-permute-done.60 = bf16[48,1920]{1,0:T(8,128)(2,1)S(1)} collective-permute-done((bf16[48,1920]{1,0:T(8,128)(2,1)S(1)}, bf16[48,1920]{1,0:T(8,128)(2,1)S(1)}, u32[]{:S(2)}, u32[]{:S(2)}) %collective-permute-start.60) | collective-permute-done | bytes 184352 | tf_op jit(solution)/shard_map/ppermute | solution.py:779
  425.4 2.5 multiply_subtract_fusion
  428.7 6.6 %tokens_grad.1 = f32[512,1536]{1,0:T(8,128)} custom-call(bf16[512,1536]{1,0:T(8,128)(2,1)} %tok.1, bf16[512,1536]{1,0:T(8,128)(2,1)} %cot.1, f32[1,1536]{1,0:T(1,128)} %slice.165.gain, bf16[512,1536]{1,0:T(8,128)(2,1)} %input_grad.7.near, bf16[512,1536]{1,0:T(8,128)(2,1)} %collective-permute-done.61.core, bf16[128,1536]{1,0:T(8,128)(2,1)} %collective-permute-done.50.rest_0_, ...), custom_call_target="tpu_custom_call" | custom-call | flops 4000000000 | bytes 14000000 | tf_op jit(solution)/shard_map/tokens_grad/pallas_call | solution.py:740
  (298 shorter events, 69.3 us)
Async XLA Ops:
  2.4 7.8 %collective-permute-start.1 = (bf16[48,1920]{1,0:T(8,128)(2,1)S(1)}, bf16[48,1920]{1,0:T(8,128)(2,1)S(1)}, u32[]{:S(2)}, u32[]{:S(2)}) collective-permute-start(bf16[48,1920]{1,0:T(8,128)(2,1)S(1)} %get-tuple-element.350), channel_id=1, source_target_pairs={{0,16},{16,0},{1,17},{17,1},{2,18},{18,2},{3,19},{19,3},{4,20},{20... | collective-permute-start | bytes 552968 | tf_op jit(solution)/shard_map/ppermute | solution.py:779
  5.6 4.5 %collective-permute-start.6 = (bf16[1,1,768]{2,1,0:T(2,128)(2,1)S(1)}, bf16[1,1,768]{2,1,0:T(2,128)(2,1)S(1)}, u32[]{:S(2)}, u32[]{:S(2)}) collective-permute-start(bf16[1,1,768]{2,1,0:T(2,128)(2,1)S(1)} %concatenate.170), channel_id=1, source_target_pairs={{0,16},{16,0},{1,17},{17,1},{2,18},{18,2},{3,19},{19,3},{4,20},{20... | collective-permute-start | bytes 4616 | tf_op jit(solution)/shard_map/ppermute | solution.py:779
  5.7 4.4 %collective-permute-start.15 = (bf16[96,768]{1,0:T(8,128)(2,1)S(1)}, bf16[96,768]{1,0:T(8,128)(2,1)S(1)}, u32[]{:S(2)}, u32[]{:S(2)}) collective-permute-start(bf16[96,768]{1,0:T(8,128)(2,1)S(1)} %get-tuple-element.342), channel_id=1, source_target_pairs={{0,1},{1,0},{2,3},{3,2},{4,5},{5,4},{6,7},{7,6},{8,9},{9,8},{10,11... | collective-permute-start | bytes 442376 | tf_op jit(solution)/shard_map/ppermute | solution.py:792
  5.8 106.1 %collective-permute-start = (bf16[512,1536]{1,0:T(8,128)(2,1)}, bf16[512,1536]{1,0:T(8,128)(2,1)}, u32[]{:S(2)}, u32[]{:S(2)}) collective-permute-start(bf16[512,1536]{1,0:T(8,128)(2,1)} %tok.1), channel_id=1, source_target_pairs={{0,1},{1,0},{2,3},{3,2},{4,5},{5,4},{6,7},{7,6},{8,9},{9,8},{10,11... | collective-permute-start | bytes 4718600 | tf_op jit(solution)/shard_map/ppermute | solution.py:792
  10.4 5.2 %collective-permute-start.2 = (bf16[48,1536]{1,0:T(8,128)(2,1)S(1)}, bf16[48,1536]{1,0:T(8,128)(2,1)S(1)}, u32[]{:S(2)}, u32[]{:S(2)}) collective-permute-start(bf16[48,1536]{1,0:T(8,128)(2,1)S(1)} %get-tuple-element.325), channel_id=1, source_target_pairs={{0,16},{16,0},{1,17},{17,1},{2,18},{18,2},{3,19},{19,3},{4,20},{20... | collective-permute-start | bytes 442376 | tf_op jit(solution)/shard_map/ppermute | solution.py:779
  12.3 3.4 collective-permute-start.7
  15.8 12.3 %collective-permute-start.8 = (bf16[2,96,1152]{2,1,0:T(8,128)(2,1)S(1)}, bf16[2,96,1152]{2,1,0:T(8,128)(2,1)S(1)}, u32[]{:S(2)}, u32[]{:S(2)}) collective-permute-start(bf16[2,96,1152]{2,1,0:T(8,128)(2,1)S(1)} %bitcast.168), channel_id=1, source_target_pairs={{0,4},{1,5},{2,6},{3,7},{4,8},{5,9},{6,10},{7,11},{8,12},{9,13},{1... | collective-permute-start | bytes 1327112 | tf_op jit(solution)/shard_map/ppermute | solution.py:805
  17.7 2.0 collective-permute-start.3
  17.8 12.7 %collective-permute-start.17 = (bf16[2,96,1152]{2,1,0:T(8,128)(2,1)S(1)}, bf16[2,96,1152]{2,1,0:T(8,128)(2,1)S(1)}, u32[]{:S(2)}, u32[]{:S(2)}) collective-permute-start(bf16[2,96,1152]{2,1,0:T(8,128)(2,1)S(1)} %bitcast.169), channel_id=1, source_target_pairs={{0,2},{1,3},{2,0},{3,1},{4,6},{5,7},{6,4},{7,5},{8,10},{9,11},{10,... | collective-permute-start | bytes 1327112 | tf_op jit(solution)/shard_map/ppermute | solution.py:792
  19.7 54.8 %collective-permute-start.4 = (bf16[512,1536]{1,0:T(8,128)(2,1)}, bf16[512,1536]{1,0:T(8,128)(2,1)}, u32[]{:S(2)}, u32[]{:S(2)}) collective-permute-start(bf16[512,1536]{1,0:T(8,128)(2,1)} %tok.1), channel_id=1, source_target_pairs={{0,16},{16,0},{1,17},{17,1},{2,18},{18,2},{3,19},{19,3},{4,20},{20... | collective-permute-start | bytes 4718600 | tf_op jit(solution)/shard_map/ppermute | solution.py:779
  28.1 2.4 collective-permute-start.9
  29.0 19.0 %collective-permute-start.18 = (bf16[2,96,1152]{2,1,0:T(8,128)(2,1)S(1)}, bf16[2,96,1152]{2,1,0:T(8,128)(2,1)S(1)}, u32[]{:S(2)}, u32[]{:S(2)}) collective-permute-start(bf16[2,96,1152]{2,1,0:T(8,128)(2,1)S(1)} %collective-permute-done.8), channel_id=1, source_target_pairs={{0,2},{1,3},{2,0},{3,1},{4,6},{5,7},{6,4},{7,5},{8,10},{9,11},{10,... | collective-permute-start | bytes 1327112 | tf_op jit(solution)/shard_map/ppermute | solution.py:792
  30.5 15.0 %collective-permute-start.12 = (bf16[2,96,1152]{2,1,0:T(8,128)(2,1)S(1)}, bf16[2,96,1152]{2,1,0:T(8,128)(2,1)}, u32[]{:S(2)}, u32[]{:S(2)}) collective-permute-start(bf16[2,96,1152]{2,1,0:T(8,128)(2,1)S(1)} %collective-permute-done.8), channel_id=1, source_target_pairs={{0,4},{1,5},{2,6},{3,7},{4,8},{5,9},{6,10},{7,11},{8,12},{9,13},{1... | collective-permute-start | bytes 1327112 | tf_op jit(solution)/shard_map/ppermute | solution.py:805
  30.5 11.1 %collective-permute-start.10 = (bf16[2,2,768]{2,1,0:T(2,128)(2,1)S(1)}, bf16[2,2,768]{2,1,0:T(2,128)(2,1)S(1)}, u32[]{:S(2)}, u32[]{:S(2)}) collective-permute-start(bf16[2,2,768]{2,1,0:T(2,128)(2,1)S(1)} %broadcast_select_fusion.1), channel_id=1, source_target_pairs={{0,2},{1,3},{2,0},{3,1},{4,6},{5,7},{6,4},{7,5},{8,10},{9,11},{10,... | collective-permute-start | bytes 18440 | tf_op jit(solution)/shard_map/ppermute | solution.py:792
  41.7 3.8 collective-permute-start.11
  45.5 5.0 %collective-permute-start.13 = (bf16[2,8,768]{2,1,0:T(8,128)(2,1)S(1)}, bf16[2,8,768]{2,1,0:T(8,128)(2,1)S(1)}, u32[]{:S(2)}, u32[]{:S(2)}) collective-permute-start(bf16[2,8,768]{2,1,0:T(8,128)(2,1)S(1)} %maximum_select_fusion.11), channel_id=1, source_target_pairs={{0,8},{1,9},{2,10},{3,11},{4,12},{5,13},{6,14},{7,15},{8,0},{9,1},... | collective-permute-start | bytes 73736 | tf_op jit(solution)/shard_map/ppermute | solution.py:792
  46.5 25.9 %collective-permute-start.19 = (bf16[2,96,1152]{2,1,0:T(8,128)(2,1)}, bf16[2,96,1152]{2,1,0:T(8,128)(2,1)}, u32[]{:S(2)}, u32[]{:S(2)}) collective-permute-start(bf16[2,96,1152]{2,1,0:T(8,128)(2,1)} %collective-permute-done.12), channel_id=1, source_target_pairs={{0,2},{1,3},{2,0},{3,1},{4,6},{5,7},{6,4},{7,5},{8,10},{9,11},{10,... | collective-permute-start | bytes 1327112 | tf_op jit(solution)/shard_map/ppermute | solution.py:792
  48.0 12.8 %collective-permute-start.14 = (bf16[2,96,1152]{2,1,0:T(8,128)(2,1)}, bf16[2,96,1152]{2,1,0:T(8,128)(2,1)}, u32[]{:S(2)}, u32[]{:S(2)}) collective-permute-start(bf16[2,96,1152]{2,1,0:T(8,128)(2,1)} %collective-permute-done.12), channel_id=1, source_target_pairs={{0,4},{1,5},{2,6},{3,7},{4,8},{5,9},{6,10},{7,11},{8,12},{9,13},{1... | collective-permute-start | bytes 1327112 | tf_op jit(solution)/shard_map/ppermute | solution.py:805
  70.4 25.1 %collective-permute-start.16 = (bf16[2,2,96,768]{3,2,1,0:T(8,128)(2,1)}, bf16[2,2,96,768]{3,2,1,0:T(8,128)(2,1)}, u32[]{:S(2)}, u32[]{:S(2)}) collective-permute-start(bf16[2,2,96,768]{3,2,1,0:T(8,128)(2,1)} %pad_maximum_fusion.1.refs_0_), channel_id=1, source_target_pairs={{0,4},{1,5},{2,6},{3,7},{4,8},{5,9},{6,10},{7,11},{8,12},{9,13},{1... | collective-permute-start | bytes 1769480 | tf_op jit(solution)/shard_map/ppermute | solution.py:805
  70.4 10.1 %collective-permute-start.20 = (bf16[2,96,1152]{2,1,0:T(8,128)(2,1)}, bf16[2,96,1152]{2,1,0:T(8,128)(2,1)S(1)}, u32[]{:S(2)}, u32[]{:S(2)}) collective-permute-start(bf16[2,96,1152]{2,1,0:T(8,128)(2,1)} %collective-permute-done.14), channel_id=1, source_target_pairs={{0,2},{1,3},{2,0},{3,1},{4,6},{5,7},{6,4},{7,5},{8,10},{9,11},{10,... | collective-permute-start | bytes 1327112 | tf_op jit(solution)/shard_map/ppermute | solution.py:792
  74.5 37.6 %collective-permute-start.5 = (bf16[512,1536]{1,0:T(8,128)(2,1)}, bf16[512,1536]{1,0:T(8,128)(2,1)}, u32[]{:S(2)}, u32[]{:S(2)}) collective-permute-start(bf16[512,1536]{1,0:T(8,128)(2,1)} %collective-permute-done.4.far), channel_id=1, source_target_pairs={{0,1},{1,0},{2,3},{3,2},{4,5},{5,4},{6,7},{7,6},{8,9},{9,8},{10,11... | collective-permute-start | bytes 4718600 | tf_op jit(solution)/shard_map/ppermute | solution.py:792
  74.6 55.4 %collective-permute-start.27 = (bf16[512,1536]{1,0:T(8,128)(2,1)}, bf16[512,1536]{1,0:T(8,128)(2,1)}, u32[]{:S(2)}, u32[]{:S(2)}) collective-permute-start(bf16[512,1536]{1,0:T(8,128)(2,1)} %cot.1), channel_id=1, source_target_pairs={{0,16},{16,0},{1,17},{17,1},{2,18},{18,2},{3,19},{19,3},{4,20},{20... | collective-permute-start | bytes 4718600 | tf_op jit(solution)/shard_map/ppermute | solution.py:779
  80.6 16.0 %collective-permute-start.22 = (bf16[2,2,96,768]{3,2,1,0:T(8,128)(2,1)}, bf16[2,2,96,768]{3,2,1,0:T(8,128)(2,1)}, u32[]{:S(2)}, u32[]{:S(2)}) collective-permute-start(bf16[2,2,96,768]{3,2,1,0:T(8,128)(2,1)} %pad_maximum_fusion.1.refs_0_), channel_id=1, source_target_pairs={{0,2},{1,3},{2,0},{3,1},{4,6},{5,7},{6,4},{7,5},{8,10},{9,11},{10,... | collective-permute-start | bytes 1769480 | tf_op jit(solution)/shard_map/ppermute | solution.py:792
  95.5 14.8 %collective-permute-start.24 = (bf16[2,2,96,768]{3,2,1,0:T(8,128)(2,1)}, bf16[2,2,96,768]{3,2,1,0:T(8,128)(2,1)}, u32[]{:S(2)}, u32[]{:S(2)}) collective-permute-start(bf16[2,2,96,768]{3,2,1,0:T(8,128)(2,1)} %collective-permute-done.16.refs_2_), channel_id=1, source_target_pairs={{0,2},{1,3},{2,0},{3,1},{4,6},{5,7},{6,4},{7,5},{8,10},{9,11},{10,... | collective-permute-start | bytes 1769480 | tf_op jit(solution)/shard_map/ppermute | solution.py:792
  96.5 13.8 %collective-permute-start.21 = (bf16[2,2,96,768]{3,2,1,0:T(8,128)(2,1)}, bf16[2,2,96,768]{3,2,1,0:T(8,128)(2,1)}, u32[]{:S(2)}, u32[]{:S(2)}) collective-permute-start(bf16[2,2,96,768]{3,2,1,0:T(8,128)(2,1)} %collective-permute-done.16.refs_2_), channel_id=1, source_target_pairs={{0,4},{1,5},{2,6},{3,7},{4,8},{5,9},{6,10},{7,11},{8,12},{9,13},{1... | collective-permute-start | bytes 1769480 | tf_op jit(solution)/shard_map/ppermute | solution.py:805
  110.3 40.5 %collective-permute-start.28 = (bf16[512,1536]{1,0:T(8,128)(2,1)S(1)}, bf16[512,1536]{1,0:T(8,128)(2,1)S(1)}, u32[]{:S(2)}, u32[]{:S(2)}) collective-permute-start(bf16[512,1536]{1,0:T(8,128)(2,1)S(1)} %copy-done.2), channel_id=1, source_target_pairs={{0,1},{1,0},{2,3},{3,2},{4,5},{5,4},{6,7},{7,6},{8,9},{9,8},{10,11... | collective-permute-start | bytes 4718600 | tf_op jit(solution)/shard_map/ppermute | solution.py:792
  110.4 16.1 %collective-permute-start.25 = (bf16[2,2,96,768]{3,2,1,0:T(8,128)(2,1)}, bf16[2,2,96,768]{3,2,1,0:T(8,128)(2,1)}, u32[]{:S(2)}, u32[]{:S(2)}) collective-permute-start(bf16[2,2,96,768]{3,2,1,0:T(8,128)(2,1)} %collective-permute-done.21.refs_4_), channel_id=1, source_target_pairs={{0,2},{1,3},{2,0},{3,1},{4,6},{5,7},{6,4},{7,5},{8,10},{9,11},{10,... | collective-permute-start | bytes 1769480 | tf_op jit(solution)/shard_map/ppermute | solution.py:792
  111.9 17.5 %collective-permute-start.23 = (bf16[2,2,96,768]{3,2,1,0:T(8,128)(2,1)}, bf16[2,2,96,768]{3,2,1,0:T(8,128)(2,1)}, u32[]{:S(2)}, u32[]{:S(2)}) collective-permute-start(bf16[2,2,96,768]{3,2,1,0:T(8,128)(2,1)} %collective-permute-done.21.refs_4_), channel_id=1, source_target_pairs={{0,4},{1,5},{2,6},{3,7},{4,8},{5,9},{6,10},{7,11},{8,12},{9,13},{1... | collective-permute-start | bytes 1769480 | tf_op jit(solution)/shard_map/ppermute | solution.py:805
  129.4 14.9 %collective-permute-start.26 = (bf16[2,2,96,768]{3,2,1,0:T(8,128)(2,1)}, bf16[2,2,96,768]{3,2,1,0:T(8,128)(2,1)}, u32[]{:S(2)}, u32[]{:S(2)}) collective-permute-start(bf16[2,2,96,768]{3,2,1,0:T(8,128)(2,1)} %collective-permute-done.23.refs_6_), channel_id=1, source_target_pairs={{0,2},{1,3},{2,0},{3,1},{4,6},{5,7},{6,4},{7,5},{8,10},{9,11},{10,... | collective-permute-start | bytes 1769480 | tf_op jit(solution)/shard_map/ppermute | solution.py:792
  130.0 20.8 %collective-permute-start.29 = (bf16[512,1536]{1,0:T(8,128)(2,1)}, bf16[512,1536]{1,0:T(8,128)(2,1)}, u32[]{:S(2)}, u32[]{:S(2)}) collective-permute-start(bf16[512,1536]{1,0:T(8,128)(2,1)} %collective-permute-done.27.cot_fa.rest_1_), channel_id=1, source_target_pairs={{0,1},{1,0},{2,3},{3,2},{4,5},{5,4},{6,7},{7,6},{8,9},{9,8},{10,11... | collective-permute-start | bytes 4718600 | tf_op jit(solution)/shard_map/ppermute | solution.py:792
  150.1 3.2 collective-permute-start.30
  172.0 4.5 %collective-permute-start.31 = (f32[8,2048]{1,0:T(8,128)}, f32[8,2048]{1,0:T(8,128)S(1)}, u32[]{:S(2)}, u32[]{:S(2)}) collective-permute-start(f32[8,2048]{1,0:T(8,128)} %get-tuple-element.207), channel_id=1, source_target_pairs={{0,16},{16,0},{1,17},{17,1},{2,18},{18,2},{3,19},{19,3},{4,20},{20... | collective-permute-start | bytes 196616 | tf_op jit(solution)/shard_map/ppermute | solution.py:779
  200.5 9.9 %collective-permute-start.33 = (bf16[1024,1536]{1,0:T(8,128)(2,1)}, bf16[1024,1536]{1,0:T(8,128)(2,1)}, u32[]{:S(2)}, u32[]{:S(2)}) collective-permute-start(bf16[1024,1536]{1,0:T(8,128)(2,1)} %get-tuple-element.213), channel_id=1, source_target_pairs={{0,1},{1,0},{2,3},{3,2},{4,5},{5,4},{6,7},{7,6},{8,9},{9,8},{10,11... | collective-permute-start | bytes 9437192 | tf_op jit(solution)/shard_map/ppermute | solution.py:792
  212.8 3.3 collective-permute-start.34
  231.5 17.8 %collective-permute-start.35 = (bf16[2,2,96,768]{3,2,1,0:T(8,128)(2,1)}, bf16[2,2,96,768]{3,2,1,0:T(8,128)(2,1)}, u32[]{:S(2)}, u32[]{:S(2)}) collective-permute-start(bf16[2,2,96,768]{3,2,1,0:T(8,128)(2,1)} %get-tuple-element.315), channel_id=1, source_target_pairs={{0,2},{1,3},{2,0},{3,1},{4,6},{5,7},{6,4},{7,5},{8,10},{9,11},{10,... | collective-permute-start | bytes 1769480 | tf_op jit(solution)/shard_map/ppermute | solution.py:792
  232.1 42.5 %collective-permute-start.39 = (bf16[512,1536]{1,0:T(8,128)(2,1)S(1)}, bf16[512,1536]{1,0:T(8,128)(2,1)S(1)}, u32[]{:S(2)}, u32[]{:S(2)}) collective-permute-start(bf16[512,1536]{1,0:T(8,128)(2,1)S(1)} %copy-done.11), channel_id=1, source_target_pairs={{0,16},{16,0},{1,17},{17,1},{2,18},{18,2},{3,19},{19,3},{4,20},{20... | collective-permute-start | bytes 4718600 | tf_op jit(solution)/shard_map/ppermute | solution.py:779
  251.6 17.0 %collective-permute-start.36 = (bf16[2,2,96,768]{3,2,1,0:T(8,128)(2,1)}, bf16[2,2,96,768]{3,2,1,0:T(8,128)(2,1)}, u32[]{:S(2)}, u32[]{:S(2)}) collective-permute-start(bf16[2,2,96,768]{3,2,1,0:T(8,128)(2,1)} %get-tuple-element.226), channel_id=1, source_target_pairs={{0,2},{1,3},{2,0},{3,1},{4,6},{5,7},{6,4},{7,5},{8,10},{9,11},{10,... | collective-permute-start | bytes 1769480 | tf_op jit(solution)/shard_map/ppermute | solution.py:792
  253.0 16.8 %collective-permute-start.37 = (bf16[2,2,96,768]{3,2,1,0:T(8,128)(2,1)}, bf16[2,2,96,768]{3,2,1,0:T(8,128)(2,1)}, u32[]{:S(2)}, u32[]{:S(2)}) collective-permute-start(bf16[2,2,96,768]{3,2,1,0:T(8,128)(2,1)} %fusion.1), channel_id=1, source_target_pairs={{0,4},{1,5},{2,6},{3,7},{4,8},{5,9},{6,10},{7,11},{8,12},{9,13},{1... | collective-permute-start | bytes 1769480 | tf_op jit(solution)/shard_map/ppermute | solution.py:805
  272.2 18.0 %collective-permute-start.38 = (bf16[2,2,96,768]{3,2,1,0:T(8,128)(2,1)}, bf16[2,2,96,768]{3,2,1,0:T(8,128)(2,1)}, u32[]{:S(2)}, u32[]{:S(2)}) collective-permute-start(bf16[2,2,96,768]{3,2,1,0:T(8,128)(2,1)} %get-tuple-element.234), channel_id=1, source_target_pairs={{0,2},{1,3},{2,0},{3,1},{4,6},{5,7},{6,4},{7,5},{8,10},{9,11},{10,... | collective-permute-start | bytes 1769480 | tf_op jit(solution)/shard_map/ppermute | solution.py:792
  272.8 17.4 %collective-permute-start.40 = (bf16[2,2,96,768]{3,2,1,0:T(8,128)(2,1)}, bf16[2,2,96,768]{3,2,1,0:T(8,128)(2,1)}, u32[]{:S(2)}, u32[]{:S(2)}) collective-permute-start(bf16[2,2,96,768]{3,2,1,0:T(8,128)(2,1)} %fusion.3), channel_id=1, source_target_pairs={{0,4},{1,5},{2,6},{3,7},{4,8},{5,9},{6,10},{7,11},{8,12},{9,13},{1... | collective-permute-start | bytes 1769480 | tf_op jit(solution)/shard_map/ppermute | solution.py:805
  292.0 20.3 %collective-permute-start.42 = (bf16[2,2,96,768]{3,2,1,0:T(8,128)(2,1)S(1)}, bf16[2,2,96,768]{3,2,1,0:T(8,128)(2,1)S(1)}, u32[]{:S(2)}, u32[]{:S(2)}) collective-permute-start(bf16[2,2,96,768]{3,2,1,0:T(8,128)(2,1)S(1)} %fusion.5), channel_id=1, source_target_pairs={{0,4},{1,5},{2,6},{3,7},{4,8},{5,9},{6,10},{7,11},{8,12},{9,13},{1... | collective-permute-start | bytes 1769480 | tf_op jit(solution)/shard_map/ppermute | solution.py:805
  292.6 19.7 %collective-permute-start.41 = (bf16[2,2,96,768]{3,2,1,0:T(8,128)(2,1)S(1)}, bf16[2,2,96,768]{3,2,1,0:T(8,128)(2,1)S(1)}, u32[]{:S(2)}, u32[]{:S(2)}) collective-permute-start(bf16[2,2,96,768]{3,2,1,0:T(8,128)(2,1)S(1)} %copy-done.15), channel_id=1, source_target_pairs={{0,2},{1,3},{2,0},{3,1},{4,6},{5,7},{6,4},{7,5},{8,10},{9,11},{10,... | collective-permute-start | bytes 1769480 | tf_op jit(solution)/shard_map/ppermute | solution.py:792
  314.4 19.3 %collective-permute-start.44 = (bf16[2,48,768]{2,1,0:T(8,128)(2,1)S(1)}, bf16[2,48,768]{2,1,0:T(8,128)(2,1)S(1)}, u32[]{:S(2)}, u32[]{:S(2)}) collective-permute-start(bf16[2,48,768]{2,1,0:T(8,128)(2,1)S(1)} %get-tuple-element.340), channel_id=1, source_target_pairs={{0,1},{1,0},{2,3},{3,2},{4,5},{5,4},{6,7},{7,6},{8,9},{9,8},{10,11... | collective-permute-start | bytes 442376 | tf_op jit(solution)/shard_map/ppermute | solution.py:792
  342.2 22.1 %collective-permute-start.46 = (bf16[512,1536]{1,0:T(8,128)(2,1)}, bf16[512,1536]{1,0:T(8,128)(2,1)}, u32[]{:S(2)}, u32[]{:S(2)}) collective-permute-start(bf16[512,1536]{1,0:T(8,128)(2,1)} %input_grad.4), channel_id=1, source_target_pairs={{0,1},{1,0},{2,3},{3,2},{4,5},{5,4},{6,7},{7,6},{8,9},{9,8},{10,11... | collective-permute-start | bytes 4718600 | tf_op jit(solution)/shard_map/ppermute | solution.py:792
  342.5 4.6 %collective-permute-start.43 = (f32[168,128]{1,0:T(8,128)S(1)}, f32[168,128]{1,0:T(8,128)S(1)}, u32[]{:S(2)}, u32[]{:S(2)}) collective-permute-start(f32[168,128]{1,0:T(8,128)S(1)} %pad_maximum_fusion.6), channel_id=1, source_target_pairs={{0,16},{16,0},{1,17},{17,1},{2,18},{18,2},{3,19},{19,3},{4,20},{20... | collective-permute-start | bytes 258056 | tf_op jit(solution)/shard_map/ppermute | solution.py:779
  342.8 15.6 %collective-permute-start.48 = (bf16[2,96,1152]{2,1,0:T(8,128)(2,1)S(1)}, bf16[2,96,1152]{2,1,0:T(8,128)(2,1)}, u32[]{:S(2)}, u32[]{:S(2)}) collective-permute-start(bf16[2,96,1152]{2,1,0:T(8,128)(2,1)S(1)} %get-tuple-element.319), channel_id=1, source_target_pairs={{0,2},{1,3},{2,0},{3,1},{4,6},{5,7},{6,4},{7,5},{8,10},{9,11},{10,... | collective-permute-start | bytes 1327112 | tf_op jit(solution)/shard_map/ppermute | solution.py:792
  347.1 9.6 %collective-permute-start.51 = (f32[168,128]{1,0:T(8,128)S(1)}, f32[168,128]{1,0:T(8,128)}, u32[]{:S(2)}, u32[]{:S(2)}) collective-permute-start(f32[168,128]{1,0:T(8,128)S(1)} %fusion.40), channel_id=1, source_target_pairs={{0,1},{1,0},{2,3},{3,2},{4,5},{5,4},{6,7},{7,6},{8,9},{9,8},{10,11... | collective-permute-start | bytes 258056 | tf_op jit(solution)/shard_map/ppermute | solution.py:792
  348.0 15.7 %collective-permute-start.52 = (bf16[48,1536]{1,0:T(8,128)(2,1)}, bf16[48,1536]{1,0:T(8,128)(2,1)}, u32[]{:S(2)}, u32[]{:S(2)}) collective-permute-start(bf16[48,1536]{1,0:T(8,128)(2,1)} %get-tuple-element.337), channel_id=1, source_target_pairs={{0,16},{16,0},{1,17},{17,1},{2,18},{18,2},{3,19},{19,3},{4,20},{20... | collective-permute-start | bytes 442376 | tf_op jit(solution)/shard_map/ppermute | solution.py:779
  360.2 18.0 %collective-permute-start.53 = (bf16[2,96,1152]{2,1,0:T(8,128)(2,1)}, bf16[2,96,1152]{2,1,0:T(8,128)(2,1)}, u32[]{:S(2)}, u32[]{:S(2)}) collective-permute-start(bf16[2,96,1152]{2,1,0:T(8,128)(2,1)} %fusion.10), channel_id=1, source_target_pairs={{0,4},{1,5},{2,6},{3,7},{4,8},{5,9},{6,10},{7,11},{8,12},{9,13},{1... | collective-permute-start | bytes 1327112 | tf_op jit(solution)/shard_map/ppermute | solution.py:805
  363.7 14.6 %collective-permute-start.49 = (bf16[2,96,1152]{2,1,0:T(8,128)(2,1)}, bf16[2,96,1152]{2,1,0:T(8,128)(2,1)}, u32[]{:S(2)}, u32[]{:S(2)}) collective-permute-start(bf16[2,96,1152]{2,1,0:T(8,128)(2,1)} %get-tuple-element.268), channel_id=1, source_target_pairs={{0,2},{1,3},{2,0},{3,1},{4,6},{5,7},{6,4},{7,5},{8,10},{9,11},{10,... | collective-permute-start | bytes 1327112 | tf_op jit(solution)/shard_map/ppermute | solution.py:792
  367.3 11.0 %collective-permute-start.50 = (bf16[128,1536]{1,0:T(8,128)(2,1)}, bf16[128,1536]{1,0:T(8,128)(2,1)}, u32[]{:S(2)}, u32[]{:S(2)}) collective-permute-start(bf16[128,1536]{1,0:T(8,128)(2,1)} %get-tuple-element.322), channel_id=1, source_target_pairs={{0,16},{16,0},{1,17},{17,1},{2,18},{18,2},{3,19},{19,3},{4,20},{20... | collective-permute-start | bytes 1179656 | tf_op jit(solution)/shard_map/ppermute | solution.py:779
  380.3 14.9 %collective-permute-start.54 = (bf16[2,96,1152]{2,1,0:T(8,128)(2,1)}, bf16[2,96,1152]{2,1,0:T(8,128)(2,1)}, u32[]{:S(2)}, u32[]{:S(2)}) collective-permute-start(bf16[2,96,1152]{2,1,0:T(8,128)(2,1)} %get-tuple-element.275), channel_id=1, source_target_pairs={{0,2},{1,3},{2,0},{3,1},{4,6},{5,7},{6,4},{7,5},{8,10},{9,11},{10,... | collective-permute-start | bytes 1327112 | tf_op jit(solution)/shard_map/ppermute | solution.py:792
  381.7 13.5 %collective-permute-start.56 = (bf16[2,96,1152]{2,1,0:T(8,128)(2,1)}, bf16[2,96,1152]{2,1,0:T(8,128)(2,1)}, u32[]{:S(2)}, u32[]{:S(2)}) collective-permute-start(bf16[2,96,1152]{2,1,0:T(8,128)(2,1)} %fusion.12), channel_id=1, source_target_pairs={{0,4},{1,5},{2,6},{3,7},{4,8},{5,9},{6,10},{7,11},{8,12},{9,13},{1... | collective-permute-start | bytes 1327112 | tf_op jit(solution)/shard_map/ppermute | solution.py:805
  382.9 12.4 %collective-permute-start.55 = (bf16[128,1536]{1,0:T(8,128)(2,1)}, bf16[128,1536]{1,0:T(8,128)(2,1)}, u32[]{:S(2)}, u32[]{:S(2)}) collective-permute-start(bf16[128,1536]{1,0:T(8,128)(2,1)} %get-tuple-element.321), channel_id=1, source_target_pairs={{0,16},{16,0},{1,17},{17,1},{2,18},{18,2},{3,19},{19,3},{4,20},{20... | collective-permute-start | bytes 1179656 | tf_op jit(solution)/shard_map/ppermute | solution.py:779
  384.0 18.9 %collective-permute-start.47 = (bf16[128,1536]{1,0:T(8,128)(2,1)}, bf16[128,1536]{1,0:T(8,128)(2,1)}, u32[]{:S(2)}, u32[]{:S(2)}) collective-permute-start(bf16[128,1536]{1,0:T(8,128)(2,1)} %get-tuple-element.323), channel_id=1, source_target_pairs={{0,16},{16,0},{1,17},{17,1},{2,18},{18,2},{3,19},{19,3},{4,20},{20... | collective-permute-start | bytes 1179656 | tf_op jit(solution)/shard_map/ppermute | solution.py:779
  396.6 10.9 %collective-permute-start.58 = (bf16[2,96,1152]{2,1,0:T(8,128)(2,1)S(1)}, bf16[2,96,1152]{2,1,0:T(8,128)(2,1)S(1)}, u32[]{:S(2)}, u32[]{:S(2)}) collective-permute-start(bf16[2,96,1152]{2,1,0:T(8,128)(2,1)S(1)} %fusion.14), channel_id=1, source_target_pairs={{0,4},{1,5},{2,6},{3,7},{4,8},{5,9},{6,10},{7,11},{8,12},{9,13},{1... | collective-permute-start | bytes 1327112 | tf_op jit(solution)/shard_map/ppermute | solution.py:805
  397.0 8.9 %collective-permute-start.57 = (bf16[2,96,1152]{2,1,0:T(8,128)(2,1)}, bf16[2,96,1152]{2,1,0:T(8,128)(2,1)S(1)}, u32[]{:S(2)}, u32[]{:S(2)}) collective-permute-start(bf16[2,96,1152]{2,1,0:T(8,128)(2,1)} %get-tuple-element.283), channel_id=1, source_target_pairs={{0,2},{1,3},{2,0},{3,1},{4,6},{5,7},{6,4},{7,5},{8,10},{9,11},{10,... | collective-permute-start | bytes 1327112 | tf_op jit(solution)/shard_map/ppermute | solution.py:792
  407.7 3.0 collective-permute-start.59
  407.8 6.9 %collective-permute-start.63 = (f32[168,128]{1,0:T(8,128)}, f32[168,128]{1,0:T(8,128)S(1)}, u32[]{:S(2)}, u32[]{:S(2)}) collective-permute-start(f32[168,128]{1,0:T(8,128)} %add.600), channel_id=1, source_target_pairs={{0,2},{1,3},{2,0},{3,1},{4,6},{5,7},{6,4},{7,5},{8,10},{9,11},{10,... | collective-permute-start | bytes 258056 | tf_op jit(solution)/shard_map/ppermute | solution.py:792
  408.5 19.5 %collective-permute-start.61 = (bf16[512,1536]{1,0:T(8,128)(2,1)}, bf16[512,1536]{1,0:T(8,128)(2,1)}, u32[]{:S(2)}, u32[]{:S(2)}) collective-permute-start(bf16[512,1536]{1,0:T(8,128)(2,1)} %input_grad.6), channel_id=1, source_target_pairs={{0,1},{1,0},{2,3},{3,2},{4,5},{5,4},{6,7},{7,6},{8,9},{9,8},{10,11... | collective-permute-start | bytes 4718600 | tf_op jit(solution)/shard_map/ppermute | solution.py:792
  408.6 19.3 %collective-permute-start.62 = (bf16[128,1536]{1,0:T(8,128)(2,1)}, bf16[128,1536]{1,0:T(8,128)(2,1)S(1)}, u32[]{:S(2)}, u32[]{:S(2)}) collective-permute-start(bf16[128,1536]{1,0:T(8,128)(2,1)} %get-tuple-element.320), channel_id=1, source_target_pairs={{0,16},{16,0},{1,17},{17,1},{2,18},{18,2},{3,19},{19,3},{4,20},{20... | collective-permute-start | bytes 1179656 | tf_op jit(solution)/shard_map/ppermute | solution.py:779
  411.0 13.2 %collective-permute-start.60 = (bf16[48,1920]{1,0:T(8,128)(2,1)S(1)}, bf16[48,1920]{1,0:T(8,128)(2,1)S(1)}, u32[]{:S(2)}, u32[]{:S(2)}) collective-permute-start(bf16[48,1920]{1,0:T(8,128)(2,1)S(1)} %get-tuple-element.333), channel_id=1, source_target_pairs={{0,16},{16,0},{1,17},{17,1},{2,18},{18,2},{3,19},{19,3},{4,20},{20... | collective-permute-start | bytes 552968 | tf_op jit(solution)/shard_map/ppermute | solution.py:779
  414.8 9.5 %collective-permute-start.64 = (f32[168,128]{1,0:T(8,128)S(1)}, f32[168,128]{1,0:T(8,128)S(1)}, u32[]{:S(2)}, u32[]{:S(2)}) collective-permute-start(f32[168,128]{1,0:T(8,128)S(1)} %add.624), channel_id=1, source_target_pairs={{0,4},{1,5},{2,6},{3,7},{4,0},{5,1},{6,2},{7,3},{8,12},{9,13},{10,... | collective-permute-start | bytes 258056 | tf_op jit(solution)/shard_map/ppermute | solution.py:792
  424.3 11.0 %collective-permute-start.65 = (f32[168,128]{1,0:T(8,128)S(1)}, f32[168,128]{1,0:T(8,128)S(1)}, u32[]{:S(2)}, u32[]{:S(2)}) collective-permute-start(f32[168,128]{1,0:T(8,128)S(1)} %add.625), channel_id=1, source_target_pairs={{0,8},{1,9},{2,10},{3,11},{4,12},{5,13},{6,14},{7,15},{8,0},{9,1},... | collective-permute-start | bytes 258056 | tf_op jit(solution)/shard_map/ppermute | solution.py:792
  (42 other events, 346.1 us)

commit v2 on v1

--- a/solution.py
+++ b/solution.py
@@ -402,13 +402,16 @@
     state_out[...] = grad_mem[...]
 
 
-def outer_kernel(left, *rest):
-    out = rest[-1]
+def outer_kernel(place, left, *rest):
+    own, send = rest[-2:]
     total = None
-    for n, right in enumerate(rest[:-1]):
+    for n, right in enumerate(rest[:-2]):
         part = mm(left[:, n * HALF : (n + 1) * HALF], right[...])
         total = part if total is None else total + part
-    out[...] = total.astype(bf16)
+    total = total.astype(bf16)
+    mine, other = by_core(place[1], total[:, :QW], total[:, QW:])
+    own[...] = mine
+    send[...] = other
 
 
 def pieces_kernel(chip_rows, blocks, place, left, right, *rest):
@@ -668,20 +671,23 @@
     )(*args, *buffers)
 
 
-def run_outer(left, rights):
+def run_outer(place, left, rights):
     tall, width = left.shape[0], rights[0].shape[1]
     tile = 384
     return pl.pallas_call(
         outer_kernel,
-        grid=(tall // tile,),
-        in_specs=[pl.BlockSpec((tile, 2 * ROWS), lambda i: (i, 0))]
-        + [whole(HALF, width) for _ in rights],
-        out_specs=pl.BlockSpec((tile, width), lambda i: (i, 0)),
-        out_shape=shape((tall, width), bf16),
+        grid_spec=pltpu.PrefetchScalarGridSpec(
+            num_scalar_prefetch=1,
+            grid=(tall // tile,),
+            in_specs=[pl.BlockSpec((tile, 2 * ROWS), lambda i, *_: (i, 0))]
+            + [whole(HALF, width) for _ in rights],
+            out_specs=[pl.BlockSpec((tile, QW), lambda i, *_: (i, 0))] * 2,
+        ),
+        out_shape=[shape((tall, QW), bf16)] * 2,
         compiler_params=params(),
         cost_estimate=cost(1),
         name="weight_grad",
-    )(left, *rights)
+    )(place, left, *rights)
 
 
 def run_pieces(place, left, right, chips, weights, columns, others=()):
@@ -697,7 +703,7 @@
     if others:
         part = others[1].shape
         beside_specs = [
-            pl.BlockSpec(part, lambda i, place: (0, 0, 0, place[1])),
+            whole(*part),
             whole(*part),
         ]
     return pl.pallas_call(
@@ -1090,14 +1096,14 @@
     )
 
     layer_far = other_core(layer_b)
-    out_grad = run_outer(shaped_turned, cots)
+    out_grad, out_send = run_outer(place, shaped_turned, cots)
     layer_far, out_grad = tie(layer_far, out_grad)
     layer_send = (layer_a[HALF:].astype(f32) + layer_far[HALF:].astype(f32)).astype(bf16)
     layer_side = other_side(layer_send)
 
     split = (chips // 2, 2, chip_rows)
-    out_far = other_core(columns_of(out_grad, 1 - core)).reshape(*split, QW)
-    out_pieces = (out_grad.reshape(*split, D), out_far)
+    out_far = other_core(out_send).reshape(*split, QW)
+    out_pieces = (out_grad.reshape(*split, QW), out_far)
     both_pieces, gate_dots = run_pieces(
         place, normed_turned, after(gate_grad, layer_send), chips, w_gate, (0, 1), out_pieces
     )

time: 446 us -> 446 us (level)
  no operation moved by 1% of the time
where the time goes in v2:
time: 446 us; the launch traced here: 437 us
  Pallas kernels  236 us (53%)
  waiting for transfers between devices  72.8 us (16%)
  starting transfers between devices  52 us (12%)
  other arithmetic  45 us (10%)
  local copies, waits for them, and re-layouts  29.8 us (7%)
    pallas_call x4, Pallas kernels, run_backward(): pl.pallas_call(backward_kernel, grid_spec=pltpu.PrefetchScalarGridSpec(nu...  62.9 us
    pallas_call x4, Pallas kernels, run_forward(): pl.pallas_call(functools.partial(forward_kernel, part % 2), grid_spec=plt...  49.5 us
    pallas_call x4, Pallas kernels, run_input_grad(): pl.pallas_call(input_grad_kernel, grid_spec=pltpu.PrefetchScalarGridSpec(...  33.3 us
    ppermute x40, waiting for transfers between devices, flip(): return lax.ppermute(block, 'dp', [(d, d ^ bit) for d in range(count)])  28.1 us
    pallas_call x2, Pallas kernels, run_pieces(): pl.pallas_call(functools.partial(pieces_kernel, chip_rows, len(columns)),...  27.5 us
    ppermute x40, starting transfers between devices, flip(): return lax.ppermute(block, 'dp', [(d, d ^ bit) for d in range(count)])  24.3 us
    ppermute x12, waiting for transfers between devices, along(): lax.ppermute(block, 'dp', [(d, (d + 4) % count) for d in range(count)])  22.7 us
    ppermute x14, waiting for transfers between devices, other_side(): return lax.ppermute(block, 'seq', [(0, 1), (1, 0)])  22 us
  transfers between devices with their start and end apart: 66, of which 20 were waited for; matrix products, arithmetic and copies ran while one was open for 13% of the time, Pallas kernels for 40%

profile of v2, /device:TPU:0, one launch (start us, length us, event | category | flops | bytes accessed | tf_op | source)
XLA Modules:
  0.0 437.5 jit_solution(8175381089283127695)
XLA Ops:
  2.4 3.0 collective-permute-start.1
  10.4 1.8 collective-permute-start.2
  12.4 3.3 collective-permute-done.2
  15.8 1.9 collective-permute-start.8
  17.8 1.6 collective-permute-start.17
  19.7 1.6 collective-permute-start.4
  21.3 6.8 %collective-permute-done.8 = bf16[2,96,1152]{2,1,0:T(8,128)(2,1)S(1)} collective-permute-done((bf16[2,96,1152]{2,1,0:T(8,128)(2,1)S(1)}, bf16[2,96,1152]{2,1,0:T(8,128)(2,1)S(1)}, u32[]{:S(2)}, u32[]{:S(2)}) %collective-permute-start.8) | collective-permute-done | bytes 442400 | tf_op jit(solution)/shard_map/ppermute | solution.py:811
  29.0 1.5 collective-permute-start.18
  31.9 9.7 %collective-permute-done.10 = bf16[2,2,768]{2,1,0:T(2,128)(2,1)S(1)} collective-permute-done((bf16[2,2,768]{2,1,0:T(2,128)(2,1)S(1)}, bf16[2,2,768]{2,1,0:T(2,128)(2,1)S(1)}, u32[]{:S(2)}, u32[]{:S(2)}) %collective-permute-start.10) | collective-permute-done | bytes 6176 | tf_op jit(solution)/shard_map/ppermute | solution.py:798
  41.8 3.6 collective-permute-done.11
  46.5 1.5 collective-permute-start.19
  50.6 10.2 %collective-permute-done.14 = bf16[2,96,1152]{2,1,0:T(8,128)(2,1)} collective-permute-done((bf16[2,96,1152]{2,1,0:T(8,128)(2,1)}, bf16[2,96,1152]{2,1,0:T(8,128)(2,1)}, u32[]{:S(2)}, u32[]{:S(2)}) %collective-permute-start.14) | collective-permute-done | bytes 442400 | tf_op jit(solution)/shard_map/ppermute | solution.py:811
  62.1 1.6 reshape.274
  63.8 1.6 copy.72
  65.3 1.6 reshape.265
  67.7 1.5 reshape.264
  74.6 1.5 collective-permute-start.27
  76.1 4.4 %collective-permute-done.20 = bf16[2,96,1152]{2,1,0:T(8,128)(2,1)S(1)} collective-permute-done((bf16[2,96,1152]{2,1,0:T(8,128)(2,1)}, bf16[2,96,1152]{2,1,0:T(8,128)(2,1)S(1)}, u32[]{:S(2)}, u32[]{:S(2)}) %collective-permute-start.20) | collective-permute-done | bytes 442400 | tf_op jit(solution)/shard_map/ppermute | solution.py:798
  83.1 12.4 %forward_scan.4 = (bf16[2048,1536]{1,0:T(8,128)(2,1)}, bf16[1536,2048]{1,0:T(8,128)(2,1)}, f32[2048,1152]{1,0:T(8,128)}, f32[2048,1152]{1,0:T(8,128)}, f32[2048,...) custom-call(s32[4]{0:T(128)} %pad_add_fusion.place, bf16[512,1536]{1,0:T(8,128)(2,1)} %tok.1, ...), custom_call_target="tpu_custom_call" | custom-call | flops 12999999488 | bytes 45500000 | tf_op jit(solution)/shard_map/forward_scan/pallas_call | solution.py:514
  97.8 12.5 %forward_scan.5 = (bf16[2048,1536]{1,0:T(8,128)(2,1)}, bf16[1536,2048]{1,0:T(8,128)(2,1)}, f32[2048,1152]{1,0:T(8,128)}, f32[2048,1152]{1,0:T(8,128)}, f32[2048,...) custom-call(s32[4]{0:T(128)} %pad_add_fusion.place, ...), custom_call_target="tpu_custom_call", output_to_operand_aliasing={{0}: (10, {}), {1}: (11, {}), {2}: (12, {}), {3}: (13, {}),... | custom-call | flops 12999999488 | bytes 45500000 | tf_op jit(solution)/shard_map/forward_scan/pallas_call | solution.py:514
  110.4 1.5 collective-permute-start.25
  112.2 12.3 %forward_scan.6 = (bf16[2048,1536]{1,0:T(8,128)(2,1)}, bf16[1536,2048]{1,0:T(8,128)(2,1)}, f32[2048,1152]{1,0:T(8,128)}, f32[2048,1152]{1,0:T(8,128)}, f32[2048,...) custom-call(s32[4]{0:T(128)} %pad_add_fusion.place, ...), custom_call_target="tpu_custom_call", output_to_operand_aliasing={{0}: (10, {}), {1}: (11, {}), {2}: (12, {}), {3}: (13, {}),... | custom-call | flops 12999999488 | bytes 45500000 | tf_op jit(solution)/shard_map/forward_scan/pallas_call | solution.py:514
  124.5 1.9 collective-permute-done.25.refs_5_
  126.5 2.9 collective-permute-done.23.refs_6_
  130.0 12.3 %forward_scan.7 = (bf16[2048,1536]{1,0:T(8,128)(2,1)}, bf16[1536,2048]{1,0:T(8,128)(2,1)}, f32[2048,1152]{1,0:T(8,128)}, f32[2048,1152]{1,0:T(8,128)}, f32[2048,...) custom-call(s32[4]{0:T(128)} %pad_add_fusion.place, ...), custom_call_target="tpu_custom_call", output_to_operand_aliasing={{0}: (10, {}), {1}: (11, {}), {2}: (12, {}), {3}: (13, {}),... | custom-call | flops 12999999488 | bytes 45500000 | tf_op jit(solution)/shard_map/forward_scan/pallas_call | solution.py:514
  142.3 1.9 collective-permute-done.26.refs_7_
  144.3 5.9 %assemble.1 = (bf16[2,8,96,768]{3,2,1,0:T(8,128)(2,1)}, bf16[4,2,96,768]{3,2,1,0:T(8,128)(2,1)}, bf16[4,2,96,768]{3,2,1,0:T(8,128)(2,1)}) custom-call(s32[12]{0:T(128)} %concatenate.191.place, bf16[2,2,96,768]{3,2,1,0:T(8,128)(2,1)} %pad_maximum_fusion.1.refs_0_, bf16[2,2,96,768]{3,2,1,0:T(8,128)(2,1)} %collective-permute-done.22.refs_1_, ...), custom_call_target="tpu_custom_call" | custom-call | flops 3000000000 | bytes 10500000 | tf_op jit(solution)/shard_map/assemble/pallas_call | solution.py:565
  150.8 2.6 collective-permute-done.30
  153.4 18.7 %gate_and_stats.1 = (f32[2048,768]{1,0:T(8,128)}, f32[2048,768]{1,0:T(8,128)}, f32[8,2048]{1,0:T(8,128)}) custom-call(s32[4]{0:T(128)} %pad_add_fusion.place, bf16[2048,1536]{1,0:T(8,128)(2,1)} %get-tuple-element.201.normed, bf16[1536,768]{1,0:T(8,128)(2,1)} %bitcast.158, bf16[512,1536]{1,0:T(8,128)(2,1)} %cot.1, ...), custom_call_target="tpu_custom_call" | custom-call | flops 2000000000 | bytes 7000000 | tf_op jit(solution)/shard_map/gate_and_stats/pallas_call | solution.py:590
  173.3 3.2 collective-permute-done.31
  179.4 21.1 %finish.1 = (bf16[768,2048]{1,0:T(8,128)(2,1)}, bf16[1024,1536]{1,0:T(8,128)(2,1)}, bf16[1024,1536]{1,0:T(8,128)(2,1)}, f32[2048,768]{1,0:T(8,128)}, bf16[2048,768]{1,0:T(8,128)(2,1)}, /*index=5*/f32[8,768]{1,0:T(8,128)}) custom-call(s32[4]{0:T(128)} %pad_add_fusion.place, f32[8,2048]{1,0:T(8,128)} %maximum_add_fusion.stats, ...), custom_call_target="tpu_custom_call" | custom-call | flops 2000000000 | bytes 7000000 | tf_op jit(solution)/shard_map/finish/pallas_call | solution.py:613
  200.7 10.5 %weight_grad.3 = (bf16[768,768]{1,0:T(8,128)(2,1)}, bf16[768,768]{1,0:T(8,128)(2,1)}) custom-call(s32[4]{0:T(128)} %pad_add_fusion.place, bf16[768,2048]{1,0:T(8,128)(2,1)} %get-tuple-element.216.left, bf16[512,1536]{1,0:T(8,128)(2,1)} %cot.1, bf16[512,1536]{1,0:T(8,128)(2,1)} %collective-permute-done.27.cot_fa.rest_1_, bf16[512,1536]{1,0:T(8,128)(2,1)} %copy-done.2, ...), custom_call_target="tpu_custom_call" | custom-call | flops 1000000000 | bytes 3500000 | tf_op jit(solution)/shard_map/weight_grad/pallas_call | solution.py:677
  211.6 2.9 add_convert_fusion.1
  214.5 12.2 %weight_grad.4 = (bf16[8,2,2,96,768]{4,3,2,1,0:T(8,128)(2,1)}, f32[8,1536]{1,0:T(8,128)}) custom-call(s32[4]{0:T(128)} %pad_add_fusion.place, bf16[1536,2048]{1,0:T(8,128)(2,1)} %get-tuple-element.213.left, bf16[2048,768]{1,0:T(8,128)(2,1)} %get-tuple-element.219.right.refs_0_, bf16[1536,768]{1,0:T(8,128)(2,1)} %bitcast.159, bf16[1536,768]{1,0:T(8,128)(2,1)} %bitcast.160, ...), custom_call_target="tpu_custom_call" | custom-call | flops 1000000000 | bytes 3500000 | tf_op jit(solution)/shard_map/weight_grad/pallas_call | solution.py:709
  226.7 3.2 dynamic-slice_bitcast_fusion
  231.7 16.0 %backward_scan.4 = (bf16[2048,1152]{1,0:T(8,128)(2,1)}, f32[8,1024]{1,0:T(8,128)}, f32[8,128]{1,0:T(8,128)}, f32[8,768]{1,0:T(8,128)}, f32[8,1024]{1,0:T(8,128)}, /*index=5*/f32[128,768]{1,0:T(8,128)}) custom-call(s32[4]{0:T(128)} %pad_add_fusion.place, f32[2048,1152]{1,0:T(8,128)} %get-tuple-element.223.proj_in, ...), custom_call_target="tpu_custom_call" | custom-call | flops 2000000000 | bytes 7000000 | tf_op jit(solution)/shard_map/backward_scan/pallas_call | solution.py:647
  247.7 2.2 fusion.1
  249.9 1.4 collective-permute-start.36
  251.3 15.6 %backward_scan.5 = (bf16[2048,1152]{1,0:T(8,128)(2,1)}, f32[8,1024]{1,0:T(8,128)}, f32[8,128]{1,0:T(8,128)}, f32[8,768]{1,0:T(8,128)}, f32[8,1024]{1,0:T(8,128)}, /*index=5*/f32[128,768]{1,0:T(8,128)}) custom-call(s32[4]{0:T(128)} %pad_add_fusion.place, f32[2048,1152]{1,0:T(8,128)} %get-tuple-element.223.proj_in, ...), custom_call_target="tpu_custom_call", output_to_operand_aliasing={{0}: (11, {})} | custom-call | flops 2000000000 | bytes 7000000 | tf_op jit(solution)/shard_map/backward_scan/pallas_call | solution.py:647
  268.1 2.4 fusion.3
  273.0 15.7 %backward_scan.6 = (bf16[2048,1152]{1,0:T(8,128)(2,1)}, f32[8,1024]{1,0:T(8,128)}, f32[8,128]{1,0:T(8,128)}, f32[8,768]{1,0:T(8,128)}, f32[8,1024]{1,0:T(8,128)}, /*index=5*/f32[128,768]{1,0:T(8,128)}) custom-call(s32[4]{0:T(128)} %pad_add_fusion.place, f32[2048,1152]{1,0:T(8,128)} %get-tuple-element.223.proj_in, ...), custom_call_target="tpu_custom_call", output_to_operand_aliasing={{0}: (11, {})} | custom-call | flops 2000000000 | bytes 7000000 | tf_op jit(solution)/shard_map/backward_scan/pallas_call | solution.py:647
  288.7 1.6 fusion.5
  292.1 15.7 %backward_scan.7 = (bf16[2048,1152]{1,0:T(8,128)(2,1)}, f32[8,1024]{1,0:T(8,128)}, f32[8,128]{1,0:T(8,128)}, f32[8,768]{1,0:T(8,128)}, f32[8,1024]{1,0:T(8,128)}, /*index=5*/f32[128,768]{1,0:T(8,128)}) custom-call(s32[4]{0:T(128)} %pad_add_fusion.place, f32[2048,1152]{1,0:T(8,128)} %get-tuple-element.223.proj_in, ...), custom_call_target="tpu_custom_call", output_to_operand_aliasing={{0}: (11, {})} | custom-call | flops 2000000000 | bytes 7000000 | tf_op jit(solution)/shard_map/backward_scan/pallas_call | solution.py:647
  312.8 15.3 %weight_grad.5 = (bf16[8,2,96,1152]{3,2,1,0:T(8,128)(2,1)}, f32[8,1536]{1,0:T(8,128)}) custom-call(s32[4]{0:T(128)} %pad_add_fusion.place, bf16[1536,2048]{1,0:T(8,128)(2,1)} %get-tuple-element.213.left, bf16[2048,1152]{1,0:T(8,128)(2,1)} %get-tuple-element.281.right.refs_1_, bf16[1536,1152]{1,0:T(8,128)(2,1)} %bitcast.151, bf16[1536,1152]{1,0:T(8,128)(2,1)} %bitcast.152, ...), custom_call_target="tpu_custom_call" | custom-call | flops 1000000000 | bytes 3500000 | tf_op jit(solution)/shard_map/weight_grad/pallas_call | solution.py:709
  328.1 2.5 dynamic-slice_bitcast_fusion.4
  332.2 8.3 %input_grad.4 = bf16[512,1536]{1,0:T(8,128)(2,1)} custom-call(s32[4]{0:T(128)} %pad_add_fusion.place, bf16[2048,768]{1,0:T(8,128)(2,1)} %get-tuple-element.219.right.refs_0_, bf16[2048,1152]{1,0:T(8,128)(2,1)} %get-tuple-element.281.right.refs_1_, bf16[1536,768]{1,0:T(8,128)(2,1)} %bitcast.161, bf16[1536,1152]{1,0:T(8,128)(2,1)} %bitcast.154), custom_call_target="tpu_custom_call" | custom-call | flops 1000000000 | bytes 3500000 | tf_op jit(solution)/shard_map/input_grad/pallas_call | solution.py:769
  341.1 1.5 collective-permute-start.48
  342.6 2.8 collective-permute-done.43
  346.6 8.4 %input_grad.5 = bf16[512,1536]{1,0:T(8,128)(2,1)} custom-call(s32[4]{0:T(128)} %pad_add_fusion.place, bf16[2048,768]{1,0:T(8,128)(2,1)} %get-tuple-element.219.right.refs_0_, bf16[2048,1152]{1,0:T(8,128)(2,1)} %get-tuple-element.281.right.refs_1_, bf16[1536,768]{1,0:T(8,128)(2,1)} %bitcast.162, bf16[1536,1152]{1,0:T(8,128)(2,1)} %bitcast.155), custom_call_target="tpu_custom_call" | custom-call | flops 1000000000 | bytes 3500000 | tf_op jit(solution)/shard_map/input_grad/pallas_call | solution.py:769
  355.0 1.5 add.599
  356.6 1.9 fusion.10
  358.4 3.4 collective-permute-start.53
  362.5 2.3 add_convert_fusion
  367.9 8.3 %input_grad.6 = bf16[512,1536]{1,0:T(8,128)(2,1)} custom-call(s32[4]{0:T(128)} %pad_add_fusion.place, bf16[2048,768]{1,0:T(8,128)(2,1)} %get-tuple-element.219.right.refs_0_, bf16[2048,1152]{1,0:T(8,128)(2,1)} %get-tuple-element.281.right.refs_1_, bf16[1536,768]{1,0:T(8,128)(2,1)} %bitcast.163, bf16[1536,1152]{1,0:T(8,128)(2,1)} %bitcast.156), custom_call_target="tpu_custom_call" | custom-call | flops 1000000000 | bytes 3500000 | tf_op jit(solution)/shard_map/input_grad/pallas_call | solution.py:769
  376.9 2.1 fusion.12
  383.6 8.3 %input_grad.7.near = bf16[512,1536]{1,0:T(8,128)(2,1)} custom-call(s32[4]{0:T(128)} %pad_add_fusion.place, bf16[2048,768]{1,0:T(8,128)(2,1)} %get-tuple-element.219.right.refs_0_, bf16[2048,1152]{1,0:T(8,128)(2,1)} %get-tuple-element.281.right.refs_1_, bf16[1536,768]{1,0:T(8,128)(2,1)} %bitcast.164, bf16[1536,1152]{1,0:T(8,128)(2,1)} %bitcast.157), custom_call_target="tpu_custom_call" | custom-call | flops 1000000000 | bytes 3500000 | tf_op jit(solution)/shard_map/input_grad/pallas_call | solution.py:769
  391.9 2.0 collective-permute-done.55.rest_1_
  396.8 5.3 %convert_add_fusion = f32[512,1536]{1,0:T(8,128)} fusion(bf16[512,1536]{1,0:T(8,128)(2,1)} %copy-done.7, bf16[512,1536]{1,0:T(8,128)(2,1)} %tok.1, bf16[1024,1536]{1,0:T(8,128)(2,1)} %collective-permute-done.33, bf16[1024,1536]{1,0:T(8,128)(2,1)} %get-tuple-element.214), kind=kLoop, calls=%fused_computation | loop fusion | flops 5505024 | bytes 9437184 | tf_op jit(solution)/shard_map/add | solution.py:1199
  402.0 2.5 collective-permute-done.57
  404.6 1.5 collective-permute-done.58
  410.5 3.2 multiply_subtract_fusion.1
  413.9 8.8 %collective-permute-done.60 = bf16[48,1920]{1,0:T(8,128)(2,1)S(1)} collective-permute-done((bf16[48,1920]{1,0:T(8,128)(2,1)S(1)}, bf16[48,1920]{1,0:T(8,128)(2,1)S(1)}, u32[]{:S(2)}, u32[]{:S(2)}) %collective-permute-start.60) | collective-permute-done | bytes 184352 | tf_op jit(solution)/shard_map/ppermute | solution.py:785
  424.0 2.5 multiply_subtract_fusion
  428.5 6.6 %tokens_grad.1 = f32[512,1536]{1,0:T(8,128)} custom-call(bf16[512,1536]{1,0:T(8,128)(2,1)} %tok.1, bf16[512,1536]{1,0:T(8,128)(2,1)} %cot.1, f32[1,1536]{1,0:T(1,128)} %slice.165.gain, bf16[512,1536]{1,0:T(8,128)(2,1)} %input_grad.7.near, bf16[512,1536]{1,0:T(8,128)(2,1)} %copy-done.34, bf16[128,1536]{1,0:T(8,128)(2,1)} %collective-permute-done.50.rest_0_, ...), custom_call_target="tpu_custom_call" | custom-call | flops 4000000000 | bytes 14000000 | tf_op jit(solution)/shard_map/tokens_grad/pallas_call | solution.py:746
  (289 shorter events, 68.9 us)
Async XLA Ops:
  2.4 7.8 %collective-permute-start.1 = (bf16[48,1920]{1,0:T(8,128)(2,1)S(1)}, bf16[48,1920]{1,0:T(8,128)(2,1)S(1)}, u32[]{:S(2)}, u32[]{:S(2)}) collective-permute-start(bf16[48,1920]{1,0:T(8,128)(2,1)S(1)} %get-tuple-element.354), channel_id=1, source_target_pairs={{0,16},{16,0},{1,17},{17,1},{2,18},{18,2},{3,19},{19,3},{4,20},{20... | collective-permute-start | bytes 552968 | tf_op jit(solution)/shard_map/ppermute | solution.py:785
  5.6 4.5 %collective-permute-start.6 = (bf16[1,1,768]{2,1,0:T(2,128)(2,1)S(1)}, bf16[1,1,768]{2,1,0:T(2,128)(2,1)S(1)}, u32[]{:S(2)}, u32[]{:S(2)}) collective-permute-start(bf16[1,1,768]{2,1,0:T(2,128)(2,1)S(1)} %concatenate.170), channel_id=1, source_target_pairs={{0,16},{16,0},{1,17},{17,1},{2,18},{18,2},{3,19},{19,3},{4,20},{20... | collective-permute-start | bytes 4616 | tf_op jit(solution)/shard_map/ppermute | solution.py:785
  5.7 4.4 %collective-permute-start.15 = (bf16[96,768]{1,0:T(8,128)(2,1)S(1)}, bf16[96,768]{1,0:T(8,128)(2,1)S(1)}, u32[]{:S(2)}, u32[]{:S(2)}) collective-permute-start(bf16[96,768]{1,0:T(8,128)(2,1)S(1)} %get-tuple-element.346), channel_id=1, source_target_pairs={{0,1},{1,0},{2,3},{3,2},{4,5},{5,4},{6,7},{7,6},{8,9},{9,8},{10,11... | collective-permute-start | bytes 442376 | tf_op jit(solution)/shard_map/ppermute | solution.py:798
  5.8 106.1 %collective-permute-start = (bf16[512,1536]{1,0:T(8,128)(2,1)}, bf16[512,1536]{1,0:T(8,128)(2,1)}, u32[]{:S(2)}, u32[]{:S(2)}) collective-permute-start(bf16[512,1536]{1,0:T(8,128)(2,1)} %tok.1), channel_id=1, source_target_pairs={{0,1},{1,0},{2,3},{3,2},{4,5},{5,4},{6,7},{7,6},{8,9},{9,8},{10,11... | collective-permute-start | bytes 4718600 | tf_op jit(solution)/shard_map/ppermute | solution.py:798
  10.4 5.2 %collective-permute-start.2 = (bf16[48,1536]{1,0:T(8,128)(2,1)S(1)}, bf16[48,1536]{1,0:T(8,128)(2,1)S(1)}, u32[]{:S(2)}, u32[]{:S(2)}) collective-permute-start(bf16[48,1536]{1,0:T(8,128)(2,1)S(1)} %get-tuple-element.329), channel_id=1, source_target_pairs={{0,16},{16,0},{1,17},{17,1},{2,18},{18,2},{3,19},{19,3},{4,20},{20... | collective-permute-start | bytes 442376 | tf_op jit(solution)/shard_map/ppermute | solution.py:785
  12.3 3.4 collective-permute-start.7
  15.8 12.3 %collective-permute-start.8 = (bf16[2,96,1152]{2,1,0:T(8,128)(2,1)S(1)}, bf16[2,96,1152]{2,1,0:T(8,128)(2,1)S(1)}, u32[]{:S(2)}, u32[]{:S(2)}) collective-permute-start(bf16[2,96,1152]{2,1,0:T(8,128)(2,1)S(1)} %bitcast.167), channel_id=1, source_target_pairs={{0,4},{1,5},{2,6},{3,7},{4,8},{5,9},{6,10},{7,11},{8,12},{9,13},{1... | collective-permute-start | bytes 1327112 | tf_op jit(solution)/shard_map/ppermute | solution.py:811
  17.7 2.0 collective-permute-start.3
  17.8 12.7 %collective-permute-start.17 = (bf16[2,96,1152]{2,1,0:T(8,128)(2,1)S(1)}, bf16[2,96,1152]{2,1,0:T(8,128)(2,1)S(1)}, u32[]{:S(2)}, u32[]{:S(2)}) collective-permute-start(bf16[2,96,1152]{2,1,0:T(8,128)(2,1)S(1)} %bitcast.168), channel_id=1, source_target_pairs={{0,2},{1,3},{2,0},{3,1},{4,6},{5,7},{6,4},{7,5},{8,10},{9,11},{10,... | collective-permute-start | bytes 1327112 | tf_op jit(solution)/shard_map/ppermute | solution.py:798
  19.7 54.8 %collective-permute-start.4 = (bf16[512,1536]{1,0:T(8,128)(2,1)}, bf16[512,1536]{1,0:T(8,128)(2,1)}, u32[]{:S(2)}, u32[]{:S(2)}) collective-permute-start(bf16[512,1536]{1,0:T(8,128)(2,1)} %tok.1), channel_id=1, source_target_pairs={{0,16},{16,0},{1,17},{17,1},{2,18},{18,2},{3,19},{19,3},{4,20},{20... | collective-permute-start | bytes 4718600 | tf_op jit(solution)/shard_map/ppermute | solution.py:785
  28.1 2.4 collective-permute-start.9
  29.0 19.0 %collective-permute-start.18 = (bf16[2,96,1152]{2,1,0:T(8,128)(2,1)S(1)}, bf16[2,96,1152]{2,1,0:T(8,128)(2,1)S(1)}, u32[]{:S(2)}, u32[]{:S(2)}) collective-permute-start(bf16[2,96,1152]{2,1,0:T(8,128)(2,1)S(1)} %collective-permute-done.8), channel_id=1, source_target_pairs={{0,2},{1,3},{2,0},{3,1},{4,6},{5,7},{6,4},{7,5},{8,10},{9,11},{10,... | collective-permute-start | bytes 1327112 | tf_op jit(solution)/shard_map/ppermute | solution.py:798
  30.5 15.0 %collective-permute-start.12 = (bf16[2,96,1152]{2,1,0:T(8,128)(2,1)S(1)}, bf16[2,96,1152]{2,1,0:T(8,128)(2,1)}, u32[]{:S(2)}, u32[]{:S(2)}) collective-permute-start(bf16[2,96,1152]{2,1,0:T(8,128)(2,1)S(1)} %collective-permute-done.8), channel_id=1, source_target_pairs={{0,4},{1,5},{2,6},{3,7},{4,8},{5,9},{6,10},{7,11},{8,12},{9,13},{1... | collective-permute-start | bytes 1327112 | tf_op jit(solution)/shard_map/ppermute | solution.py:811
  30.5 11.1 %collective-permute-start.10 = (bf16[2,2,768]{2,1,0:T(2,128)(2,1)S(1)}, bf16[2,2,768]{2,1,0:T(2,128)(2,1)S(1)}, u32[]{:S(2)}, u32[]{:S(2)}) collective-permute-start(bf16[2,2,768]{2,1,0:T(2,128)(2,1)S(1)} %broadcast_select_fusion.1), channel_id=1, source_target_pairs={{0,2},{1,3},{2,0},{3,1},{4,6},{5,7},{6,4},{7,5},{8,10},{9,11},{10,... | collective-permute-start | bytes 18440 | tf_op jit(solution)/shard_map/ppermute | solution.py:798
  41.7 3.8 collective-permute-start.11
  45.5 5.0 %collective-permute-start.13 = (bf16[2,8,768]{2,1,0:T(8,128)(2,1)S(1)}, bf16[2,8,768]{2,1,0:T(8,128)(2,1)S(1)}, u32[]{:S(2)}, u32[]{:S(2)}) collective-permute-start(bf16[2,8,768]{2,1,0:T(8,128)(2,1)S(1)} %maximum_select_fusion.11), channel_id=1, source_target_pairs={{0,8},{1,9},{2,10},{3,11},{4,12},{5,13},{6,14},{7,15},{8,0},{9,1},... | collective-permute-start | bytes 73736 | tf_op jit(solution)/shard_map/ppermute | solution.py:798
  46.5 25.9 %collective-permute-start.19 = (bf16[2,96,1152]{2,1,0:T(8,128)(2,1)}, bf16[2,96,1152]{2,1,0:T(8,128)(2,1)}, u32[]{:S(2)}, u32[]{:S(2)}) collective-permute-start(bf16[2,96,1152]{2,1,0:T(8,128)(2,1)} %collective-permute-done.12), channel_id=1, source_target_pairs={{0,2},{1,3},{2,0},{3,1},{4,6},{5,7},{6,4},{7,5},{8,10},{9,11},{10,... | collective-permute-start | bytes 1327112 | tf_op jit(solution)/shard_map/ppermute | solution.py:798
  48.0 12.8 %collective-permute-start.14 = (bf16[2,96,1152]{2,1,0:T(8,128)(2,1)}, bf16[2,96,1152]{2,1,0:T(8,128)(2,1)}, u32[]{:S(2)}, u32[]{:S(2)}) collective-permute-start(bf16[2,96,1152]{2,1,0:T(8,128)(2,1)} %collective-permute-done.12), channel_id=1, source_target_pairs={{0,4},{1,5},{2,6},{3,7},{4,8},{5,9},{6,10},{7,11},{8,12},{9,13},{1... | collective-permute-start | bytes 1327112 | tf_op jit(solution)/shard_map/ppermute | solution.py:811
  70.4 25.1 %collective-permute-start.16 = (bf16[2,2,96,768]{3,2,1,0:T(8,128)(2,1)}, bf16[2,2,96,768]{3,2,1,0:T(8,128)(2,1)}, u32[]{:S(2)}, u32[]{:S(2)}) collective-permute-start(bf16[2,2,96,768]{3,2,1,0:T(8,128)(2,1)} %pad_maximum_fusion.1.refs_0_), channel_id=1, source_target_pairs={{0,4},{1,5},{2,6},{3,7},{4,8},{5,9},{6,10},{7,11},{8,12},{9,13},{1... | collective-permute-start | bytes 1769480 | tf_op jit(solution)/shard_map/ppermute | solution.py:811
  70.4 10.1 %collective-permute-start.20 = (bf16[2,96,1152]{2,1,0:T(8,128)(2,1)}, bf16[2,96,1152]{2,1,0:T(8,128)(2,1)S(1)}, u32[]{:S(2)}, u32[]{:S(2)}) collective-permute-start(bf16[2,96,1152]{2,1,0:T(8,128)(2,1)} %collective-permute-done.14), channel_id=1, source_target_pairs={{0,2},{1,3},{2,0},{3,1},{4,6},{5,7},{6,4},{7,5},{8,10},{9,11},{10,... | collective-permute-start | bytes 1327112 | tf_op jit(solution)/shard_map/ppermute | solution.py:798
  74.5 37.7 %collective-permute-start.5 = (bf16[512,1536]{1,0:T(8,128)(2,1)}, bf16[512,1536]{1,0:T(8,128)(2,1)}, u32[]{:S(2)}, u32[]{:S(2)}) collective-permute-start(bf16[512,1536]{1,0:T(8,128)(2,1)} %collective-permute-done.4.far), channel_id=1, source_target_pairs={{0,1},{1,0},{2,3},{3,2},{4,5},{5,4},{6,7},{7,6},{8,9},{9,8},{10,11... | collective-permute-start | bytes 4718600 | tf_op jit(solution)/shard_map/ppermute | solution.py:798
  74.6 55.4 %collective-permute-start.27 = (bf16[512,1536]{1,0:T(8,128)(2,1)}, bf16[512,1536]{1,0:T(8,128)(2,1)}, u32[]{:S(2)}, u32[]{:S(2)}) collective-permute-start(bf16[512,1536]{1,0:T(8,128)(2,1)} %cot.1), channel_id=1, source_target_pairs={{0,16},{16,0},{1,17},{17,1},{2,18},{18,2},{3,19},{19,3},{4,20},{20... | collective-permute-start | bytes 4718600 | tf_op jit(solution)/shard_map/ppermute | solution.py:785
  80.6 16.0 %collective-permute-start.22 = (bf16[2,2,96,768]{3,2,1,0:T(8,128)(2,1)}, bf16[2,2,96,768]{3,2,1,0:T(8,128)(2,1)}, u32[]{:S(2)}, u32[]{:S(2)}) collective-permute-start(bf16[2,2,96,768]{3,2,1,0:T(8,128)(2,1)} %pad_maximum_fusion.1.refs_0_), channel_id=1, source_target_pairs={{0,2},{1,3},{2,0},{3,1},{4,6},{5,7},{6,4},{7,5},{8,10},{9,11},{10,... | collective-permute-start | bytes 1769480 | tf_op jit(solution)/shard_map/ppermute | solution.py:798
  95.5 14.8 %collective-permute-start.24 = (bf16[2,2,96,768]{3,2,1,0:T(8,128)(2,1)}, bf16[2,2,96,768]{3,2,1,0:T(8,128)(2,1)}, u32[]{:S(2)}, u32[]{:S(2)}) collective-permute-start(bf16[2,2,96,768]{3,2,1,0:T(8,128)(2,1)} %collective-permute-done.16.refs_2_), channel_id=1, source_target_pairs={{0,2},{1,3},{2,0},{3,1},{4,6},{5,7},{6,4},{7,5},{8,10},{9,11},{10,... | collective-permute-start | bytes 1769480 | tf_op jit(solution)/shard_map/ppermute | solution.py:798
  96.5 13.9 %collective-permute-start.21 = (bf16[2,2,96,768]{3,2,1,0:T(8,128)(2,1)}, bf16[2,2,96,768]{3,2,1,0:T(8,128)(2,1)}, u32[]{:S(2)}, u32[]{:S(2)}) collective-permute-start(bf16[2,2,96,768]{3,2,1,0:T(8,128)(2,1)} %collective-permute-done.16.refs_2_), channel_id=1, source_target_pairs={{0,4},{1,5},{2,6},{3,7},{4,8},{5,9},{6,10},{7,11},{8,12},{9,13},{1... | collective-permute-start | bytes 1769480 | tf_op jit(solution)/shard_map/ppermute | solution.py:811
  110.3 40.5 %collective-permute-start.28 = (bf16[512,1536]{1,0:T(8,128)(2,1)S(1)}, bf16[512,1536]{1,0:T(8,128)(2,1)S(1)}, u32[]{:S(2)}, u32[]{:S(2)}) collective-permute-start(bf16[512,1536]{1,0:T(8,128)(2,1)S(1)} %copy-done.1), channel_id=1, source_target_pairs={{0,1},{1,0},{2,3},{3,2},{4,5},{5,4},{6,7},{7,6},{8,9},{9,8},{10,11... | collective-permute-start | bytes 4718600 | tf_op jit(solution)/shard_map/ppermute | solution.py:798
  110.4 16.1 %collective-permute-start.25 = (bf16[2,2,96,768]{3,2,1,0:T(8,128)(2,1)}, bf16[2,2,96,768]{3,2,1,0:T(8,128)(2,1)}, u32[]{:S(2)}, u32[]{:S(2)}) collective-permute-start(bf16[2,2,96,768]{3,2,1,0:T(8,128)(2,1)} %collective-permute-done.21.refs_4_), channel_id=1, source_target_pairs={{0,2},{1,3},{2,0},{3,1},{4,6},{5,7},{6,4},{7,5},{8,10},{9,11},{10,... | collective-permute-start | bytes 1769480 | tf_op jit(solution)/shard_map/ppermute | solution.py:798
  111.9 17.5 %collective-permute-start.23 = (bf16[2,2,96,768]{3,2,1,0:T(8,128)(2,1)}, bf16[2,2,96,768]{3,2,1,0:T(8,128)(2,1)}, u32[]{:S(2)}, u32[]{:S(2)}) collective-permute-start(bf16[2,2,96,768]{3,2,1,0:T(8,128)(2,1)} %collective-permute-done.21.refs_4_), channel_id=1, source_target_pairs={{0,4},{1,5},{2,6},{3,7},{4,8},{5,9},{6,10},{7,11},{8,12},{9,13},{1... | collective-permute-start | bytes 1769480 | tf_op jit(solution)/shard_map/ppermute | solution.py:811
  129.4 14.9 %collective-permute-start.26 = (bf16[2,2,96,768]{3,2,1,0:T(8,128)(2,1)}, bf16[2,2,96,768]{3,2,1,0:T(8,128)(2,1)}, u32[]{:S(2)}, u32[]{:S(2)}) collective-permute-start(bf16[2,2,96,768]{3,2,1,0:T(8,128)(2,1)} %collective-permute-done.23.refs_6_), channel_id=1, source_target_pairs={{0,2},{1,3},{2,0},{3,1},{4,6},{5,7},{6,4},{7,5},{8,10},{9,11},{10,... | collective-permute-start | bytes 1769480 | tf_op jit(solution)/shard_map/ppermute | solution.py:798
  130.0 20.8 %collective-permute-start.29 = (bf16[512,1536]{1,0:T(8,128)(2,1)}, bf16[512,1536]{1,0:T(8,128)(2,1)}, u32[]{:S(2)}, u32[]{:S(2)}) collective-permute-start(bf16[512,1536]{1,0:T(8,128)(2,1)} %collective-permute-done.27.cot_fa.rest_1_), channel_id=1, source_target_pairs={{0,1},{1,0},{2,3},{3,2},{4,5},{5,4},{6,7},{7,6},{8,9},{9,8},{10,11... | collective-permute-start | bytes 4718600 | tf_op jit(solution)/shard_map/ppermute | solution.py:798
  150.2 3.2 collective-permute-start.30
  172.0 4.5 %collective-permute-start.31 = (f32[8,2048]{1,0:T(8,128)}, f32[8,2048]{1,0:T(8,128)S(1)}, u32[]{:S(2)}, u32[]{:S(2)}) collective-permute-start(f32[8,2048]{1,0:T(8,128)} %get-tuple-element.209), channel_id=1, source_target_pairs={{0,16},{16,0},{1,17},{17,1},{2,18},{18,2},{3,19},{19,3},{4,20},{20... | collective-permute-start | bytes 196616 | tf_op jit(solution)/shard_map/ppermute | solution.py:785
  200.5 11.1 %collective-permute-start.33 = (bf16[1024,1536]{1,0:T(8,128)(2,1)}, bf16[1024,1536]{1,0:T(8,128)(2,1)}, u32[]{:S(2)}, u32[]{:S(2)}) collective-permute-start(bf16[1024,1536]{1,0:T(8,128)(2,1)} %get-tuple-element.215), channel_id=1, source_target_pairs={{0,1},{1,0},{2,3},{3,2},{4,5},{5,4},{6,7},{7,6},{8,9},{9,8},{10,11... | collective-permute-start | bytes 9437192 | tf_op jit(solution)/shard_map/ppermute | solution.py:798
  211.2 3.3 collective-permute-start.34
  229.9 17.8 %collective-permute-start.35 = (bf16[2,2,96,768]{3,2,1,0:T(8,128)(2,1)}, bf16[2,2,96,768]{3,2,1,0:T(8,128)(2,1)}, u32[]{:S(2)}, u32[]{:S(2)}) collective-permute-start(bf16[2,2,96,768]{3,2,1,0:T(8,128)(2,1)} %get-tuple-element.319), channel_id=1, source_target_pairs={{0,2},{1,3},{2,0},{3,1},{4,6},{5,7},{6,4},{7,5},{8,10},{9,11},{10,... | collective-permute-start | bytes 1769480 | tf_op jit(solution)/shard_map/ppermute | solution.py:798
  230.5 42.5 %collective-permute-start.39 = (bf16[512,1536]{1,0:T(8,128)(2,1)S(1)}, bf16[512,1536]{1,0:T(8,128)(2,1)S(1)}, u32[]{:S(2)}, u32[]{:S(2)}) collective-permute-start(bf16[512,1536]{1,0:T(8,128)(2,1)S(1)} %copy-done.8), channel_id=1, source_target_pairs={{0,16},{16,0},{1,17},{17,1},{2,18},{18,2},{3,19},{19,3},{4,20},{20... | collective-permute-start | bytes 4718600 | tf_op jit(solution)/shard_map/ppermute | solution.py:785
  249.9 17.0 %collective-permute-start.36 = (bf16[2,2,96,768]{3,2,1,0:T(8,128)(2,1)}, bf16[2,2,96,768]{3,2,1,0:T(8,128)(2,1)}, u32[]{:S(2)}, u32[]{:S(2)}) collective-permute-start(bf16[2,2,96,768]{3,2,1,0:T(8,128)(2,1)} %get-tuple-element.230), channel_id=1, source_target_pairs={{0,2},{1,3},{2,0},{3,1},{4,6},{5,7},{6,4},{7,5},{8,10},{9,11},{10,... | collective-permute-start | bytes 1769480 | tf_op jit(solution)/shard_map/ppermute | solution.py:798
  251.3 16.8 %collective-permute-start.37 = (bf16[2,2,96,768]{3,2,1,0:T(8,128)(2,1)}, bf16[2,2,96,768]{3,2,1,0:T(8,128)(2,1)}, u32[]{:S(2)}, u32[]{:S(2)}) collective-permute-start(bf16[2,2,96,768]{3,2,1,0:T(8,128)(2,1)} %fusion.1), channel_id=1, source_target_pairs={{0,4},{1,5},{2,6},{3,7},{4,8},{5,9},{6,10},{7,11},{8,12},{9,13},{1... | collective-permute-start | bytes 1769480 | tf_op jit(solution)/shard_map/ppermute | solution.py:811
  270.5 18.2 %collective-permute-start.38 = (bf16[2,2,96,768]{3,2,1,0:T(8,128)(2,1)}, bf16[2,2,96,768]{3,2,1,0:T(8,128)(2,1)}, u32[]{:S(2)}, u32[]{:S(2)}) collective-permute-start(bf16[2,2,96,768]{3,2,1,0:T(8,128)(2,1)} %get-tuple-element.238), channel_id=1, source_target_pairs={{0,2},{1,3},{2,0},{3,1},{4,6},{5,7},{6,4},{7,5},{8,10},{9,11},{10,... | collective-permute-start | bytes 1769480 | tf_op jit(solution)/shard_map/ppermute | solution.py:798
  271.1 17.6 %collective-permute-start.40 = (bf16[2,2,96,768]{3,2,1,0:T(8,128)(2,1)}, bf16[2,2,96,768]{3,2,1,0:T(8,128)(2,1)}, u32[]{:S(2)}, u32[]{:S(2)}) collective-permute-start(bf16[2,2,96,768]{3,2,1,0:T(8,128)(2,1)} %fusion.3), channel_id=1, source_target_pairs={{0,4},{1,5},{2,6},{3,7},{4,8},{5,9},{6,10},{7,11},{8,12},{9,13},{1... | collective-permute-start | bytes 1769480 | tf_op jit(solution)/shard_map/ppermute | solution.py:811
  290.4 20.3 %collective-permute-start.42 = (bf16[2,2,96,768]{3,2,1,0:T(8,128)(2,1)S(1)}, bf16[2,2,96,768]{3,2,1,0:T(8,128)(2,1)S(1)}, u32[]{:S(2)}, u32[]{:S(2)}) collective-permute-start(bf16[2,2,96,768]{3,2,1,0:T(8,128)(2,1)S(1)} %fusion.5), channel_id=1, source_target_pairs={{0,4},{1,5},{2,6},{3,7},{4,8},{5,9},{6,10},{7,11},{8,12},{9,13},{1... | collective-permute-start | bytes 1769480 | tf_op jit(solution)/shard_map/ppermute | solution.py:811
  291.0 19.7 %collective-permute-start.41 = (bf16[2,2,96,768]{3,2,1,0:T(8,128)(2,1)S(1)}, bf16[2,2,96,768]{3,2,1,0:T(8,128)(2,1)S(1)}, u32[]{:S(2)}, u32[]{:S(2)}) collective-permute-start(bf16[2,2,96,768]{3,2,1,0:T(8,128)(2,1)S(1)} %copy-done.11), channel_id=1, source_target_pairs={{0,2},{1,3},{2,0},{3,1},{4,6},{5,7},{6,4},{7,5},{8,10},{9,11},{10,... | collective-permute-start | bytes 1769480 | tf_op jit(solution)/shard_map/ppermute | solution.py:798
  312.8 19.3 %collective-permute-start.44 = (bf16[2,48,768]{2,1,0:T(8,128)(2,1)S(1)}, bf16[2,48,768]{2,1,0:T(8,128)(2,1)S(1)}, u32[]{:S(2)}, u32[]{:S(2)}) collective-permute-start(bf16[2,48,768]{2,1,0:T(8,128)(2,1)S(1)} %get-tuple-element.344), channel_id=1, source_target_pairs={{0,1},{1,0},{2,3},{3,2},{4,5},{5,4},{6,7},{7,6},{8,9},{9,8},{10,11... | collective-permute-start | bytes 442376 | tf_op jit(solution)/shard_map/ppermute | solution.py:798
  340.5 22.0 %collective-permute-start.46 = (bf16[512,1536]{1,0:T(8,128)(2,1)}, bf16[512,1536]{1,0:T(8,128)(2,1)}, u32[]{:S(2)}, u32[]{:S(2)}) collective-permute-start(bf16[512,1536]{1,0:T(8,128)(2,1)} %input_grad.4), channel_id=1, source_target_pairs={{0,1},{1,0},{2,3},{3,2},{4,5},{5,4},{6,7},{7,6},{8,9},{9,8},{10,11... | collective-permute-start | bytes 4718600 | tf_op jit(solution)/shard_map/ppermute | solution.py:798
  340.8 4.6 %collective-permute-start.43 = (f32[168,128]{1,0:T(8,128)S(1)}, f32[168,128]{1,0:T(8,128)S(1)}, u32[]{:S(2)}, u32[]{:S(2)}) collective-permute-start(f32[168,128]{1,0:T(8,128)S(1)} %pad_maximum_fusion.6), channel_id=1, source_target_pairs={{0,16},{16,0},{1,17},{17,1},{2,18},{18,2},{3,19},{19,3},{4,20},{20... | collective-permute-start | bytes 258056 | tf_op jit(solution)/shard_map/ppermute | solution.py:785
  341.1 15.5 %collective-permute-start.48 = (bf16[2,96,1152]{2,1,0:T(8,128)(2,1)S(1)}, bf16[2,96,1152]{2,1,0:T(8,128)(2,1)}, u32[]{:S(2)}, u32[]{:S(2)}) collective-permute-start(bf16[2,96,1152]{2,1,0:T(8,128)(2,1)S(1)} %get-tuple-element.323), channel_id=1, source_target_pairs={{0,2},{1,3},{2,0},{3,1},{4,6},{5,7},{6,4},{7,5},{8,10},{9,11},{10,... | collective-permute-start | bytes 1327112 | tf_op jit(solution)/shard_map/ppermute | solution.py:798
  345.5 9.5 %collective-permute-start.51 = (f32[168,128]{1,0:T(8,128)S(1)}, f32[168,128]{1,0:T(8,128)}, u32[]{:S(2)}, u32[]{:S(2)}) collective-permute-start(f32[168,128]{1,0:T(8,128)S(1)} %fusion.40), channel_id=1, source_target_pairs={{0,1},{1,0},{2,3},{3,2},{4,5},{5,4},{6,7},{7,6},{8,9},{9,8},{10,11... | collective-permute-start | bytes 258056 | tf_op jit(solution)/shard_map/ppermute | solution.py:798
  346.3 15.6 %collective-permute-start.52 = (bf16[48,1536]{1,0:T(8,128)(2,1)}, bf16[48,1536]{1,0:T(8,128)(2,1)}, u32[]{:S(2)}, u32[]{:S(2)}) collective-permute-start(bf16[48,1536]{1,0:T(8,128)(2,1)} %get-tuple-element.341), channel_id=1, source_target_pairs={{0,16},{16,0},{1,17},{17,1},{2,18},{18,2},{3,19},{19,3},{4,20},{20... | collective-permute-start | bytes 442376 | tf_op jit(solution)/shard_map/ppermute | solution.py:785
  358.4 18.5 %collective-permute-start.53 = (bf16[2,96,1152]{2,1,0:T(8,128)(2,1)}, bf16[2,96,1152]{2,1,0:T(8,128)(2,1)}, u32[]{:S(2)}, u32[]{:S(2)}) collective-permute-start(bf16[2,96,1152]{2,1,0:T(8,128)(2,1)} %fusion.10), channel_id=1, source_target_pairs={{0,4},{1,5},{2,6},{3,7},{4,8},{5,9},{6,10},{7,11},{8,12},{9,13},{1... | collective-permute-start | bytes 1327112 | tf_op jit(solution)/shard_map/ppermute | solution.py:811
  361.9 15.0 %collective-permute-start.49 = (bf16[2,96,1152]{2,1,0:T(8,128)(2,1)}, bf16[2,96,1152]{2,1,0:T(8,128)(2,1)}, u32[]{:S(2)}, u32[]{:S(2)}) collective-permute-start(bf16[2,96,1152]{2,1,0:T(8,128)(2,1)} %get-tuple-element.272), channel_id=1, source_target_pairs={{0,2},{1,3},{2,0},{3,1},{4,6},{5,7},{6,4},{7,5},{8,10},{9,11},{10,... | collective-permute-start | bytes 1327112 | tf_op jit(solution)/shard_map/ppermute | solution.py:798
  365.9 11.0 %collective-permute-start.50 = (bf16[128,1536]{1,0:T(8,128)(2,1)}, bf16[128,1536]{1,0:T(8,128)(2,1)}, u32[]{:S(2)}, u32[]{:S(2)}) collective-permute-start(bf16[128,1536]{1,0:T(8,128)(2,1)} %get-tuple-element.326), channel_id=1, source_target_pairs={{0,16},{16,0},{1,17},{17,1},{2,18},{18,2},{3,19},{19,3},{4,20},{20... | collective-permute-start | bytes 1179656 | tf_op jit(solution)/shard_map/ppermute | solution.py:785
  379.0 15.0 %collective-permute-start.54 = (bf16[2,96,1152]{2,1,0:T(8,128)(2,1)}, bf16[2,96,1152]{2,1,0:T(8,128)(2,1)}, u32[]{:S(2)}, u32[]{:S(2)}) collective-permute-start(bf16[2,96,1152]{2,1,0:T(8,128)(2,1)} %get-tuple-element.279), channel_id=1, source_target_pairs={{0,2},{1,3},{2,0},{3,1},{4,6},{5,7},{6,4},{7,5},{8,10},{9,11},{10,... | collective-permute-start | bytes 1327112 | tf_op jit(solution)/shard_map/ppermute | solution.py:798
  380.4 13.6 %collective-permute-start.56 = (bf16[2,96,1152]{2,1,0:T(8,128)(2,1)}, bf16[2,96,1152]{2,1,0:T(8,128)(2,1)}, u32[]{:S(2)}, u32[]{:S(2)}) collective-permute-start(bf16[2,96,1152]{2,1,0:T(8,128)(2,1)} %fusion.12), channel_id=1, source_target_pairs={{0,4},{1,5},{2,6},{3,7},{4,8},{5,9},{6,10},{7,11},{8,12},{9,13},{1... | collective-permute-start | bytes 1327112 | tf_op jit(solution)/shard_map/ppermute | solution.py:811
  381.6 12.4 %collective-permute-start.55 = (bf16[128,1536]{1,0:T(8,128)(2,1)}, bf16[128,1536]{1,0:T(8,128)(2,1)}, u32[]{:S(2)}, u32[]{:S(2)}) collective-permute-start(bf16[128,1536]{1,0:T(8,128)(2,1)} %get-tuple-element.325), channel_id=1, source_target_pairs={{0,16},{16,0},{1,17},{17,1},{2,18},{18,2},{3,19},{19,3},{4,20},{20... | collective-permute-start | bytes 1179656 | tf_op jit(solution)/shard_map/ppermute | solution.py:785
  382.7 19.3 %collective-permute-start.47 = (bf16[128,1536]{1,0:T(8,128)(2,1)}, bf16[128,1536]{1,0:T(8,128)(2,1)}, u32[]{:S(2)}, u32[]{:S(2)}) collective-permute-start(bf16[128,1536]{1,0:T(8,128)(2,1)} %get-tuple-element.327), channel_id=1, source_target_pairs={{0,16},{16,0},{1,17},{17,1},{2,18},{18,2},{3,19},{19,3},{4,20},{20... | collective-permute-start | bytes 1179656 | tf_op jit(solution)/shard_map/ppermute | solution.py:785
  395.3 10.8 %collective-permute-start.58 = (bf16[2,96,1152]{2,1,0:T(8,128)(2,1)S(1)}, bf16[2,96,1152]{2,1,0:T(8,128)(2,1)S(1)}, u32[]{:S(2)}, u32[]{:S(2)}) collective-permute-start(bf16[2,96,1152]{2,1,0:T(8,128)(2,1)S(1)} %fusion.14), channel_id=1, source_target_pairs={{0,4},{1,5},{2,6},{3,7},{4,8},{5,9},{6,10},{7,11},{8,12},{9,13},{1... | collective-permute-start | bytes 1327112 | tf_op jit(solution)/shard_map/ppermute | solution.py:811
  395.7 8.9 %collective-permute-start.57 = (bf16[2,96,1152]{2,1,0:T(8,128)(2,1)}, bf16[2,96,1152]{2,1,0:T(8,128)(2,1)S(1)}, u32[]{:S(2)}, u32[]{:S(2)}) collective-permute-start(bf16[2,96,1152]{2,1,0:T(8,128)(2,1)} %get-tuple-element.287), channel_id=1, source_target_pairs={{0,2},{1,3},{2,0},{3,1},{4,6},{5,7},{6,4},{7,5},{8,10},{9,11},{10,... | collective-permute-start | bytes 1327112 | tf_op jit(solution)/shard_map/ppermute | solution.py:798
  406.3 3.1 collective-permute-start.59
  406.4 7.4 %collective-permute-start.63 = (f32[168,128]{1,0:T(8,128)}, f32[168,128]{1,0:T(8,128)S(1)}, u32[]{:S(2)}, u32[]{:S(2)}) collective-permute-start(f32[168,128]{1,0:T(8,128)} %add.599), channel_id=1, source_target_pairs={{0,2},{1,3},{2,0},{3,1},{4,6},{5,7},{6,4},{7,5},{8,10},{9,11},{10,... | collective-permute-start | bytes 258056 | tf_op jit(solution)/shard_map/ppermute | solution.py:798
  407.0 19.6 %collective-permute-start.61 = (bf16[512,1536]{1,0:T(8,128)(2,1)}, bf16[512,1536]{1,0:T(8,128)(2,1)S(1)}, u32[]{:S(2)}, u32[]{:S(2)}) collective-permute-start(bf16[512,1536]{1,0:T(8,128)(2,1)} %input_grad.6), channel_id=1, source_target_pairs={{0,1},{1,0},{2,3},{3,2},{4,5},{5,4},{6,7},{7,6},{8,9},{9,8},{10,11... | collective-permute-start | bytes 4718600 | tf_op jit(solution)/shard_map/ppermute | solution.py:798
  407.2 19.4 %collective-permute-start.62 = (bf16[128,1536]{1,0:T(8,128)(2,1)}, bf16[128,1536]{1,0:T(8,128)(2,1)S(1)}, u32[]{:S(2)}, u32[]{:S(2)}) collective-permute-start(bf16[128,1536]{1,0:T(8,128)(2,1)} %get-tuple-element.324), channel_id=1, source_target_pairs={{0,16},{16,0},{1,17},{17,1},{2,18},{18,2},{3,19},{19,3},{4,20},{20... | collective-permute-start | bytes 1179656 | tf_op jit(solution)/shard_map/ppermute | solution.py:785
  409.6 13.1 %collective-permute-start.60 = (bf16[48,1920]{1,0:T(8,128)(2,1)S(1)}, bf16[48,1920]{1,0:T(8,128)(2,1)S(1)}, u32[]{:S(2)}, u32[]{:S(2)}) collective-permute-start(bf16[48,1920]{1,0:T(8,128)(2,1)S(1)} %get-tuple-element.337), channel_id=1, source_target_pairs={{0,16},{16,0},{1,17},{17,1},{2,18},{18,2},{3,19},{19,3},{4,20},{20... | collective-permute-start | bytes 552968 | tf_op jit(solution)/shard_map/ppermute | solution.py:785
  413.8 9.0 %collective-permute-start.64 = (f32[168,128]{1,0:T(8,128)S(1)}, f32[168,128]{1,0:T(8,128)S(1)}, u32[]{:S(2)}, u32[]{:S(2)}) collective-permute-start(f32[168,128]{1,0:T(8,128)S(1)} %add.623), channel_id=1, source_target_pairs={{0,4},{1,5},{2,6},{3,7},{4,0},{5,1},{6,2},{7,3},{8,12},{9,13},{10,... | collective-permute-start | bytes 258056 | tf_op jit(solution)/shard_map/ppermute | solution.py:798
  422.9 12.2 %collective-permute-start.65 = (f32[168,128]{1,0:T(8,128)S(1)}, f32[168,128]{1,0:T(8,128)S(1)}, u32[]{:S(2)}, u32[]{:S(2)}) collective-permute-start(f32[168,128]{1,0:T(8,128)S(1)} %add.624), channel_id=1, source_target_pairs={{0,8},{1,9},{2,10},{3,11},{4,12},{5,13},{6,14},{7,15},{8,0},{9,1},... | collective-permute-start | bytes 258056 | tf_op jit(solution)/shard_map/ppermute | solution.py:798
  (38 other events, 352.6 us)
